TPU v7x, 128 devices: a whole 4x4x4 slice. The times are simulated.
128 devices in a mesh: obs: 32 (over y, z_hi, x), vox: 4 (over z_lo, core).
Axes of the slice: x: 4, y: 4, z: 4 (z_hi: 2, z_lo: 2; z = z_hi * 2 + z_lo), core: 2. Of those that a mesh axis runs over, the one named last changes fastest.
Arguments:
- cov_slab: float32 [65536, 4096], P('vox', 'obs'), may hold values from -6 to 6
- cross_cov: bfloat16 [65536, 1024], P('vox', 'obs'), may hold values from -0.1875 to 0.1875
- ray_blocks: int32 [1024, 16], P('obs'), may hold values from 0 to 1023
- ray_coeff: float32 [1024, 1024], P('obs'), may hold values from -0.1875 to 0.1875
- region_rows: int32 [32], P('obs'), may hold values from 8 to 32, as said below
- innov_cov: float32 [1024, 1024], P('obs'), as said below
Outputs:
- new_slab: float32 [65536, 4096], P('vox', 'obs')
Inputs may be any that keep to these rules, and one draw needn't show every extreme that they name: `region_rows`: every station region holds at most 32 live slots, and some region holds exactly 32. `innov_cov`: symmetric positive definite; its smallest eigenvalue is at least 2.
All inputs are finite; a program needn't handle non-finite values.
Results may differ from a plain program's by a relative error of at most 0.00068.
Values may be sent and summed in bfloat16 or wider, within the bound.
No kernel may reach another device: no remote copies, remote signals or barrier semaphores. Data moves between devices by JAX's collectives and lax.ppermute only.
A program may use at most 192 MiB of HBM per device.

v0:
```python
import math

import jax
import jax.numpy as jnp
from jax import lax
from jax.sharding import PartitionSpec as P


def solve_with(factor, right_side):
    middle = lax.linalg.triangular_solve(factor, right_side, left_side=True, lower=True)
    return lax.linalg.triangular_solve(factor, middle, left_side=True, lower=True, transpose_a=True)


def shards(cov_slab, cross_cov, ray_blocks, ray_coeff, region_rows, innov_cov):
    local_rows, columns = cov_slab.shape
    slot_count = ray_blocks.shape[0]
    crossing = ray_blocks.shape[1]
    block_size = ray_coeff.shape[1] // crossing
    local_blocks = local_rows // block_size
    live_slots = (jnp.arange(slot_count, dtype=jnp.int32) < region_rows[0]).astype(jnp.float32)
    weights = ray_coeff * live_slots[:, None]
    first_block = lax.axis_index("vox") * local_blocks
    block_index = jnp.arange(local_blocks, dtype=jnp.int32)
    index_piece = lax.all_gather(ray_blocks, "obs", axis=0, tiled=True)
    weight_piece = lax.all_gather(weights, "obs", axis=0, tiled=True)
    piece_rows = index_piece.shape[0]
    batch_rows = math.gcd(piece_rows, 256)
    batches = piece_rows // batch_rows
    shifted = (index_piece - first_block).reshape(batches, batch_rows, crossing)
    scaled = weight_piece.reshape(batches, batch_rows, crossing, block_size)

    def one_batch(packed):
        index_batch, weight_batch = packed
        onehot = (index_batch[:, :, None] == block_index[None, None, :]).astype(jnp.float32)
        dense_rows = jnp.einsum(
            "snk,snj->skj", onehot, weight_batch, precision=lax.Precision.HIGHEST
        )
        dense_rows = dense_rows.reshape(batch_rows, local_rows)
        return jnp.dot(
            dense_rows,
            cov_slab,
            preferred_element_type=jnp.float32,
            precision=lax.Precision.HIGHEST,
        )

    rows_out = lax.map(one_batch, (shifted, scaled)).reshape(piece_rows, columns)
    whole_innov = lax.all_gather(innov_cov, "obs", axis=0, tiled=True)
    factor = jnp.linalg.cholesky(whole_innov)
    predicted = lax.psum(rows_out, "vox")
    solved = solve_with(factor, predicted).astype(jnp.bfloat16)
    downdate = jnp.dot(
        lax.all_gather(cross_cov, "obs", axis=1, tiled=True),
        solved,
        preferred_element_type=jnp.float32,
    )
    return cov_slab - downdate


def solution(mesh):
    placed = (
        P("vox", "obs"),
        P("vox", "obs"),
        P("obs", None),
        P("obs", None),
        P("obs"),
        P("obs", None),
    )
    return jax.shard_map(
        shards, mesh=mesh, in_specs=placed, out_specs=P("vox", "obs"), check_vma=False
    )
```

profile of v0, /device:TPU:0, one launch (start us, length us, event | category | flops | bytes accessed | tf_op | source)
XLA Modules:
  0.0 747.2 jit_solution(11841899275142934022)
XLA Ops:
  9.7 97.9 %all-gather = s32[32,32,16]{1,2,0:T(8,128)S(1)} all-gather(s32[1,32,16]{1,2,0:T(8,128)} %bitcast.165), channel_id=1, replica_groups=mesh['obs'=32,'vox'=4] {'obs'}, dimensions={0}, use_global_device_ids=true | all-gather | bytes 67584 | tf_op jit(solution)/shard_map/all_gather | solution.py:24
  115.1 244.0 %while.13 = (s32[]{:T(128)}, f32[4,256,128]{2,1,0:T(8,128)}, s32[4,256,16]{2,1,0:T(8,128)S(1)}, f32[4,256,16,64]{3,2,1,0:T(8,128)}, f32[16384,128]{1,0:T(8,128)}, /*index=5*/s32[]{:T(128)}) while((s32[]{:T(128)}, f32[4,256,128]{2,1,0:T(8,128)}, s32[4,256,16]{2,1,0:T(8,128)S(1)}, f32[4,256,16,64]{3,2,1,0:T(8,128)}, ...), condition=%wide.region_17.18_spmd.clone, body=%wide.region_16.17_spmd.clone.sunk | while | flops 7248805888 | bytes 77775944 | solution.py:46
  115.1 12.3 %fusion.143 = f32[256,256,64]{1,2,0:T(8,128)} fusion(f32[4,256,16,64]{3,2,1,0:T(8,128)} %get-tuple-element.227, s32[]{:T(128)} %get-tuple-element.218, s32[256,16]{1,0:T(8,128)S(1)} %dynamic-slice_bitcast_fusion.2), kind=kOutput, calls=%fused_computation.4.clone.1 | convolution fusion | flops 806354944 | bytes 18891264 | tf_op jit(solution)/shard_map/while/body/eval_jaxpr/snk,snj->skj/dot_general | solution.py:35
  127.4 17.7 %copy.38 = f32[256,256,64]{0,2,1:T(8,128)} copy(f32[256,256,64]{1,2,0:T(8,128)} %fusion.143) | data formatting | bytes 33554432 | tf_op jit(solution)/shard_map/while/body/eval_jaxpr/snk,snj->skj/dot_general | solution.py:35
  145.1 30.9 %fusion.144 = f32[4,256,128]{2,1,0:T(8,128)} fusion(f32[4,256,128]{2,1,0:T(8,128)} %get-tuple-element.219, s32[]{:T(128)} %get-tuple-element.218, f32[256,16384]{0,1:T(8,128)} %bitcast.162, f32[16384,128]{1,0:T(8,128)} %get-tuple-element.228), kind=kOutput, calls=%fused_computation.9.clone.1 | convolution fusion | flops 6442450944 | bytes 25297408 | tf_op jit(solution)/shard_map/while/body/eval_jaxpr/dot_general | solution.py:39
  176.1 12.3 %fusion.143 = f32[256,256,64]{1,2,0:T(8,128)} fusion(f32[4,256,16,64]{3,2,1,0:T(8,128)} %get-tuple-element.227, s32[]{:T(128)} %get-tuple-element.218, s32[256,16]{1,0:T(8,128)S(1)} %dynamic-slice_bitcast_fusion.2), kind=kOutput, calls=%fused_computation.4.clone.1 | convolution fusion | flops 806354944 | bytes 18891264 | tf_op jit(solution)/shard_map/while/body/eval_jaxpr/snk,snj->skj/dot_general | solution.py:35
  188.4 17.7 %copy.38 = f32[256,256,64]{0,2,1:T(8,128)} copy(f32[256,256,64]{1,2,0:T(8,128)} %fusion.143) | data formatting | bytes 33554432 | tf_op jit(solution)/shard_map/while/body/eval_jaxpr/snk,snj->skj/dot_general | solution.py:35
  206.1 30.9 %fusion.144 = f32[4,256,128]{2,1,0:T(8,128)} fusion(f32[4,256,128]{2,1,0:T(8,128)} %get-tuple-element.219, s32[]{:T(128)} %get-tuple-element.218, f32[256,16384]{0,1:T(8,128)} %bitcast.162, f32[16384,128]{1,0:T(8,128)} %get-tuple-element.228), kind=kOutput, calls=%fused_computation.9.clone.1 | convolution fusion | flops 6442450944 | bytes 25297408 | tf_op jit(solution)/shard_map/while/body/eval_jaxpr/dot_general | solution.py:39
  237.0 12.3 %fusion.143 = f32[256,256,64]{1,2,0:T(8,128)} fusion(f32[4,256,16,64]{3,2,1,0:T(8,128)} %get-tuple-element.227, s32[]{:T(128)} %get-tuple-element.218, s32[256,16]{1,0:T(8,128)S(1)} %dynamic-slice_bitcast_fusion.2), kind=kOutput, calls=%fused_computation.4.clone.1 | convolution fusion | flops 806354944 | bytes 18891264 | tf_op jit(solution)/shard_map/while/body/eval_jaxpr/snk,snj->skj/dot_general | solution.py:35
  249.3 17.7 %copy.38 = f32[256,256,64]{0,2,1:T(8,128)} copy(f32[256,256,64]{1,2,0:T(8,128)} %fusion.143) | data formatting | bytes 33554432 | tf_op jit(solution)/shard_map/while/body/eval_jaxpr/snk,snj->skj/dot_general | solution.py:35
  267.0 30.9 %fusion.144 = f32[4,256,128]{2,1,0:T(8,128)} fusion(f32[4,256,128]{2,1,0:T(8,128)} %get-tuple-element.219, s32[]{:T(128)} %get-tuple-element.218, f32[256,16384]{0,1:T(8,128)} %bitcast.162, f32[16384,128]{1,0:T(8,128)} %get-tuple-element.228), kind=kOutput, calls=%fused_computation.9.clone.1 | convolution fusion | flops 6442450944 | bytes 25297408 | tf_op jit(solution)/shard_map/while/body/eval_jaxpr/dot_general | solution.py:39
  297.9 12.3 %fusion.143 = f32[256,256,64]{1,2,0:T(8,128)} fusion(f32[4,256,16,64]{3,2,1,0:T(8,128)} %get-tuple-element.227, s32[]{:T(128)} %get-tuple-element.218, s32[256,16]{1,0:T(8,128)S(1)} %dynamic-slice_bitcast_fusion.2), kind=kOutput, calls=%fused_computation.4.clone.1 | convolution fusion | flops 806354944 | bytes 18891264 | tf_op jit(solution)/shard_map/while/body/eval_jaxpr/snk,snj->skj/dot_general | solution.py:35
  310.2 17.7 %copy.38 = f32[256,256,64]{0,2,1:T(8,128)} copy(f32[256,256,64]{1,2,0:T(8,128)} %fusion.143) | data formatting | bytes 33554432 | tf_op jit(solution)/shard_map/while/body/eval_jaxpr/snk,snj->skj/dot_general | solution.py:35
  327.9 30.9 %fusion.144 = f32[4,256,128]{2,1,0:T(8,128)} fusion(f32[4,256,128]{2,1,0:T(8,128)} %get-tuple-element.219, s32[]{:T(128)} %get-tuple-element.218, f32[256,16384]{0,1:T(8,128)} %bitcast.162, f32[16384,128]{1,0:T(8,128)} %get-tuple-element.228), kind=kOutput, calls=%fused_computation.9.clone.1 | convolution fusion | flops 6442450944 | bytes 25297408 | tf_op jit(solution)/shard_map/while/body/eval_jaxpr/dot_general | solution.py:39
  380.6 11.7 %cholesky.223 = f32[128,128]{1,0:T(8,128)S(1)} custom-call(f32[128,128]{1,0:T(8,128)S(1)} %cholesky.580), custom_call_target="Cholesky" | custom-call | tf_op jit(solution)/shard_map/jit(cholesky)/cholesky | solution.py:48
  408.6 11.9 %cholesky.244 = f32[128,128]{1,0:T(8,128)S(1)} custom-call(f32[128,128]{1,0:T(8,128)S(1)} %cholesky.584), custom_call_target="Cholesky" | custom-call | tf_op jit(solution)/shard_map/jit(cholesky)/cholesky | solution.py:48
  434.7 11.7 %cholesky.468 = f32[128,128]{1,0:T(8,128)S(1)} custom-call(f32[128,128]{1,0:T(8,128)S(1)} %cholesky.589), custom_call_target="Cholesky" | custom-call | tf_op jit(solution)/shard_map/jit(cholesky)/cholesky | solution.py:48
  460.5 11.9 %cholesky.487 = f32[128,128]{1,0:T(8,128)S(1)} custom-call(f32[128,128]{1,0:T(8,128)S(1)} %cholesky.594), custom_call_target="Cholesky" | custom-call | tf_op jit(solution)/shard_map/jit(cholesky)/cholesky | solution.py:48
  486.3 11.7 %cholesky.506 = f32[128,128]{1,0:T(8,128)S(1)} custom-call(f32[128,128]{1,0:T(8,128)S(1)} %cholesky.599), custom_call_target="Cholesky" | custom-call | tf_op jit(solution)/shard_map/jit(cholesky)/cholesky | solution.py:48
  512.1 11.7 %cholesky.526 = f32[128,128]{1,0:T(8,128)S(1)} custom-call(f32[128,128]{1,0:T(8,128)S(1)} %cholesky.604), custom_call_target="Cholesky" | custom-call | tf_op jit(solution)/shard_map/jit(cholesky)/cholesky | solution.py:48
  537.3 11.7 %cholesky.546 = f32[128,128]{1,0:T(8,128)S(1)} custom-call(f32[128,128]{1,0:T(8,128)S(1)} %cholesky.609), custom_call_target="Cholesky" | custom-call | tf_op jit(solution)/shard_map/jit(cholesky)/cholesky | solution.py:48
  589.7 22.4 %while.12 = (s32[]{:T(128)}, f32[1024,1024]{1,0:T(8,128)}, s32[8,2]{0,1:T(2,128)S(1)}, f32[8,128,128]{2,1,0:T(8,128)S(1)}, s32[]{:T(128)}) while((s32[]{:T(128)}, f32[1024,1024]{1,0:T(8,128)}, s32[8,2]{0,1:T(2,128)S(1)}, f32[8,128,128]{2,1,0:T(8,128)S(1)}, s32[]{:T(128)}) %tuple.79), condition=%wide.while_cond, body=%wide.while_body.sunk | while | flops 2 | bytes 131181 | solution.py:11
  612.1 78.8 %custom-call.71 = f32[8,128,128]{1,2,0:T(8,128)S(1)} custom-call(f32[8,128,128]{2,1,0:T(8,128)S(1)} %get-tuple-element.45), custom_call_target="InvertDiagBlocksLowerTriangular" | custom-call | tf_op jit(solution)/shard_map/triangular_solve | solution.py:11
  709.7 21.5 %fusion.8 = f32[16384,128]{0,1:T(8,128)} fusion(f32[16384,128]{0,1:T(8,128)} %copy.32, bf16[1024,128]{1,0:T(8,128)(2,1)S(1)} %constant_dynamic-update-slice_fusion.36, bf16[16384,1024]{0,1:T(8,128)(2,1)} %all-gather.9.cloned.1.call-done), kind=kOutput, calls=%fused_computation.13 | convolution fusion | flops 4297064448 | bytes 50593792 | tf_op jit(solution)/shard_map/dot_general | solution.py:51
  (155 shorter events, 202.4 us)
Async XLA Ops:
  6.5 101.3 %all-gather.7.cloned.1.call-start = ((), (), s32[]{:S(2)}) async-start(), calls=%async_computation.1 | async-start | bytes 4325376 | tf_op jit(solution)/shard_map/all_gather | solution.py:25
  8.9 359.9 %all-gather.5.cloned.1.call-start = ((), (), s32[]{:S(2)}) async-start(), calls=%async_computation | async-start | bytes 4325376 | tf_op jit(solution)/shard_map/all_gather | solution.py:47
  9.6 681.3 %all-reduce.3.cloned.1.call-start = ((), (), s32[]{:S(2)}) async-start(), calls=%async_computation.2 | async-start | bytes 1048576 | tf_op jit(solution)/shard_map/psum | solution.py:49
  359.1 350.6 %all-gather.9.cloned.1.call-start = ((), (), s32[]{:S(2)}) async-start(), calls=%async_computation.3 | async-start | bytes 34603008 | tf_op jit(solution)/shard_map/all_gather | solution.py:52
  378.6 2.0 copy-start.1
  691.0 9.1 %copy-start = (f32[1024,1024]{1,0:T(8,128)S(1)}, f32[1024,1024]{1,0:T(8,128)}, u32[]{:S(2)}) copy-start(f32[1024,1024]{1,0:T(8,128)} %get-tuple-element.252) | copy-start | bytes 12582916
Sparse Core Ops, SparseCore 0:
  10.3 85.3 all-gather.6
  98.7 79.5 all-gather.4
  359.2 31.9 all-reduce.2
  394.2 262.8 all-gather.8
where the time goes:
time: 760 us; the launch traced here: 747 us
  other arithmetic  262 us (34%)
  matrix products  236 us (31%)
  local copies, waits for them, and re-layouts  129 us (17%)
  blocking collectives  97.9 us (13%)
  between operations  20.2 us (3%)
    another operation x30, other arithmetic, shards(): factor = jnp.linalg.cholesky(whole_innov)  173 us
    dot_general x4, matrix products, one_batch(): jnp.dot(dense_rows, cov_slab, preferred_element_type=jnp.float32, precisi...  124 us
    all_gather x1, blocking collectives, shards(): index_piece = lax.all_gather(ray_blocks, 'obs', axis=0, tiled=True)  97.9 us
    another operation x4, other arithmetic, solve_with(): lax.linalg.triangular_solve(factor, middle, left_side=True, lower=True, t...  83.8 us
    dot_general x4, local copies, waits for them, and re-layouts, one_batch(): jnp.einsum('snk,snj->skj', onehot, weight_batch, precision=lax.Precision....  70.8 us
    dot_general x4, matrix products, one_batch(): jnp.einsum('snk,snj->skj', onehot, weight_batch, precision=lax.Precision....  49.2 us
    another operation x14, matrix products, shards(): factor = jnp.linalg.cholesky(whole_innov)  23.6 us
    another operation x24, local copies, waits for them, and re-layouts  22.2 us
  transfers between devices with their start and end apart: 4, of which 0 were waited for; matrix products, arithmetic and copies ran while one was open for 79% of the time, Pallas kernels for 0%

commit v1 on v0

v1 whole, which is shorter than its diff:
```python
import functools

import jax
import jax.numpy as jnp
from jax import lax
from jax.experimental import pallas as pl
from jax.experimental.pallas import tpu as pltpu
from jax.sharding import PartitionSpec as P

F32 = jnp.float32
BF16 = jnp.bfloat16
VMEM_LIMIT = 60 * 1024 * 1024


def halves(x):
    high = x.astype(BF16)
    return high, (x - high.astype(F32)).astype(BF16)


def dot(a, b):
    return jnp.dot(a, b, preferred_element_type=F32)


def dot_split(a, b):
    ah, al = halves(a)
    bh, bl = halves(b)
    return dot(ah, bh) + (dot(ah, bl) + dot(al, bh))


def predict_kernel(place_ref, block_ref, weight_ref, cov_ref, out_ref, dense, cov_split, *, tile, crossing, block):
    step = pl.program_id(0)
    rows, columns = cov_ref.shape
    pairs = rows // (2 * block)
    deep = 2 * 2 * block
    quads = rows // deep
    lane = lax.broadcasted_iota(jnp.int32, (8, 2 * block), 1)
    sub = lax.broadcasted_iota(jnp.int32, (8, 2 * block), 0)
    upper = (lane >= block).astype(jnp.int32)

    @pl.when(step == 0)
    def _():
        def clear(i, c):
            dense[i] = jnp.zeros_like(dense[i])
            return c

        lax.fori_loop(0, pairs, clear, 0)

        def split(i, c):
            high, low = halves(cov_ref[pl.ds(pl.multiple_of(i * deep, deep), deep), :])
            cov_split[i, :, :columns] = high
            cov_split[i, :, columns:] = low
            return c

        lax.fori_loop(0, quads, split, 0)

    def scatter(group, c):
        row = pl.multiple_of(group * 8, 8)
        first = (step * tile + row) * crossing
        blocks = block_ref[pl.ds(row, 8), :] & 1
        for n in range(crossing):
            if n % 2 == 0:
                plain = weight_ref[pl.ds(row, 8), pl.ds(n * block, 2 * block)]
                turned = pltpu.roll(plain, block, 1)
                both = jnp.where(upper == 0, plain, turned)
            else:
                both = jnp.where(upper == 0, turned, plain)
            half = blocks[:, n : n + 1] == upper
            for i in range(8):
                where = place_ref[first + i * crossing + n]
                pltpu.store(dense.at[where, pl.ds(row, 8), :], both, mask=half & (sub == i))
        return c

    lax.fori_loop(0, tile // 8, scatter, 0)
    out_ref[...] = jnp.zeros_like(out_ref)
    together = 4

    def multiply(i, c):
        total = jnp.zeros((tile, 2 * columns), F32)
        small = jnp.zeros((tile, columns), F32)
        for k in range(together):
            q = i * together + k
            wide = jnp.concatenate([dense[2 * q], dense[2 * q + 1]], axis=1)
            high, low = halves(wide)
            total = total + dot(high, cov_split[q])
            small = small + dot(low, cov_split[q, :, :columns])
            dense[2 * q] = jnp.zeros((tile, 2 * block), F32)
            dense[2 * q + 1] = jnp.zeros((tile, 2 * block), F32)
        out_ref[...] += total[:, :columns] + (total[:, columns:] + small)
        return c

    lax.fori_loop(0, quads // together, multiply, 0)


def predict(place, blocks, weights, cov_slab, crossing, block):
    slots = blocks.shape[0]
    rows, columns = cov_slab.shape
    tile = 256
    return pl.pallas_call(
        functools.partial(predict_kernel, tile=tile, crossing=crossing, block=block),
        grid=(slots // tile,),
        in_specs=[
            pl.BlockSpec(memory_space=pltpu.SMEM),
            pl.BlockSpec((tile, crossing), lambda i: (i, 0)),
            pl.BlockSpec((tile, crossing * block), lambda i: (i, 0)),
            pl.BlockSpec(memory_space=pltpu.VMEM),
        ],
        out_specs=pl.BlockSpec((tile, columns), lambda i: (i, 0)),
        out_shape=jax.ShapeDtypeStruct((slots, columns), F32),
        scratch_shapes=[
            pltpu.VMEM((rows // (2 * block) + 1, tile, 2 * block), F32),
            pltpu.VMEM((rows // (4 * block), 4 * block, 2 * columns), BF16),
        ],
        compiler_params=pltpu.CompilerParams(vmem_limit_bytes=VMEM_LIMIT),
        cost_estimate=pl.CostEstimate(
            flops=6 * slots * rows * columns, bytes_accessed=rows * columns * 4, transcendentals=0
        ),
        name="predict",
    )(place, blocks, weights, cov_slab)


def strip_sweep(strip):
    sub = lax.broadcasted_iota(jnp.int32, strip.shape, 0)
    lane = lax.broadcasted_iota(jnp.int32, strip.shape, 1)
    cols = [jnp.broadcast_to(strip[:, j : j + 1], strip.shape) for j in range(8)]
    for p in range(8):
        mine = sub == p
        inv = 1.0 / jnp.broadcast_to(cols[p][p : p + 1, :], strip.shape)
        strip = jnp.where(lane == p, jnp.where(mine, 1.0, 0.0), strip)
        head = jnp.broadcast_to(strip[p : p + 1, :], strip.shape) * inv
        strip = jnp.where(mine, head, strip - cols[p] * head)
        for j in range(p + 1, 8):
            top = jnp.broadcast_to(cols[j][p : p + 1, :], strip.shape) * inv
            cols[j] = jnp.where(mine, top, cols[j] - cols[p] * top)
    return jnp.where(lane < 8, -strip, strip)


def small_sweep(block):
    size = block.shape[0]
    lane = lax.broadcasted_iota(jnp.int32, block.shape, 1)

    def group(_, s):
        top = strip_sweep(s[:8, :])
        rest = jnp.where(lane < 8, 0.0, s)
        for j in range(8):
            rest = rest - s[:, j : j + 1] * top[j : j + 1, :]
        new = jnp.concatenate([rest[8:, :], top], axis=0)
        return pltpu.roll(new, size - 8, 1)

    return lax.fori_loop(0, size // 8, group, block)


def inverse_kernel(a_ref, m_ref, left, right, pivot, *, size):
    n = a_ref.shape[0]
    m_ref[...] = a_ref[...]

    def sweep(k, c):
        at = pl.ds(pl.multiple_of(k * size, size), size)
        minus = small_sweep(m_ref[at, at])
        pivot[...] = dot_split(minus, m_ref[at, :]) * -1.0
        pivot[:, at] = minus
        high, low = halves(m_ref[:, at])
        left[:, :size] = high
        left[:, size:] = low
        m_ref[:, at] = jnp.zeros((n, size), F32)
        high, low = halves(pivot[...])
        right[:size, :] = high
        right[size : 2 * size, :] = high
        right[2 * size :, :] = low

        def update(i, c):
            here = pl.ds(pl.multiple_of(i * size, size), size)
            both = left[here, :]
            product = dot(both, right[: 2 * size, :]) + dot(both[:, :size], right[2 * size :, :])
            m_ref[here, :] = m_ref[here, :] - product
            return c

        lax.fori_loop(0, n // size, update, 0)
        m_ref[at, :] = pivot[...]
        return c

    lax.fori_loop(0, n // size, sweep, 0)


def minus_inverse(a):
    n = a.shape[0]
    size = 128
    return pl.pallas_call(
        functools.partial(inverse_kernel, size=size),
        in_specs=[pl.BlockSpec(memory_space=pltpu.VMEM)],
        out_specs=pl.BlockSpec(memory_space=pltpu.VMEM),
        out_shape=jax.ShapeDtypeStruct((n, n), F32),
        scratch_shapes=[
            pltpu.VMEM((n, 2 * size), BF16),
            pltpu.VMEM((3 * size, n), BF16),
            pltpu.VMEM((size, n), F32),
        ],
        compiler_params=pltpu.CompilerParams(vmem_limit_bytes=VMEM_LIMIT),
        cost_estimate=pl.CostEstimate(flops=60 * n * n * n, bytes_accessed=8 * n * n, transcendentals=0),
        name="minus_inverse",
    )(a)


def update_kernel(minus_ref, predicted_ref, cross_ref, cov_ref, out_ref, solved):
    @pl.when(pl.program_id(0) == 0)
    def _():
        turned = predicted_ref[...].T
        solved[...] = (-dot_split(turned, minus_ref[...])).astype(BF16)

    product = dot(solved[...], cross_ref[...])
    out_ref[...] = cov_ref[...] - product.T


def update(minus, predicted, cross_turned, cov_slab):
    rows, columns = cov_slab.shape
    n = minus.shape[0]
    tile = 1024
    return pl.pallas_call(
        update_kernel,
        grid=(rows // tile,),
        in_specs=[
            pl.BlockSpec(memory_space=pltpu.VMEM),
            pl.BlockSpec(memory_space=pltpu.VMEM),
            pl.BlockSpec((n, tile), lambda i: (0, i)),
            pl.BlockSpec((tile, columns), lambda i: (i, 0)),
        ],
        out_specs=pl.BlockSpec((tile, columns), lambda i: (i, 0)),
        out_shape=jax.ShapeDtypeStruct((rows, columns), F32),
        scratch_shapes=[pltpu.VMEM((columns, n), BF16)],
        compiler_params=pltpu.CompilerParams(vmem_limit_bytes=VMEM_LIMIT),
        cost_estimate=pl.CostEstimate(
            flops=2 * rows * columns * n, bytes_accessed=rows * (2 * n + 8 * columns), transcendentals=0
        ),
        name="downdate",
    )(minus, predicted, cross_turned, cov_slab)


def merged(ray_blocks, weights):
    slots, crossing = ray_blocks.shape
    same = ray_blocks[:, :, None] == ray_blocks[:, None, :]
    order = jnp.arange(crossing, dtype=jnp.int32)
    first = ~jnp.any(same & (order[None, None, :] < order[None, :, None]), axis=2)
    parts = weights.reshape(slots, crossing, -1)
    total = jnp.sum(jnp.where(same[:, :, :, None], parts[:, None, :, :], 0.0), axis=2)
    return jnp.where(first, ray_blocks, -1), total.reshape(weights.shape)


def shards(cov_slab, cross_cov, ray_blocks, ray_coeff, region_rows, innov_cov):
    local_rows, columns = cov_slab.shape
    slot_count, crossing = ray_blocks.shape
    block_size = ray_coeff.shape[1] // crossing
    local_blocks = local_rows // block_size
    live = jnp.arange(slot_count, dtype=jnp.int32) < region_rows[0]
    weights = jnp.where(live[:, None], ray_coeff, 0.0)
    blocks, weights = merged(ray_blocks, weights)
    first_block = lax.axis_index("vox") * local_blocks
    blocks = lax.all_gather(blocks, "obs", axis=0, tiled=True)
    weights = lax.all_gather(weights, "obs", axis=0, tiled=True)
    local = blocks - first_block
    inside = (local >= 0) & (local < local_blocks) & (blocks >= 0)
    place = jnp.where(inside, local // 2, local_blocks // 2).reshape(-1)
    predicted = lax.psum(predict(place, blocks, weights, cov_slab, crossing, block_size), "vox")
    whole_innov = lax.all_gather(innov_cov, "obs", axis=0, tiled=True)
    minus = minus_inverse(whole_innov)
    cross_turned = lax.all_gather(cross_cov.T, "obs", axis=0, tiled=True)
    return update(minus, predicted, cross_turned, cov_slab)


def solution(mesh):
    placed = (
        P("vox", "obs"),
        P("vox", "obs"),
        P("obs", None),
        P("obs", None),
        P("obs"),
        P("obs", None),
    )
    return jax.shard_map(
        shards, mesh=mesh, in_specs=placed, out_specs=P("vox", "obs"), check_vma=False
    )
```

time: 760 us -> 515 us (0.68)
  the two profiles are of different devices: /device:TPU:0 before, /device:TPU:66 now
where the time goes in v1:
time: 515 us; the launch traced here: 511 us
  waiting for transfers between devices  255 us (50%)
  Pallas kernels  156 us (30%)
  blocking collectives  79.4 us (15%)
  between operations  13.8 us (3%)
    all_gather x1, waiting for transfers between devices, shards(): cross_turned = lax.all_gather(cross_cov.T, 'obs', axis=0, tiled=True)  235 us
    all_gather x1, blocking collectives, shards(): blocks = lax.all_gather(blocks, 'obs', axis=0, tiled=True)  79.4 us
    pallas_call x1, Pallas kernels, minus_inverse(): pl.pallas_call(functools.partial(inverse_kernel, size=size), in_specs=[pl...  68.9 us
    pallas_call x1, Pallas kernels, predict(): pl.pallas_call(functools.partial(predict_kernel, tile=tile, crossing=cros...  61.5 us
    pallas_call x1, Pallas kernels, update(): pl.pallas_call(update_kernel, grid=(rows // tile,), in_specs=[pl.BlockSpe...  25.4 us
    all_gather x1, waiting for transfers between devices, shards(): whole_innov = lax.all_gather(innov_cov, 'obs', axis=0, tiled=True)  18.9 us
  transfers between devices with their start and end apart: 4, of which 2 were waited for; matrix products, arithmetic and copies ran while one was open for 0% of the time, Pallas kernels for 26%

profile of v1, /device:TPU:66, one launch (start us, length us, event | category | flops | bytes accessed | tf_op | source)
XLA Modules:
  0.0 511.0 jit_solution(9864651778898424671)
XLA Ops:
  7.2 0.9 broadcast_compare_fusion
  8.1 0.2 copy.17
  8.3 1.0 broadcast_select_fusion
  9.3 0.1 broadcast_in_dim.53
  9.4 1.7 select_reduce_fusion
  11.1 0.8 reshape.30
  11.9 0.0 all-gather.7.cloned.1.call-update
  11.9 0.0 all-gather.5.cloned.1.call-start
  11.9 0.7 all-gather.5.cloned.1.call-update
  12.6 0.0 all-reduce.2.cloned.1.call-start
  12.7 0.7 select_bitcast_fusion
  13.4 79.4 %all-gather = s32[32,32,16]{1,2,0:T(8,128)S(1)} all-gather(s32[1,32,16]{1,2,0:T(8,128)S(1)} %select_bitcast_fusion), channel_id=1, replica_groups=mesh['obs'=32,'vox'=4] {'obs'}, dimensions={0}, use_global_device_ids=true | all-gather | bytes 67584 | tf_op jit(solution)/shard_map/all_gather | solution.py:256
  92.8 0.2 copy.16
  93.0 0.0 copy-start
  93.0 0.4 fusion.1
  93.4 0.8 reshape.29.place_ref
  94.2 61.5 %predict.1 = f32[1024,128]{1,0:T(8,128)} custom-call(s32[16384]{0:T(1024)} %reshape.29.place_ref, s32[1024,16]{1,0:T(8,128)} %bitcast.7, f32[1024,1024]{1,0:T(8,128)} %all-gather.7.cloned.1.call-done.weight_ref, f32[16384,128]{1,0:T(8,128)} %cov_ref.3), custom_call_target="tpu_custom_call" | custom-call | flops 12884901888 | bytes 8388608 | tf_op jit(solution)/shard_map/predict/pallas_call | solution.py:98
  155.8 0.0 all-reduce.2.cloned.1.call-update
  155.8 0.0 all-gather.9.cloned.1.call-start
  155.8 0.5 all-gather.9.cloned.1.call-update
  156.4 18.9 %all-gather.5.cloned.1.call-done.a_ref = f32[1024,1024]{1,0:T(8,128)} async-done(((f32[32,1024]{1,0:T(8,128)}), f32[1024,1024]{1,0:T(8,128)}) %all-gather.5.cloned.1.call-update) | async-done | bytes 4194320 | tf_op jit(solution)/shard_map/all_gather | solution.py:262
  175.3 68.9 %minus_inverse.1.minus_ref = f32[1024,1024]{1,0:T(8,128)} custom-call(f32[1024,1024]{1,0:T(8,128)} %all-gather.5.cloned.1.call-done.a_ref), custom_call_target="tpu_custom_call" | custom-call | flops 64424509440 | bytes 8388608 | tf_op jit(solution)/shard_map/minus_inverse/pallas_call | solution.py:187
  244.2 234.8 %all-gather.9.cloned.1.call-done.cross_ref = bf16[1024,16384]{1,0:T(8,128)(2,1)} async-done(((bf16[32,16384]{1,0:T(8,128)(2,1)}), bf16[1024,16384]{1,0:T(8,128)(2,1)}) %all-gather.9.cloned.1.call-update) | async-done | bytes 33554448 | tf_op jit(solution)/shard_map/all_gather | solution.py:264
  479.0 25.4 %downdate.1 = f32[16384,128]{1,0:T(8,128)} custom-call(f32[1024,1024]{1,0:T(8,128)} %minus_inverse.1.minus_ref, f32[1024,128]{1,0:T(8,128)} %all-reduce.2.cloned.1.call-done.predicted_ref, bf16[1024,16384]{1,0:T(8,128)(2,1)} %all-gather.9.cloned.1.call-done.cross_ref, f32[16384,128]{1,0:T(8,128)} %cov_ref.3), custom_call_target="tpu_custom_call" | custom-call | flops 4294967296 | bytes 50331648 | tf_op jit(solution)/shard_map/downdate/pallas_call | solution.py:217
  (6 shorter events, 0.0 us)
Async XLA Ops:
  6.5 87.7 %all-gather.7.cloned.1.call-start = ((), (), s32[]{:S(2)}) async-start(), calls=%async_computation.1 | async-start | bytes 4325376 | tf_op jit(solution)/shard_map/all_gather | solution.py:257
  11.9 163.4 %all-gather.5.cloned.1.call-start = ((), (), s32[]{:S(2)}) async-start(), calls=%async_computation | async-start | bytes 4325376 | tf_op jit(solution)/shard_map/all_gather | solution.py:262
  12.6 231.6 %all-reduce.2.cloned.1.call-start = ((), (), s32[]{:S(2)}) async-start(), calls=%async_computation.2 | async-start | bytes 1048576 | tf_op jit(solution)/shard_map/psum | solution.py:261
  93.0 1.2 copy-start
  155.8 323.3 %all-gather.9.cloned.1.call-start = ((), (), s32[]{:S(2)}) async-start(), calls=%async_computation.3 | async-start | bytes 34603008 | tf_op jit(solution)/shard_map/all_gather | solution.py:264
Sparse Core Ops, SparseCore 0:
  12.0 80.3 all-gather.6
  95.4 79.8 all-gather.4
  177.8 38.0 all-reduce.1
  218.9 260.1 all-gather.8

commit v2 on v1

v2 whole, which is shorter than its diff:
```python
import functools
import math

import jax
import jax.numpy as jnp
from jax import lax
from jax.experimental import pallas as pl
from jax.experimental.pallas import tpu as pltpu
from jax.sharding import PartitionSpec as P

F32 = jnp.float32
BF16 = jnp.bfloat16
VMEM_LIMIT = 60 * 1024 * 1024


def halves(x):
    high = x.astype(BF16)
    return high, (x - high.astype(F32)).astype(BF16)


def dot(a, b):
    return jnp.dot(a, b, preferred_element_type=F32)


def dot_split(a, b):
    ah, al = halves(a)
    bh, bl = halves(b)
    return dot(ah, bh) + (dot(ah, bl) + dot(al, bh))


def split_kernel(cov_ref, out_ref):
    columns = cov_ref.shape[1]
    high, low = halves(cov_ref[...])
    out_ref[:, :columns] = high
    out_ref[:, columns:] = low


def split_slab(cov_slab):
    rows, columns = cov_slab.shape
    tile = 2048
    return pl.pallas_call(
        split_kernel,
        grid=(rows // tile,),
        in_specs=[pl.BlockSpec((tile, columns), lambda i: (i, 0))],
        out_specs=pl.BlockSpec((tile, 2 * columns), lambda i: (i, 0)),
        out_shape=jax.ShapeDtypeStruct((rows, 2 * columns), BF16),
        compiler_params=pltpu.CompilerParams(vmem_limit_bytes=VMEM_LIMIT),
        cost_estimate=pl.CostEstimate(flops=4 * rows * columns, bytes_accessed=8 * rows * columns, transcendentals=0),
        name="split",
    )(cov_slab)


def predict_kernel(place_ref, slots_ref, split_ref, out_ref, dense, *, tile, crossing, block):
    step = pl.program_id(0)
    rows, columns = split_ref.shape
    columns = columns // 2
    pairs = rows // (2 * block)
    deep = 2 * 2 * block
    quads = rows // deep
    lane = lax.broadcasted_iota(jnp.int32, (8, 2 * block), 1)
    sub = lax.broadcasted_iota(jnp.int32, (8, 2 * block), 0)
    upper = (lane >= block).astype(jnp.int32)

    @pl.when(step == 0)
    def _():
        def clear(i, c):
            dense[i] = jnp.zeros_like(dense[i])
            return c

        lax.fori_loop(0, pairs, clear, 0)

    def scatter(group, c):
        row = pl.multiple_of(group * 8, 8)
        first = (step * tile + row) * crossing
        blocks = slots_ref[pl.ds(row, 8), crossing * block :].astype(jnp.int32) & 1
        for n in range(crossing):
            if n % 2 == 0:
                plain = slots_ref[pl.ds(row, 8), pl.ds(n * block, 2 * block)]
                turned = pltpu.roll(plain, block, 1)
                both = jnp.where(upper == 0, plain, turned)
            else:
                both = jnp.where(upper == 0, turned, plain)
            half = blocks[:, n : n + 1] == upper
            for i in range(8):
                where = place_ref[first + i * crossing + n]
                pltpu.store(dense.at[where, pl.ds(row, 8), :], both, mask=half & (sub == i))
        return c

    lax.fori_loop(0, tile // 8, scatter, 0)
    out_ref[...] = jnp.zeros_like(out_ref)
    together = 8

    def multiply(i, c):
        wide_sum = jnp.zeros((tile, 2 * columns), F32)
        small = jnp.zeros((tile, columns), F32)
        for k in range(together):
            q = i * together + k
            here = pl.ds(pl.multiple_of(q * deep, deep), deep)
            wide = jnp.concatenate([dense[2 * q], dense[2 * q + 1]], axis=1)
            high, low = halves(wide)
            wide_sum = wide_sum + dot(high, split_ref[here, :])
            small = small + dot(low, split_ref[here, :columns])
            dense[2 * q] = jnp.zeros((tile, 2 * block), F32)
            dense[2 * q + 1] = jnp.zeros((tile, 2 * block), F32)
        out_ref[...] += wide_sum[:, :columns] + (wide_sum[:, columns:] + small)
        return c

    lax.fori_loop(0, quads // together, multiply, 0)


def predict(slots, slab_split, first_block, local_blocks, crossing, block):
    count, width = slots.shape
    rows, columns = slab_split.shape
    columns = columns // 2
    tile = 256
    lanes = crossing * block
    blocks = slots[:, lanes : lanes + crossing].astype(jnp.int32)
    local = blocks - first_block
    inside = (local >= 0) & (local < local_blocks) & (blocks >= 0)
    place = jnp.where(inside, local // 2, local_blocks // 2).reshape(-1)
    return pl.pallas_call(
        functools.partial(predict_kernel, tile=tile, crossing=crossing, block=block),
        grid_spec=pltpu.PrefetchScalarGridSpec(
            num_scalar_prefetch=1,
            grid=(count // tile,),
            in_specs=[
                pl.BlockSpec((tile, width), lambda i, place: (i, 0)),
                pl.BlockSpec(memory_space=pltpu.VMEM),
            ],
            out_specs=pl.BlockSpec((tile, columns), lambda i, place: (i, 0)),
            scratch_shapes=[pltpu.VMEM((rows // (2 * block) + 1, tile, 2 * block), F32)],
        ),
        out_shape=jax.ShapeDtypeStruct((count, columns), F32),
        compiler_params=pltpu.CompilerParams(vmem_limit_bytes=VMEM_LIMIT),
        cost_estimate=pl.CostEstimate(
            flops=12 * count * rows * columns, bytes_accessed=rows * columns * 4, transcendentals=0
        ),
        name="predict",
    )(place, slots, slab_split)


def sweep_rows(rows, first):
    sub = lax.broadcasted_iota(jnp.int32, rows.shape, 0)
    lane = lax.broadcasted_iota(jnp.int32, rows.shape, 1) - first
    cols = [jnp.broadcast_to(rows[:, first + j : first + j + 1], rows.shape) for j in range(8)]

    def row(v, p):
        return jnp.broadcast_to(v[p : p + 1, :], rows.shape)

    out = rows
    for p in range(0, 8, 2):
        q = p + 1
        a, b, d = row(cols[p], p), row(cols[q], p), row(cols[q], q)
        inv = 1.0 / (a * d - b * b)
        a, b, d = a * inv, b * inv, d * inv
        out = jnp.where((lane == p) | (lane == q), jnp.where(sub == lane, 1.0, 0.0), out)

        def eliminate(v):
            at_p, at_q = row(v, p), row(v, q)
            new_p = d * at_p - b * at_q
            new_q = a * at_q - b * at_p
            rest = v - cols[p] * new_p - cols[q] * new_q
            return jnp.where(sub == p, new_p, jnp.where(sub == q, new_q, rest))

        out = eliminate(out)
        cols = [eliminate(col) if j > q else col for j, col in enumerate(cols)]
    return jnp.where((lane >= 0) & (lane < 8), -out, out)


def small_sweep(block):
    size = block.shape[0]
    strip = 16
    lanes = lax.broadcasted_iota(jnp.int32, (8, size), 1)
    all_lanes = lax.broadcasted_iota(jnp.int32, (size, size), 1)
    for base in range(0, size, strip):
        rows = [block[at : at + 8, :] for at in range(base, base + strip, 8)]
        for g in range(strip // 8):
            first = base + 8 * g
            top = sweep_rows(rows[g], first)
            pivots = (lanes >= first) & (lanes < first + 8)
            for e in range(strip // 8):
                if e != g:
                    rest = jnp.where(pivots, 0.0, rows[e])
                    for j in range(8):
                        rest = rest - rows[e][:, first + j : first + j + 1] * top[j : j + 1, :]
                    rows[e] = rest
            rows[g] = top
        middle = jnp.concatenate(rows, axis=0)
        above = [jnp.zeros((base, size), F32)] if base else []
        below = [jnp.zeros((size - base - strip, size), F32)] if base + strip < size else []
        high, low = halves(jnp.concatenate(above + [middle] + below, axis=0))
        block_high, block_low = halves(block)
        keep = jnp.where((all_lanes >= base) & (all_lanes < base + strip), 0.0, block)
        new = keep - (
            dot(jnp.concatenate([block_high, block_low], axis=1), jnp.concatenate([high, high], axis=0))
            + dot(block_high, low)
        )
        above = [new[:base]] if base else []
        below = [new[base + strip :]] if base + strip < size else []
        block = jnp.concatenate(above + [middle] + below, axis=0)
    return block


def inverse_kernel(core_ref, own_ref, other_ref, m_ref, left, right, pivot, *, size):
    n = m_ref.shape[0]
    regions, share, _ = own_ref.shape
    core = core_ref[0]

    def place(i, c):
        mine = pl.multiple_of((2 * i + core) * share, share)
        theirs = pl.multiple_of((2 * i + 1 - core) * share, share)
        m_ref[pl.ds(mine, share), :] = own_ref[i]
        m_ref[pl.ds(theirs, share), :] = other_ref[i]
        return c

    lax.fori_loop(0, regions, place, 0)

    def sweep(k, c):
        at = pl.ds(pl.multiple_of(k * size, size), size)
        minus = small_sweep(m_ref[at, at])
        pivot[...] = dot_split(minus, m_ref[at, :]) * -1.0
        pivot[:, at] = minus
        high, low = halves(m_ref[:, at])
        left[:, :size] = high
        left[:, size:] = low
        m_ref[:, at] = jnp.zeros((n, size), F32)
        high, low = halves(pivot[...])
        right[:size, :] = high
        right[size : 2 * size, :] = high
        right[2 * size :, :] = low
        wide = n // 2

        def update(i, c):
            here = pl.ds(pl.multiple_of(i * wide, wide), wide)
            product = dot(left[...], right[: 2 * size, here]) + dot(left[:, :size], right[2 * size :, here])
            m_ref[:, here] = m_ref[:, here] - product
            return c

        lax.fori_loop(0, n // wide, update, 0)
        m_ref[at, :] = pivot[...]
        return c

    lax.fori_loop(0, n // size, sweep, 0)


def minus_inverse(core, own, other):
    n = own.shape[2]
    size = 128
    return pl.pallas_call(
        functools.partial(inverse_kernel, size=size),
        in_specs=[pl.BlockSpec(memory_space=pltpu.SMEM)] + [pl.BlockSpec(memory_space=pltpu.VMEM)] * 2,
        out_specs=pl.BlockSpec(memory_space=pltpu.VMEM),
        out_shape=jax.ShapeDtypeStruct((n, n), F32),
        scratch_shapes=[
            pltpu.VMEM((n, 2 * size), BF16),
            pltpu.VMEM((3 * size, n), BF16),
            pltpu.VMEM((size, n), F32),
        ],
        compiler_params=pltpu.CompilerParams(vmem_limit_bytes=VMEM_LIMIT),
        cost_estimate=pl.CostEstimate(flops=60 * n * n * n, bytes_accessed=8 * n * n, transcendentals=0),
        name="minus_inverse",
    )(core, own, other)


def solve_kernel(minus_ref, predicted_ref, out_ref):
    predicted = predicted_ref[...].reshape(minus_ref.shape[0], -1)
    out_ref[...] = (-dot_split(predicted.T, minus_ref[...])).astype(BF16)


def solve_turned(minus, predicted):
    n, columns = minus.shape[0], predicted.shape[-1]
    return pl.pallas_call(
        solve_kernel,
        in_specs=[pl.BlockSpec(memory_space=pltpu.VMEM)] * 2,
        out_specs=pl.BlockSpec(memory_space=pltpu.VMEM),
        out_shape=jax.ShapeDtypeStruct((columns, n), BF16),
        compiler_params=pltpu.CompilerParams(vmem_limit_bytes=VMEM_LIMIT),
        cost_estimate=pl.CostEstimate(flops=6 * n * n * columns, bytes_accessed=4 * n * n, transcendentals=0),
        name="solve",
    )(minus, predicted)


def spread_kernel(by_x_ref, by_y_ref, out_ref):
    out_ref[0, 0] = by_x_ref[...]
    out_ref[0, 1] = by_y_ref[...]


def spread(turned):
    slots, rows = turned.shape
    width = rows // 8
    everyone = math.prod(SIZES)
    return pl.pallas_call(
        spread_kernel,
        grid=(everyone,),
        in_specs=[
            pl.BlockSpec((slots, width), lambda i: (0, i % 4)),
            pl.BlockSpec((slots, width), lambda i: (0, 4 + i // 8)),
        ],
        out_specs=pl.BlockSpec((1, 2, slots, width), lambda i: (i, 0, 0, 0)),
        out_shape=jax.ShapeDtypeStruct((everyone, 2, slots, width), turned.dtype),
        compiler_params=pltpu.CompilerParams(vmem_limit_bytes=VMEM_LIMIT),
        cost_estimate=pl.CostEstimate(flops=0, bytes_accessed=16 * slots * rows, transcendentals=0),
        name="spread",
    )(turned, turned)


def product_kernel(*refs, members):
    solved_refs, cross_ref, out_refs, stack = refs[:members], refs[members], refs[members + 1 : -1], refs[-1]
    columns = solved_refs[0].shape[0]

    @pl.when(pl.program_id(0) == 0)
    def _():
        for i, ref in enumerate(solved_refs):
            stack[i * columns : (i + 1) * columns, :] = ref[...]

    everyone, _, slots, tile = cross_ref.shape
    product = dot(stack[...], cross_ref[...].reshape(everyone * slots, tile))
    for i, ref in enumerate(out_refs):
        ref[...] = product[i * columns : (i + 1) * columns, :].astype(ref.dtype)


def products(solved, cross, half):
    members = len(solved)
    columns, n = solved[0].shape
    everyone, _, slots, width = cross.shape
    tile = 512
    return pl.pallas_call(
        functools.partial(product_kernel, members=members),
        grid=(width // tile,),
        in_specs=[pl.BlockSpec(memory_space=pltpu.VMEM)] * members
        + [pl.BlockSpec((everyone, 1, slots, tile), lambda i: (0, half, 0, i))],
        out_specs=[pl.BlockSpec((columns, tile), lambda i: (0, i))] * members,
        out_shape=[jax.ShapeDtypeStruct((columns, width), BF16 if i else F32) for i in range(members)],
        scratch_shapes=[pltpu.VMEM((members * columns, n), BF16)],
        compiler_params=pltpu.CompilerParams(vmem_limit_bytes=VMEM_LIMIT),
        cost_estimate=pl.CostEstimate(
            flops=2 * members * columns * n * width, bytes_accessed=2 * n * width, transcendentals=0
        ),
        name="products",
    )(*solved, cross)


def downdate_kernel(chunk_ref, *refs):
    product_refs, cov_ref, out_ref = refs[:-2], refs[-2], refs[-1]
    for i, ref in enumerate(product_refs):

        @pl.when(pl.program_id(0) == i)
        def _():
            out_ref[...] = cov_ref[...] - ref[...].astype(F32).T


def downdate(chunks, parts, cov_slab):
    rows, columns = cov_slab.shape
    tile = rows // len(parts)
    return pl.pallas_call(
        downdate_kernel,
        grid_spec=pltpu.PrefetchScalarGridSpec(
            num_scalar_prefetch=1,
            grid=(len(parts),),
            in_specs=[pl.BlockSpec(memory_space=pltpu.VMEM)] * len(parts)
            + [pl.BlockSpec((tile, columns), lambda i, chunk: (chunk[i], 0))],
            out_specs=pl.BlockSpec((tile, columns), lambda i, chunk: (chunk[i], 0)),
        ),
        out_shape=jax.ShapeDtypeStruct((rows, columns), F32),
        compiler_params=pltpu.CompilerParams(vmem_limit_bytes=VMEM_LIMIT),
        cost_estimate=pl.CostEstimate(flops=rows * columns, bytes_accessed=10 * rows * columns, transcendentals=0),
        name="downdate",
    )(chunks, *parts, cov_slab)


def merged(ray_blocks, weights):
    slots, crossing = ray_blocks.shape
    same = ray_blocks[:, :, None] == ray_blocks[:, None, :]
    order = jnp.arange(crossing, dtype=jnp.int32)
    first = ~jnp.any(same & (order[None, None, :] < order[None, :, None]), axis=2)
    parts = weights.reshape(slots, crossing, -1)
    total = jnp.sum(jnp.where(same[:, :, :, None], parts[:, None, :, :], 0.0), axis=2)
    return jnp.where(first, ray_blocks, -1), total.reshape(weights.shape)


SIZES = (4, 2, 4)
SWAP = [(0, 1), (1, 0), (2, 3), (3, 2)]


def steps_along(axis, distance):
    pairs = []
    for y in range(SIZES[0]):
        for z in range(SIZES[1]):
            for x in range(SIZES[2]):
                to = [y, z, x]
                to[axis] = (to[axis] + distance) % SIZES[axis]
                pairs.append(((y * SIZES[1] + z) * SIZES[2] + x, (to[0] * SIZES[1] + to[1]) * SIZES[2] + to[2]))
    return pairs


def to_all(piece):
    everyone = math.prod(SIZES)
    return lax.all_to_all(jnp.broadcast_to(piece[None], (everyone,) + piece.shape), "obs", 0, 0)


def shards(cov_slab, cross_cov, ray_blocks, ray_coeff, region_rows, innov_cov):
    local_rows, columns = cov_slab.shape
    slot_count, crossing = ray_blocks.shape
    block_size = ray_coeff.shape[1] // crossing
    local_blocks = local_rows // block_size
    everyone = math.prod(SIZES)
    device = lax.axis_index("obs")
    core = lax.axis_index("vox") % 2
    core_array = core.astype(jnp.int32).reshape(1)
    share = slot_count // 2
    start = core * share

    my_blocks = lax.dynamic_slice_in_dim(ray_blocks, start, share, 0)
    my_coeff = lax.dynamic_slice_in_dim(ray_coeff, start, share, 0)
    live = start + jnp.arange(share, dtype=jnp.int32) < region_rows[0]
    weights = jnp.where(live[:, None], my_coeff, 0.0)
    blocks, weights = merged(my_blocks, weights)
    message = jnp.concatenate([weights, jnp.pad(blocks.astype(F32), ((0, 0), (0, 128 - crossing)))], axis=1)
    own = to_all(message)

    slab_split = split_slab(cov_slab)
    send = spread(cross_cov.T)
    my_innov = lax.dynamic_slice_in_dim(innov_cov, start, share, 0)
    own, send, slab_split, my_innov = lax.optimization_barrier((own, send, slab_split, my_innov))
    innov_own = to_all(my_innov)
    other = lax.ppermute(own, "vox", SWAP)
    first_block = lax.axis_index("vox") * local_blocks
    flat = (everyone * share, -1)
    partial_own = predict(own.reshape(flat), slab_split, first_block, local_blocks, crossing, block_size)
    innov_own, send, other, partial_own = lax.optimization_barrier((innov_own, send, other, partial_own))
    cross = lax.all_to_all(send, "obs", 0, 0)
    innov_other = lax.ppermute(innov_own, "vox", SWAP)
    partial_other = predict(other.reshape(flat), slab_split, first_block, local_blocks, crossing, block_size)

    mine = partial_own + lax.ppermute(partial_other, "vox", SWAP)
    theirs = partial_other + lax.ppermute(partial_own, "vox", SWAP)
    low = jnp.where(core == 0, mine, theirs).reshape(everyone, 1, share, columns)
    high = jnp.where(core == 0, theirs, mine).reshape(everyone, 1, share, columns)
    chip_sum = jnp.concatenate([low, high], axis=1)
    chip_sum, innov_own, innov_other = lax.optimization_barrier((chip_sum, innov_own, innov_other))
    predicted = chip_sum + lax.ppermute(chip_sum, "vox", [(0, 2), (2, 0), (1, 3), (3, 1)])
    minus = minus_inverse(core_array, innov_own, innov_other)
    solved = solve_turned(minus, predicted)

    at_x = device % 4
    at_y = device // 8
    from_x = [lax.ppermute(solved, "obs", steps_along(2, d)) for d in (1, 3, 2)]
    from_y = [lax.ppermute(solved, "obs", steps_along(0, d)) for d in (1, 3, 2)]
    solved, from_x, from_y = lax.optimization_barrier((solved, from_x, from_y))
    parts_x = products([solved] + from_x, cross, 0)
    back_x = [lax.ppermute(part, "obs", steps_along(2, -d)) for part, d in zip(parts_x[1:], (1, 3, 2))]
    parts_y = products([solved] + from_y, cross, 1)
    back_y = [lax.ppermute(part, "obs", steps_along(0, -d)) for part, d in zip(parts_y[1:], (1, 3, 2))]
    chunks = jnp.stack([(at_x + d) % 4 for d in (0, 1, 3, 2)] + [4 + (at_y + d) % 4 for d in (0, 1, 3, 2)])
    parts = [parts_x[0]] + back_x + [parts_y[0]] + back_y
    return downdate(chunks.astype(jnp.int32), parts, cov_slab)


def solution(mesh):
    placed = (
        P("vox", "obs"),
        P("vox", "obs"),
        P("obs", None),
        P("obs", None),
        P("obs"),
        P("obs", None),
    )
    return jax.shard_map(
        shards, mesh=mesh, in_specs=placed, out_specs=P("vox", "obs"), check_vma=False
    )
```

time: 515 us -> 301 us (0.58)
  waiting for transfers between devices: 255 us -> 42.1 us
  blocking collectives: 79.4 us -> 0 us
  starting transfers between devices: 0.12 us -> 66.2 us
  Pallas kernels: 156 us -> 175 us
  between operations: 13.8 us -> 0.93 us
  local copies, waits for them, and re-layouts: 2.08 us -> 8.24 us
    all_gather x3 -> x0, waiting for transfers between devices: 254 us -> none  [the longest x1 235 us: shards(): cross_turned = lax.all_gather(cross_cov.T, 'obs', axis=0, tiled=True)]
    all_gather x1 -> x0, blocking collectives: 79.4 us -> none  [shards(): blocks = lax.all_gather(blocks, 'obs', axis=0, tiled=True)]
    ppermute x0 -> x17, waiting for transfers between devices: none -> 39.3 us  [the longest x3 12.6 us: shards(): from_y = [lax.ppermute(solved, 'obs', steps_along(0, d)) for d in (1, 3, 2)]]
    ppermute x0 -> x17, starting transfers between devices: none -> 38.1 us  [the longest x3 14.9 us: shards(): from_y = [lax.ppermute(solved, 'obs', steps_along(0, d)) for d in (1, 3, 2)]]
    pallas_call x1 -> x6, Pallas kernels: 25.4 us -> 56.5 us  [the longest x1 18.7 us: spread(): pl.pallas_call(spread_kernel, grid=(everyone,), in_specs=[pl.BlockSpec((s...]
    all_to_all x0 -> x3, starting transfers between devices: none -> 28.1 us  [the longest x2 18.2 us: to_all(): lax.all_to_all(jnp.broadcast_to(piece[None], (everyone,) + piece.shape),...]
    pallas_call x1, Pallas kernels: 68.9 us -> 55 us  [minus_inverse(): pl.pallas_call(functools.partial(inverse_kernel, size=size), in_specs=[pl...]
    pallas_call x1 -> x2, Pallas kernels: 61.5 us -> 63.3 us  [predict(): pl.pallas_call(functools.partial(predict_kernel, tile=tile, crossing=cros...]
  transfers between devices with their start and end apart: 4 -> 20, of which waited for: 2 -> 10; matrix products, arithmetic and copies ran while one was open for 0% -> 2% of each run, Pallas kernels for 26% -> 53%
where the time goes in v2:
time: 301 us; the launch traced here: 298 us
  Pallas kernels  175 us (58%)
  starting transfers between devices  66.2 us (22%)
  waiting for transfers between devices  42.1 us (14%)
  local copies, waits for them, and re-layouts  8.24 us (3%)
  other arithmetic  5.56 us (2%)
    pallas_call x2, Pallas kernels, predict(): pl.pallas_call(functools.partial(predict_kernel, tile=tile, crossing=cros...  63.3 us
    pallas_call x1, Pallas kernels, minus_inverse(): pl.pallas_call(functools.partial(inverse_kernel, size=size), in_specs=[pl...  55 us
    pallas_call x1, Pallas kernels, spread(): pl.pallas_call(spread_kernel, grid=(everyone,), in_specs=[pl.BlockSpec((s...  18.7 us
    all_to_all x2, starting transfers between devices, to_all(): lax.all_to_all(jnp.broadcast_to(piece[None], (everyone,) + piece.shape),...  18.2 us
    ppermute x3, starting transfers between devices, shards(): from_y = [lax.ppermute(solved, 'obs', steps_along(0, d)) for d in (1, 3, 2)]  14.9 us
    ppermute x3, waiting for transfers between devices, shards(): from_y = [lax.ppermute(solved, 'obs', steps_along(0, d)) for d in (1, 3, 2)]  12.6 us
    pallas_call x1, Pallas kernels, downdate(): pl.pallas_call(downdate_kernel, grid_spec=pltpu.PrefetchScalarGridSpec(nu...  12.2 us
    pallas_call x2, Pallas kernels, products(): pl.pallas_call(functools.partial(product_kernel, members=members), grid=(...  12.1 us
  transfers between devices with their start and end apart: 20, of which 10 were waited for; matrix products, arithmetic and copies ran while one was open for 2% of the time, Pallas kernels for 53%

profile of v2, /device:TPU:66, one launch (start us, length us, event | category | flops | bytes accessed | tf_op | source)
XLA Modules:
  0.0 297.9 jit_solution(13976350924543659115)
XLA Ops:
  5.6 10.0 %all-to-all-start = ((f32[32,16,1152]{2,1,0:T(8,128)}), f32[32,16,1152]{2,1,0:T(8,128)S(1)}, u32[]{:S(2)}, u32[]{:S(2)}) async-start(f32[32,16,1152]{2,1,0:T(8,128)} %broadcast_in_dim.68), calls=%async_computation | async-start | bytes 4718592 | tf_op jit(solution)/shard_map/all_to_all | solution.py:398
  15.7 18.7 %spread.1 = bf16[32,2,32,2048]{3,2,1,0:T(8,128)(2,1)} custom-call(bf16[32,16384]{1,0:T(8,128)(2,1)} %bitcast.16, bf16[32,16384]{1,0:T(8,128)(2,1)} %bitcast.17), custom_call_target="tpu_custom_call" | custom-call | bytes 8388608 | tf_op jit(solution)/shard_map/spread/pallas_call | solution.py:292
  34.4 9.3 %split.1.split_ref = bf16[16384,256]{1,0:T(8,128)(2,1)} custom-call(f32[16384,128]{1,0:T(8,128)} %refs_8_.1), custom_call_target="tpu_custom_call" | custom-call | flops 8388608 | bytes 16777216 | tf_op jit(solution)/shard_map/split/pallas_call | solution.py:41
  43.7 2.8 all-to-all-done
  48.4 8.2 %all-to-all-start.1 = ((f32[32,16,1024]{2,1,0:T(8,128)}), f32[32,16,1024]{2,1,0:T(8,128)}, u32[]{:S(2)}, u32[]{:S(2)}) async-start(f32[32,16,1024]{2,1,0:T(8,128)} %broadcast_in_dim.69), calls=%async_computation.1 | async-start | bytes 4194304 | tf_op jit(solution)/shard_map/all_to_all | solution.py:398
  57.7 31.6 %predict.2 = f32[512,128]{1,0:T(8,128)} custom-call(s32[8192]{0:T(1024)} %reshape.53.place_ref, f32[512,1152]{1,0:T(8,128)} %bitcast.19, bf16[16384,256]{1,0:T(8,128)(2,1)} %split.1.split_ref), custom_call_target="tpu_custom_call" | custom-call | flops 12884901888 | bytes 8388608 | tf_op jit(solution)/shard_map/predict/pallas_call | solution.py:121
  91.2 9.9 %all-to-all-start.2 = ((bf16[32,2,32,2048]{3,2,1,0:T(8,128)(2,1)}), bf16[32,2,32,2048]{3,2,1,0:T(8,128)(2,1)}, u32[]{:S(2)}, u32[]{:S(2)}) async-start(bf16[32,2,32,2048]{3,2,1,0:T(8,128)(2,1)} %spread.1), calls=%async_computation.2 | async-start | bytes 16777216 | tf_op jit(solution)/shard_map/all_to_all | solution.py:431
  101.1 31.7 %predict.3 = f32[512,128]{1,0:T(8,128)} custom-call(s32[8192]{0:T(1024)} %reshape.55.place_ref, f32[512,1152]{1,0:T(8,128)} %bitcast.12.slots_ref, bf16[16384,256]{1,0:T(8,128)(2,1)} %split.1.split_ref), custom_call_target="tpu_custom_call" | custom-call | flops 12884901888 | bytes 8388608 | tf_op jit(solution)/shard_map/predict/pallas_call | solution.py:121
  137.5 55.0 %minus_inverse.1.minus_ref = f32[1024,1024]{1,0:T(8,128)} custom-call(s32[1]{0:T(128)} %bitcast.8.core_ref, f32[32,16,1024]{2,1,0:T(8,128)} %all-to-all-done.1.own_ref, f32[32,16,1024]{2,1,0:T(8,128)} %collective-permute-done.3.other_ref), custom_call_target="tpu_custom_call" | custom-call | flops 64424509440 | bytes 8388608 | tf_op jit(solution)/shard_map/minus_inverse/pallas_call | solution.py:249
  193.4 4.2 %solve.1.refs_0_ = bf16[128,1024]{1,0:T(8,128)(2,1)} custom-call(f32[1024,1024]{1,0:T(8,128)} %minus_inverse.1.minus_ref, f32[32,2,16,128]{3,2,1,0:T(8,128)} %add.115.predicted_ref), custom_call_target="tpu_custom_call" | custom-call | flops 805306368 | bytes 4194304 | tf_op jit(solution)/shard_map/solve/pallas_call | solution.py:272
  197.6 3.0 %collective-permute-start.10 = (bf16[128,1024]{1,0:T(8,128)(2,1)}, bf16[128,1024]{1,0:T(8,128)(2,1)S(1)}, u32[]{:S(2)}, u32[]{:S(2)}) collective-permute-start(bf16[128,1024]{1,0:T(8,128)(2,1)} %solve.1.refs_0_), channel_id=1, source_target_pairs={{0,64},{4,68},{8,72},{12,76},{16,80},{20,84},{24,88},{28,92},{32,9... | collective-permute-start | bytes 786440 | tf_op jit(solution)/shard_map/ppermute | solution.py:448
  200.6 6.0 %collective-permute-start.5 = (bf16[128,1024]{1,0:T(8,128)(2,1)}, bf16[128,1024]{1,0:T(8,128)(2,1)S(1)}, u32[]{:S(2)}, u32[]{:S(2)}) collective-permute-start(bf16[128,1024]{1,0:T(8,128)(2,1)} %solve.1.refs_0_), channel_id=1, source_target_pairs={{0,4},{4,8},{8,12},{12,0},{16,20},{20,24},{24,28},{28,16},{32,36},... | collective-permute-start | bytes 786440 | tf_op jit(solution)/shard_map/ppermute | solution.py:447
  206.6 3.2 %collective-permute-start.7 = (bf16[128,1024]{1,0:T(8,128)(2,1)}, bf16[128,1024]{1,0:T(8,128)(2,1)S(1)}, u32[]{:S(2)}, u32[]{:S(2)}) collective-permute-start(bf16[128,1024]{1,0:T(8,128)(2,1)} %solve.1.refs_0_), channel_id=1, source_target_pairs={{0,8},{4,12},{8,0},{12,4},{16,24},{20,28},{24,16},{28,20},{32,40},... | collective-permute-start | bytes 786440 | tf_op jit(solution)/shard_map/ppermute | solution.py:447
  209.8 9.7 %collective-permute-done.10.refs_3_ = bf16[128,1024]{1,0:T(8,128)(2,1)S(1)} collective-permute-done((bf16[128,1024]{1,0:T(8,128)(2,1)}, bf16[128,1024]{1,0:T(8,128)(2,1)S(1)}, u32[]{:S(2)}, u32[]{:S(2)}) %collective-permute-start.10) | collective-permute-done | bytes 262176 | tf_op jit(solution)/shard_map/ppermute | solution.py:448
  219.6 11.9 %collective-permute-start.9 = (bf16[128,1024]{1,0:T(8,128)(2,1)}, bf16[128,1024]{1,0:T(8,128)(2,1)S(1)}, u32[]{:S(2)}, u32[]{:S(2)}) collective-permute-start(bf16[128,1024]{1,0:T(8,128)(2,1)} %solve.1.refs_0_), channel_id=1, source_target_pairs={{0,96},{4,100},{8,104},{12,108},{16,112},{20,116},{24,120},{28,124... | collective-permute-start | bytes 786440 | tf_op jit(solution)/shard_map/ppermute | solution.py:448
  231.4 2.9 collective-permute-done.5.refs_1_
  234.4 2.8 collective-permute-done.9.refs_2_
  237.9 6.1 %products.3 = (f32[128,2048]{1,0:T(8,128)}, bf16[128,2048]{1,0:T(8,128)(2,1)}, bf16[128,2048]{1,0:T(8,128)(2,1)}, bf16[128,2048]{1,0:T(8,128)(2,1)}) custom-call(bf16[128,1024]{1,0:T(8,128)(2,1)} %solve.1.refs_0_, bf16[128,1024]{1,0:T(8,128)(2,1)} %copy-done.13, bf16[128,1024]{1,0:T(8,128)(2,1)} %copy-done.14, bf16[128,1024]{1,0:T(8,128)(2,1)} %copy-done.12, ...), custom_call_target="tpu_custom_call" | custom-call | flops 2147483648 | bytes 4194304 | tf_op jit(solution)/shard_map/products/pallas_call | solution.py:327
  244.0 4.4 %collective-permute-start.14 = (bf16[128,2048]{1,0:T(8,128)(2,1)}, bf16[128,2048]{1,0:T(8,128)(2,1)S(1)}, u32[]{:S(2)}, u32[]{:S(2)}) collective-permute-start(bf16[128,2048]{1,0:T(8,128)(2,1)} %get-tuple-element.54), channel_id=1, source_target_pairs={{0,96},{4,100},{8,104},{12,108},{16,112},{20,116},{24,120},{28,124... | collective-permute-start | bytes 1572872 | tf_op jit(solution)/shard_map/ppermute | solution.py:453
  249.9 6.0 %products.2 = (f32[128,2048]{1,0:T(8,128)}, bf16[128,2048]{1,0:T(8,128)(2,1)}, bf16[128,2048]{1,0:T(8,128)(2,1)}, bf16[128,2048]{1,0:T(8,128)(2,1)}) custom-call(bf16[128,1024]{1,0:T(8,128)(2,1)} %solve.1.refs_0_, bf16[128,1024]{1,0:T(8,128)(2,1)} %copy-done.9, bf16[128,1024]{1,0:T(8,128)(2,1)} %copy-done.10, bf16[128,1024]{1,0:T(8,128)(2,1)} %copy-done.11, ...), custom_call_target="tpu_custom_call" | custom-call | flops 2147483648 | bytes 4194304 | tf_op jit(solution)/shard_map/products/pallas_call | solution.py:327
  256.0 4.6 %collective-permute-start.11 = (bf16[128,2048]{1,0:T(8,128)(2,1)}, bf16[128,2048]{1,0:T(8,128)(2,1)S(1)}, u32[]{:S(2)}, u32[]{:S(2)}) collective-permute-start(bf16[128,2048]{1,0:T(8,128)(2,1)} %get-tuple-element.47), channel_id=1, source_target_pairs={{0,12},{4,0},{8,4},{12,8},{16,28},{20,16},{24,20},{28,24},{32,44},... | collective-permute-start | bytes 1572872 | tf_op jit(solution)/shard_map/ppermute | solution.py:451
  261.7 8.9 %collective-permute-done.14.refs_5_ = bf16[128,2048]{1,0:T(8,128)(2,1)S(1)} collective-permute-done((bf16[128,2048]{1,0:T(8,128)(2,1)}, bf16[128,2048]{1,0:T(8,128)(2,1)S(1)}, u32[]{:S(2)}, u32[]{:S(2)}) %collective-permute-start.14) | collective-permute-done | bytes 524320 | tf_op jit(solution)/shard_map/ppermute | solution.py:453
  275.6 9.3 %collective-permute-done.13.refs_3_ = bf16[128,2048]{1,0:T(8,128)(2,1)S(1)} collective-permute-done((bf16[128,2048]{1,0:T(8,128)(2,1)}, bf16[128,2048]{1,0:T(8,128)(2,1)S(1)}, u32[]{:S(2)}, u32[]{:S(2)}) %collective-permute-start.13) | collective-permute-done | bytes 524320 | tf_op jit(solution)/shard_map/ppermute | solution.py:451
  285.7 12.2 %downdate.1 = f32[16384,128]{1,0:T(8,128)} custom-call(s32[8]{0:T(128)} %stack.35.chunk_ref, f32[128,2048]{1,0:T(8,128)} %get-tuple-element.46.refs_0_, bf16[128,2048]{1,0:T(8,128)(2,1)} %copy-done.6, bf16[128,2048]{1,0:T(8,128)(2,1)} %copy-done.7, bf16[128,2048]{1,0:T(8,128)(2,1)} %copy-done.8, f32[128,2048]{1,0:T(8,128)} %get-tuple-element.53.refs_4_, ...), custom_call_target="tpu_custom_call" | custom-call | flops 2097152 | bytes 20971520 | tf_op jit(solution)/shard_map/downdate/pallas_call | solution.py:355
  (79 shorter events, 24.4 us)
Async XLA Ops:
  0.0 43.7 %copy-start = (f32[32,1024]{1,0:T(8,128)S(1)}, f32[32,1024]{1,0:T(8,128)}, u32[]{:S(2)}) copy-start(f32[32,1024]{1,0:T(8,128)} %param.11) | copy-start | bytes 393220
  5.6 41.0 %all-to-all-start = ((f32[32,16,1152]{2,1,0:T(8,128)}), f32[32,16,1152]{2,1,0:T(8,128)S(1)}, u32[]{:S(2)}, u32[]{:S(2)}) async-start(f32[32,16,1152]{2,1,0:T(8,128)} %broadcast_in_dim.68), calls=%async_computation | async-start | bytes 4718592 | tf_op jit(solution)/shard_map/all_to_all | solution.py:398
  46.6 42.6 %collective-permute-start = (f32[32,16,1152]{2,1,0:T(8,128)S(1)}, f32[32,16,1152]{2,1,0:T(8,128)}, u32[]{:S(2)}, u32[]{:S(2)}) collective-permute-start(f32[32,16,1152]{2,1,0:T(8,128)S(1)} %all-to-all-done), channel_id=1, source_target_pairs={{0,1},{1,0},{2,3},{3,2},{4,5},{5,4},{6,7},{7,6},{8,9},{9,8},{10,11... | collective-permute-start | bytes 7077896 | tf_op jit(solution)/shard_map/ppermute | solution.py:426
  48.4 40.8 %all-to-all-start.1 = ((f32[32,16,1024]{2,1,0:T(8,128)}), f32[32,16,1024]{2,1,0:T(8,128)}, u32[]{:S(2)}, u32[]{:S(2)}) async-start(f32[32,16,1024]{2,1,0:T(8,128)} %broadcast_in_dim.69), calls=%async_computation.1 | async-start | bytes 4194304 | tf_op jit(solution)/shard_map/all_to_all | solution.py:398
  89.2 46.5 %collective-permute-start.3 = (f32[32,16,1024]{2,1,0:T(8,128)}, f32[32,16,1024]{2,1,0:T(8,128)}, u32[]{:S(2)}, u32[]{:S(2)}) collective-permute-start(f32[32,16,1024]{2,1,0:T(8,128)} %all-to-all-done.1.own_ref), channel_id=1, source_target_pairs={{0,1},{1,0},{2,3},{3,2},{4,5},{5,4},{6,7},{7,6},{8,9},{9,8},{10,11... | collective-permute-start | bytes 6291464 | tf_op jit(solution)/shard_map/ppermute | solution.py:432
  91.2 146.0 %all-to-all-start.2 = ((bf16[32,2,32,2048]{3,2,1,0:T(8,128)(2,1)}), bf16[32,2,32,2048]{3,2,1,0:T(8,128)(2,1)}, u32[]{:S(2)}, u32[]{:S(2)}) async-start(bf16[32,2,32,2048]{3,2,1,0:T(8,128)(2,1)} %spread.1), calls=%async_computation.2 | async-start | bytes 16777216 | tf_op jit(solution)/shard_map/all_to_all | solution.py:431
  101.1 31.7 %copy-start.15 = (f32[512,128]{1,0:T(8,128)S(1)}, f32[512,128]{1,0:T(8,128)}, u32[]{:S(2)}) copy-start(f32[512,128]{1,0:T(8,128)} %predict.2) | copy-start | bytes 786436
  132.8 1.7 collective-permute-start.1
  132.8 1.9 collective-permute-start.2
  135.8 56.7 %collective-permute-start.4 = (f32[32,2,16,128]{3,2,1,0:T(8,128)S(1)}, f32[32,2,16,128]{3,2,1,0:T(8,128)S(1)}, u32[]{:S(2)}, u32[]{:S(2)}) collective-permute-start(f32[32,2,16,128]{3,2,1,0:T(8,128)S(1)} %pad_maximum_fusion), channel_id=1, source_target_pairs={{0,2},{2,0},{1,3},{3,1},{4,6},{6,4},{5,7},{7,5},{8,10},{10,8},{9,1... | collective-permute-start | bytes 1572872 | tf_op jit(solution)/shard_map/ppermute | solution.py:441
  197.6 21.9 %collective-permute-start.10 = (bf16[128,1024]{1,0:T(8,128)(2,1)}, bf16[128,1024]{1,0:T(8,128)(2,1)S(1)}, u32[]{:S(2)}, u32[]{:S(2)}) collective-permute-start(bf16[128,1024]{1,0:T(8,128)(2,1)} %solve.1.refs_0_), channel_id=1, source_target_pairs={{0,64},{4,68},{8,72},{12,76},{16,80},{20,84},{24,88},{28,92},{32,9... | collective-permute-start | bytes 786440 | tf_op jit(solution)/shard_map/ppermute | solution.py:448
  200.6 33.8 %collective-permute-start.5 = (bf16[128,1024]{1,0:T(8,128)(2,1)}, bf16[128,1024]{1,0:T(8,128)(2,1)S(1)}, u32[]{:S(2)}, u32[]{:S(2)}) collective-permute-start(bf16[128,1024]{1,0:T(8,128)(2,1)} %solve.1.refs_0_), channel_id=1, source_target_pairs={{0,4},{4,8},{8,12},{12,0},{16,20},{20,24},{24,28},{28,16},{32,36},... | collective-permute-start | bytes 786440 | tf_op jit(solution)/shard_map/ppermute | solution.py:447
  206.6 27.8 %collective-permute-start.6 = (bf16[128,1024]{1,0:T(8,128)(2,1)}, bf16[128,1024]{1,0:T(8,128)(2,1)S(1)}, u32[]{:S(2)}, u32[]{:S(2)}) collective-permute-start(bf16[128,1024]{1,0:T(8,128)(2,1)} %solve.1.refs_0_), channel_id=1, source_target_pairs={{0,12},{4,0},{8,4},{12,8},{16,28},{20,16},{24,20},{28,24},{32,44},... | collective-permute-start | bytes 786440 | tf_op jit(solution)/shard_map/ppermute | solution.py:447
  206.6 27.8 %collective-permute-start.7 = (bf16[128,1024]{1,0:T(8,128)(2,1)}, bf16[128,1024]{1,0:T(8,128)(2,1)S(1)}, u32[]{:S(2)}, u32[]{:S(2)}) collective-permute-start(bf16[128,1024]{1,0:T(8,128)(2,1)} %solve.1.refs_0_), channel_id=1, source_target_pairs={{0,8},{4,12},{8,0},{12,4},{16,24},{20,28},{24,16},{28,20},{32,40},... | collective-permute-start | bytes 786440 | tf_op jit(solution)/shard_map/ppermute | solution.py:447
  209.8 24.6 %collective-permute-start.8 = (bf16[128,1024]{1,0:T(8,128)(2,1)}, bf16[128,1024]{1,0:T(8,128)(2,1)S(1)}, u32[]{:S(2)}, u32[]{:S(2)}) collective-permute-start(bf16[128,1024]{1,0:T(8,128)(2,1)} %solve.1.refs_0_), channel_id=1, source_target_pairs={{0,32},{4,36},{8,40},{12,44},{16,48},{20,52},{24,56},{28,60},{32,6... | collective-permute-start | bytes 786440 | tf_op jit(solution)/shard_map/ppermute | solution.py:448
  219.6 17.7 %copy-start.12 = (bf16[128,1024]{1,0:T(8,128)(2,1)}, bf16[128,1024]{1,0:T(8,128)(2,1)S(1)}, u32[]{:S(2)}) copy-start(bf16[128,1024]{1,0:T(8,128)(2,1)S(1)} %collective-permute-done.10.refs_3_) | copy-start | bytes 786436
  219.6 17.7 %collective-permute-start.9 = (bf16[128,1024]{1,0:T(8,128)(2,1)}, bf16[128,1024]{1,0:T(8,128)(2,1)S(1)}, u32[]{:S(2)}, u32[]{:S(2)}) collective-permute-start(bf16[128,1024]{1,0:T(8,128)(2,1)} %solve.1.refs_0_), channel_id=1, source_target_pairs={{0,96},{4,100},{8,104},{12,108},{16,112},{20,116},{24,120},{28,124... | collective-permute-start | bytes 786440 | tf_op jit(solution)/shard_map/ppermute | solution.py:448
  244.0 26.7 %collective-permute-start.14 = (bf16[128,2048]{1,0:T(8,128)(2,1)}, bf16[128,2048]{1,0:T(8,128)(2,1)S(1)}, u32[]{:S(2)}, u32[]{:S(2)}) collective-permute-start(bf16[128,2048]{1,0:T(8,128)(2,1)} %get-tuple-element.54), channel_id=1, source_target_pairs={{0,96},{4,100},{8,104},{12,108},{16,112},{20,116},{24,120},{28,124... | collective-permute-start | bytes 1572872 | tf_op jit(solution)/shard_map/ppermute | solution.py:453
  248.4 25.6 %collective-permute-start.15 = (bf16[128,2048]{1,0:T(8,128)(2,1)}, bf16[128,2048]{1,0:T(8,128)(2,1)S(1)}, u32[]{:S(2)}, u32[]{:S(2)}) collective-permute-start(bf16[128,2048]{1,0:T(8,128)(2,1)} %get-tuple-element.55), channel_id=1, source_target_pairs={{0,32},{4,36},{8,40},{12,44},{16,48},{20,52},{24,56},{28,60},{32,6... | collective-permute-start | bytes 1572872 | tf_op jit(solution)/shard_map/ppermute | solution.py:453
  248.4 25.6 %collective-permute-start.16 = (bf16[128,2048]{1,0:T(8,128)(2,1)}, bf16[128,2048]{1,0:T(8,128)(2,1)S(1)}, u32[]{:S(2)}, u32[]{:S(2)}) collective-permute-start(bf16[128,2048]{1,0:T(8,128)(2,1)} %get-tuple-element.56), channel_id=1, source_target_pairs={{0,64},{4,68},{8,72},{12,76},{16,80},{20,84},{24,88},{28,92},{32,9... | collective-permute-start | bytes 1572872 | tf_op jit(solution)/shard_map/ppermute | solution.py:453
  256.0 18.0 %collective-permute-start.11 = (bf16[128,2048]{1,0:T(8,128)(2,1)}, bf16[128,2048]{1,0:T(8,128)(2,1)S(1)}, u32[]{:S(2)}, u32[]{:S(2)}) collective-permute-start(bf16[128,2048]{1,0:T(8,128)(2,1)} %get-tuple-element.47), channel_id=1, source_target_pairs={{0,12},{4,0},{8,4},{12,8},{16,28},{20,16},{24,20},{28,24},{32,44},... | collective-permute-start | bytes 1572872 | tf_op jit(solution)/shard_map/ppermute | solution.py:451
  260.5 15.1 %collective-permute-start.12 = (bf16[128,2048]{1,0:T(8,128)(2,1)}, bf16[128,2048]{1,0:T(8,128)(2,1)S(1)}, u32[]{:S(2)}, u32[]{:S(2)}) collective-permute-start(bf16[128,2048]{1,0:T(8,128)(2,1)} %get-tuple-element.48), channel_id=1, source_target_pairs={{0,4},{4,8},{8,12},{12,0},{16,20},{20,24},{24,28},{28,16},{32,36},... | collective-permute-start | bytes 1572872 | tf_op jit(solution)/shard_map/ppermute | solution.py:451
  270.7 14.3 %copy-start.3 = (bf16[128,2048]{1,0:T(8,128)(2,1)}, bf16[128,2048]{1,0:T(8,128)(2,1)S(1)}, u32[]{:S(2)}) copy-start(bf16[128,2048]{1,0:T(8,128)(2,1)S(1)} %collective-permute-done.14.refs_5_) | copy-start | bytes 1572868
  270.7 14.3 %collective-permute-start.13 = (bf16[128,2048]{1,0:T(8,128)(2,1)}, bf16[128,2048]{1,0:T(8,128)(2,1)S(1)}, u32[]{:S(2)}, u32[]{:S(2)}) collective-permute-start(bf16[128,2048]{1,0:T(8,128)(2,1)} %get-tuple-element.49), channel_id=1, source_target_pairs={{0,8},{4,12},{8,0},{12,4},{16,24},{20,28},{24,16},{28,20},{32,40},... | collective-permute-start | bytes 1572872 | tf_op jit(solution)/shard_map/ppermute | solution.py:451
  (12 other events, 97.7 us)

commit v3 on v2

--- a/solution.py
+++ b/solution.py
@@ -50,7 +50,7 @@
     )(cov_slab)
 
 
-def predict_kernel(place_ref, slots_ref, split_ref, out_ref, dense, *, tile, crossing, block):
+def predict_kernel(place_ref, slots_ref, split_ref, out_ref, dense, *, tile, crossing, block, skip):
     step = pl.program_id(0)
     rows, columns = split_ref.shape
     columns = columns // 2
@@ -72,10 +72,10 @@
     def scatter(group, c):
         row = pl.multiple_of(group * 8, 8)
         first = (step * tile + row) * crossing
-        blocks = slots_ref[pl.ds(row, 8), crossing * block :].astype(jnp.int32) & 1
+        blocks = slots_ref[pl.ds(row, 8), skip + crossing * block :].astype(jnp.int32) & 1
         for n in range(crossing):
             if n % 2 == 0:
-                plain = slots_ref[pl.ds(row, 8), pl.ds(n * block, 2 * block)]
+                plain = slots_ref[pl.ds(row, 8), pl.ds(skip + n * block, 2 * block)]
                 turned = pltpu.roll(plain, block, 1)
                 both = jnp.where(upper == 0, plain, turned)
             else:
@@ -108,18 +108,18 @@
     lax.fori_loop(0, quads // together, multiply, 0)
 
 
-def predict(slots, slab_split, first_block, local_blocks, crossing, block):
+def predict(slots, skip, slab_split, first_block, local_blocks, crossing, block):
     count, width = slots.shape
     rows, columns = slab_split.shape
     columns = columns // 2
     tile = 256
-    lanes = crossing * block
+    lanes = skip + crossing * block
     blocks = slots[:, lanes : lanes + crossing].astype(jnp.int32)
     local = blocks - first_block
     inside = (local >= 0) & (local < local_blocks) & (blocks >= 0)
     place = jnp.where(inside, local // 2, local_blocks // 2).reshape(-1)
     return pl.pallas_call(
-        functools.partial(predict_kernel, tile=tile, crossing=crossing, block=block),
+        functools.partial(predict_kernel, tile=tile, crossing=crossing, block=block, skip=skip),
         grid_spec=pltpu.PrefetchScalarGridSpec(
             num_scalar_prefetch=1,
             grid=(count // tile,),
@@ -203,17 +203,30 @@
 
 def inverse_kernel(core_ref, own_ref, other_ref, m_ref, left, right, pivot, *, size):
     n = m_ref.shape[0]
-    regions, share, _ = own_ref.shape
+    regions, share, lanes = own_ref.shape
     core = core_ref[0]
+    blocks = n // size
+    per_block = regions // blocks
 
     def place(i, c):
         mine = pl.multiple_of((2 * i + core) * share, share)
         theirs = pl.multiple_of((2 * i + 1 - core) * share, share)
-        m_ref[pl.ds(mine, share), :] = own_ref[i]
-        m_ref[pl.ds(theirs, share), :] = other_ref[i]
+        for j in range(lanes // size):
+            at = pl.ds(pl.multiple_of(lax.rem(lax.div(i, per_block) + j, blocks) * size, size), size)
+            m_ref[pl.ds(mine, share), at] = own_ref[i, :, j * size : (j + 1) * size]
+            m_ref[pl.ds(theirs, share), at] = other_ref[i, :, j * size : (j + 1) * size]
         return c
 
     lax.fori_loop(0, regions, place, 0)
+
+    def mirror(i, c):
+        at = pl.ds(pl.multiple_of(i * size, size), size)
+        for j in range(1, blocks - lanes // size + 1):
+            to = pl.ds(pl.multiple_of(lax.rem(i + j, blocks) * size, size), size)
+            m_ref[to, at] = m_ref[at, to].T
+        return c
+
+    lax.fori_loop(0, blocks, mirror, 0)
 
     def sweep(k, c):
         at = pl.ds(pl.multiple_of(k * size, size), size)
@@ -243,12 +256,15 @@
     lax.fori_loop(0, n // size, sweep, 0)
 
 
-def minus_inverse(core, own, other):
-    n = own.shape[2]
+def minus_inverse(core, own, other, lanes):
+    regions, share, _ = own.shape
+    n = 2 * regions * share
     size = 128
     return pl.pallas_call(
         functools.partial(inverse_kernel, size=size),
-        in_specs=[pl.BlockSpec(memory_space=pltpu.SMEM)] + [pl.BlockSpec(memory_space=pltpu.VMEM)] * 2,
+        grid=(1,),
+        in_specs=[pl.BlockSpec(memory_space=pltpu.SMEM)]
+        + [pl.BlockSpec((regions, share, lanes), lambda i: (0, 0, 0))] * 2,
         out_specs=pl.BlockSpec(memory_space=pltpu.VMEM),
         out_shape=jax.ShapeDtypeStruct((n, n), F32),
         scratch_shapes=[
@@ -340,26 +356,29 @@
     )(*solved, cross)
 
 
-def downdate_kernel(chunk_ref, *refs):
+def downdate_kernel(chunk_ref, *refs, pieces):
     product_refs, cov_ref, out_ref = refs[:-2], refs[-2], refs[-1]
+    tile = cov_ref.shape[0]
     for i, ref in enumerate(product_refs):
-
-        @pl.when(pl.program_id(0) == i)
-        def _():
-            out_ref[...] = cov_ref[...] - ref[...].astype(F32).T
+        for k in range(pieces):
+
+            @pl.when(pl.program_id(0) == i * pieces + k)
+            def _():
+                out_ref[...] = cov_ref[...] - ref[:, k * tile : (k + 1) * tile].T.astype(F32)
 
 
 def downdate(chunks, parts, cov_slab):
     rows, columns = cov_slab.shape
-    tile = rows // len(parts)
-    return pl.pallas_call(
-        downdate_kernel,
+    pieces = 1
+    tile = rows // (len(parts) * pieces)
+    spec = pl.BlockSpec((tile, columns), lambda i, chunk: (chunk[i // pieces] * pieces + i % pieces, 0))
+    return pl.pallas_call(
+        functools.partial(downdate_kernel, pieces=pieces),
         grid_spec=pltpu.PrefetchScalarGridSpec(
             num_scalar_prefetch=1,
-            grid=(len(parts),),
-            in_specs=[pl.BlockSpec(memory_space=pltpu.VMEM)] * len(parts)
-            + [pl.BlockSpec((tile, columns), lambda i, chunk: (chunk[i], 0))],
-            out_specs=pl.BlockSpec((tile, columns), lambda i, chunk: (chunk[i], 0)),
+            grid=(len(parts) * pieces,),
+            in_specs=[pl.BlockSpec(memory_space=pltpu.VMEM)] * len(parts) + [spec],
+            out_specs=spec,
         ),
         out_shape=jax.ShapeDtypeStruct((rows, columns), F32),
         compiler_params=pltpu.CompilerParams(vmem_limit_bytes=VMEM_LIMIT),
@@ -415,31 +434,31 @@
     live = start + jnp.arange(share, dtype=jnp.int32) < region_rows[0]
     weights = jnp.where(live[:, None], my_coeff, 0.0)
     blocks, weights = merged(my_blocks, weights)
-    message = jnp.concatenate([weights, jnp.pad(blocks.astype(F32), ((0, 0), (0, 128 - crossing)))], axis=1)
+    my_innov = lax.dynamic_slice_in_dim(innov_cov, start, share, 0)
+    skip = 640
+    my_innov = lax.dynamic_slice_in_dim(jnp.concatenate([my_innov, my_innov], axis=1), device // 4 * 128, skip, 1)
+    message = jnp.concatenate([my_innov, weights, jnp.pad(blocks.astype(F32), ((0, 0), (0, 128 - crossing)))], axis=1)
     own = to_all(message)
 
     slab_split = split_slab(cov_slab)
     send = spread(cross_cov.T)
-    my_innov = lax.dynamic_slice_in_dim(innov_cov, start, share, 0)
-    own, send, slab_split, my_innov = lax.optimization_barrier((own, send, slab_split, my_innov))
-    innov_own = to_all(my_innov)
+    own, send, slab_split = lax.optimization_barrier((own, send, slab_split))
+    cross = lax.all_to_all(send, "obs", 0, 0)
     other = lax.ppermute(own, "vox", SWAP)
     first_block = lax.axis_index("vox") * local_blocks
     flat = (everyone * share, -1)
-    partial_own = predict(own.reshape(flat), slab_split, first_block, local_blocks, crossing, block_size)
-    innov_own, send, other, partial_own = lax.optimization_barrier((innov_own, send, other, partial_own))
-    cross = lax.all_to_all(send, "obs", 0, 0)
-    innov_other = lax.ppermute(innov_own, "vox", SWAP)
-    partial_other = predict(other.reshape(flat), slab_split, first_block, local_blocks, crossing, block_size)
+    partial_own = predict(own.reshape(flat), skip, slab_split, first_block, local_blocks, crossing, block_size)
+    other, partial_own = lax.optimization_barrier((other, partial_own))
+    partial_other = predict(other.reshape(flat), skip, slab_split, first_block, local_blocks, crossing, block_size)
 
     mine = partial_own + lax.ppermute(partial_other, "vox", SWAP)
     theirs = partial_other + lax.ppermute(partial_own, "vox", SWAP)
     low = jnp.where(core == 0, mine, theirs).reshape(everyone, 1, share, columns)
     high = jnp.where(core == 0, theirs, mine).reshape(everyone, 1, share, columns)
     chip_sum = jnp.concatenate([low, high], axis=1)
-    chip_sum, innov_own, innov_other = lax.optimization_barrier((chip_sum, innov_own, innov_other))
+    chip_sum, other = lax.optimization_barrier((chip_sum, other))
     predicted = chip_sum + lax.ppermute(chip_sum, "vox", [(0, 2), (2, 0), (1, 3), (3, 1)])
-    minus = minus_inverse(core_array, innov_own, innov_other)
+    minus = minus_inverse(core_array, own, other, skip)
     solved = solve_turned(minus, predicted)
 
     at_x = device % 4

time: 301 us -> 286 us (0.950)
  starting transfers between devices: 66.2 us -> 40.9 us
  waiting for transfers between devices: 42.1 us -> 49.3 us
  Pallas kernels: 175 us -> 180 us
    all_to_all x2 -> x1, waiting for transfers between devices: 2.85 us -> 19.2 us  [to_all(): lax.all_to_all(jnp.broadcast_to(piece[None], (everyone,) + piece.shape),...]
    ppermute x3, waiting for transfers between devices: 12.6 us -> 3.65 us  [shards(): from_y = [lax.ppermute(solved, 'obs', steps_along(0, d)) for d in (1, 3, 2)]]
    ppermute x3, starting transfers between devices: 14.9 us -> 6.23 us  [shards(): from_y = [lax.ppermute(solved, 'obs', steps_along(0, d)) for d in (1, 3, 2)]]
    all_to_all x2 -> x1, starting transfers between devices: 18.2 us -> 10.1 us  [to_all(): lax.all_to_all(jnp.broadcast_to(piece[None], (everyone,) + piece.shape),...]
    ppermute x3, starting transfers between devices: 9.21 us -> 4.1 us  [shards(): from_x = [lax.ppermute(solved, 'obs', steps_along(2, d)) for d in (1, 3, 2)]]
  transfers between devices with their start and end apart: 20 -> 18, of which waited for: 10 -> 11; matrix products, arithmetic and copies ran while one was open for 2% -> 2% of each run, Pallas kernels for 53% -> 57%
where the time goes in v3:
time: 286 us; the launch traced here: 284 us
  Pallas kernels  180 us (63%)
  waiting for transfers between devices  49.3 us (17%)
  starting transfers between devices  40.9 us (14%)
  other arithmetic  6.61 us (2%)
  local copies, waits for them, and re-layouts  6.29 us (2%)
    pallas_call x2, Pallas kernels, predict(): pl.pallas_call(functools.partial(predict_kernel, tile=tile, crossing=cros...  65.6 us
    pallas_call x1, Pallas kernels, minus_inverse(): pl.pallas_call(functools.partial(inverse_kernel, size=size), grid=(1,), i...  57.5 us
    all_to_all x1, waiting for transfers between devices, to_all(): lax.all_to_all(jnp.broadcast_to(piece[None], (everyone,) + piece.shape),...  19.2 us
    pallas_call x1, Pallas kernels, spread(): pl.pallas_call(spread_kernel, grid=(everyone,), in_specs=[pl.BlockSpec((s...  18.8 us
    pallas_call x2, Pallas kernels, products(): pl.pallas_call(functools.partial(product_kernel, members=members), grid=(...  12.2 us
    pallas_call x1, Pallas kernels, downdate(): pl.pallas_call(functools.partial(downdate_kernel, pieces=pieces), grid_sp...  12.1 us
    ppermute x3, waiting for transfers between devices, shards(): lax.ppermute(part, 'obs', steps_along(0, -d))  11.5 us
    all_to_all x1, starting transfers between devices, to_all(): lax.all_to_all(jnp.broadcast_to(piece[None], (everyone,) + piece.shape),...  10.1 us
  transfers between devices with their start and end apart: 18, of which 11 were waited for; matrix products, arithmetic and copies ran while one was open for 2% of the time, Pallas kernels for 57%

profile of v3, /device:TPU:66, one launch (start us, length us, event | category | flops | bytes accessed | tf_op | source)
XLA Modules:
  0.0 283.7 jit_solution(4019413145072863311)
XLA Ops:
  4.0 2.2 broadcast_in_dim.62
  6.2 10.1 %all-to-all-start = ((f32[32,16,1792]{2,1,0:T(8,128)}), f32[32,16,1792]{2,1,0:T(8,128)}, u32[]{:S(2)}, u32[]{:S(2)}) async-start(f32[32,16,1792]{2,1,0:T(8,128)} %broadcast_in_dim.62), calls=%async_computation | async-start | bytes 7340032 | tf_op jit(solution)/shard_map/all_to_all | solution.py:417
  16.3 18.8 %spread.1 = bf16[32,2,32,2048]{3,2,1,0:T(8,128)(2,1)} custom-call(bf16[32,16384]{1,0:T(8,128)(2,1)} %bitcast.16, bf16[32,16384]{1,0:T(8,128)(2,1)} %bitcast.17), custom_call_target="tpu_custom_call" | custom-call | bytes 8388608 | tf_op jit(solution)/shard_map/spread/pallas_call | solution.py:308
  35.1 9.3 %split.1.split_ref = bf16[16384,256]{1,0:T(8,128)(2,1)} custom-call(f32[16384,128]{1,0:T(8,128)} %refs_8_.1), custom_call_target="tpu_custom_call" | custom-call | flops 8388608 | bytes 16777216 | tf_op jit(solution)/shard_map/split/pallas_call | solution.py:41
  44.4 19.2 %all-to-all-done.own_ref = f32[32,16,1792]{2,1,0:T(8,128)} async-done(((f32[32,16,1792]{2,1,0:T(8,128)}), f32[32,16,1792]{2,1,0:T(8,128)}, u32[]{:S(2)}, u32[]{:S(2)}) %all-to-all-start) | async-done | bytes 3670048 | tf_op jit(solution)/shard_map/all_to_all | solution.py:417
  65.5 8.8 %all-to-all-start.1 = ((bf16[32,2,32,2048]{3,2,1,0:T(8,128)(2,1)}), bf16[32,2,32,2048]{3,2,1,0:T(8,128)(2,1)}, u32[]{:S(2)}, u32[]{:S(2)}) async-start(bf16[32,2,32,2048]{3,2,1,0:T(8,128)(2,1)} %spread.1), calls=%async_computation.1 | async-start | bytes 16777216 | tf_op jit(solution)/shard_map/all_to_all | solution.py:446
  74.3 32.7 %predict.2 = f32[512,128]{1,0:T(8,128)} custom-call(s32[8192]{0:T(1024)} %reshape.52.place_ref, f32[512,1792]{1,0:T(8,128)} %bitcast.11.slots_ref, bf16[16384,256]{1,0:T(8,128)(2,1)} %split.1.split_ref), custom_call_target="tpu_custom_call" | custom-call | flops 12884901888 | bytes 8388608 | tf_op jit(solution)/shard_map/predict/pallas_call | solution.py:121
  108.9 32.9 %predict.3 = f32[512,128]{1,0:T(8,128)} custom-call(s32[8192]{0:T(1024)} %reshape.54.place_ref, f32[512,1792]{1,0:T(8,128)} %bitcast.12.slots_ref, bf16[16384,256]{1,0:T(8,128)(2,1)} %split.1.split_ref), custom_call_target="tpu_custom_call" | custom-call | flops 12884901888 | bytes 8388608 | tf_op jit(solution)/shard_map/predict/pallas_call | solution.py:121
  146.7 57.5 %minus_inverse.1.minus_ref = f32[1024,1024]{1,0:T(8,128)} custom-call(s32[1]{0:T(128)} %bitcast.8.core_ref, f32[32,16,1792]{2,1,0:T(8,128)} %all-to-all-done.own_ref, f32[32,16,1792]{2,1,0:T(8,128)} %collective-permute-done.other_ref), custom_call_target="tpu_custom_call" | custom-call | flops 64424509440 | bytes 8388608 | tf_op jit(solution)/shard_map/minus_inverse/pallas_call | solution.py:263
  205.1 4.2 %solve.1.refs_0_ = bf16[128,1024]{1,0:T(8,128)(2,1)} custom-call(f32[1024,1024]{1,0:T(8,128)} %minus_inverse.1.minus_ref, f32[32,2,16,128]{3,2,1,0:T(8,128)} %add.120.predicted_ref), custom_call_target="tpu_custom_call" | custom-call | flops 805306368 | bytes 4194304 | tf_op jit(solution)/shard_map/solve/pallas_call | solution.py:288
  211.3 2.1 collective-permute-start.6
  214.9 1.8 collective-permute-start.8
  216.7 2.1 collective-permute-done.4.refs_1_
  218.7 3.0 %collective-permute-start.9 = (bf16[128,1024]{1,0:T(8,128)(2,1)}, bf16[128,1024]{1,0:T(8,128)(2,1)S(1)}, u32[]{:S(2)}, u32[]{:S(2)}) collective-permute-start(bf16[128,1024]{1,0:T(8,128)(2,1)} %solve.1.refs_0_), channel_id=1, source_target_pairs={{0,64},{4,68},{8,72},{12,76},{16,80},{20,84},{24,88},{28,92},{32,9... | collective-permute-start | bytes 786440 | tf_op jit(solution)/shard_map/ppermute | solution.py:467
  221.7 3.3 %collective-permute-done.6.refs_3_ = bf16[128,1024]{1,0:T(8,128)(2,1)S(1)} collective-permute-done((bf16[128,1024]{1,0:T(8,128)(2,1)}, bf16[128,1024]{1,0:T(8,128)(2,1)S(1)}, u32[]{:S(2)}, u32[]{:S(2)}) %collective-permute-start.6) | collective-permute-done | bytes 262176 | tf_op jit(solution)/shard_map/ppermute | solution.py:466
  225.0 2.1 collective-permute-done.8.refs_2_
  228.7 6.1 %products.2 = (f32[128,2048]{1,0:T(8,128)}, bf16[128,2048]{1,0:T(8,128)(2,1)}, bf16[128,2048]{1,0:T(8,128)(2,1)}, bf16[128,2048]{1,0:T(8,128)(2,1)}) custom-call(bf16[128,1024]{1,0:T(8,128)(2,1)} %solve.1.refs_0_, bf16[128,1024]{1,0:T(8,128)(2,1)} %copy-done.11, bf16[128,1024]{1,0:T(8,128)(2,1)} %copy-done.12, bf16[128,1024]{1,0:T(8,128)(2,1)} %copy-done.13, ...), custom_call_target="tpu_custom_call" | custom-call | flops 2147483648 | bytes 4194304 | tf_op jit(solution)/shard_map/products/pallas_call | solution.py:343
  236.9 2.7 collective-permute-start.12
  239.6 6.1 %products.3 = (f32[128,2048]{1,0:T(8,128)}, bf16[128,2048]{1,0:T(8,128)(2,1)}, bf16[128,2048]{1,0:T(8,128)(2,1)}, bf16[128,2048]{1,0:T(8,128)(2,1)}) custom-call(bf16[128,1024]{1,0:T(8,128)(2,1)} %solve.1.refs_0_, bf16[128,1024]{1,0:T(8,128)(2,1)} %copy-done.8, bf16[128,1024]{1,0:T(8,128)(2,1)} %copy-done.9, bf16[128,1024]{1,0:T(8,128)(2,1)} %copy-done.10, ...), custom_call_target="tpu_custom_call" | custom-call | flops 2147483648 | bytes 4194304 | tf_op jit(solution)/shard_map/products/pallas_call | solution.py:343
  245.7 2.1 collective-permute-start.13
  249.1 2.6 collective-permute-start.15
  252.4 6.7 %collective-permute-done.12.refs_3_ = bf16[128,2048]{1,0:T(8,128)(2,1)S(1)} collective-permute-done((bf16[128,2048]{1,0:T(8,128)(2,1)}, bf16[128,2048]{1,0:T(8,128)(2,1)S(1)}, u32[]{:S(2)}, u32[]{:S(2)}) %collective-permute-start.12) | collective-permute-done | bytes 524320 | tf_op jit(solution)/shard_map/ppermute | solution.py:470
  260.8 9.8 %collective-permute-done.14.refs_6_ = bf16[128,2048]{1,0:T(8,128)(2,1)S(1)} collective-permute-done((bf16[128,2048]{1,0:T(8,128)(2,1)}, bf16[128,2048]{1,0:T(8,128)(2,1)S(1)}, u32[]{:S(2)}, u32[]{:S(2)}) %collective-permute-start.14) | collective-permute-done | bytes 524320 | tf_op jit(solution)/shard_map/ppermute | solution.py:472
  271.5 12.1 %downdate.1 = f32[16384,128]{1,0:T(8,128)} custom-call(s32[8]{0:T(128)} %stack.35.chunk_ref, f32[128,2048]{1,0:T(8,128)} %get-tuple-element.38.refs_0_, bf16[128,2048]{1,0:T(8,128)(2,1)} %copy-done.2, bf16[128,2048]{1,0:T(8,128)(2,1)} %copy-done.3, bf16[128,2048]{1,0:T(8,128)(2,1)} %copy-done.4, f32[128,2048]{1,0:T(8,128)} %get-tuple-element.45.refs_4_, ...), custom_call_target="tpu_custom_call" | custom-call | flops 2097152 | bytes 20971520 | tf_op jit(solution)/shard_map/downdate/pallas_call | solution.py:375
  (72 shorter events, 24.7 us)
Async XLA Ops:
  6.2 57.4 %all-to-all-start = ((f32[32,16,1792]{2,1,0:T(8,128)}), f32[32,16,1792]{2,1,0:T(8,128)}, u32[]{:S(2)}, u32[]{:S(2)}) async-start(f32[32,16,1792]{2,1,0:T(8,128)} %broadcast_in_dim.62), calls=%async_computation | async-start | bytes 7340032 | tf_op jit(solution)/shard_map/all_to_all | solution.py:417
  63.6 43.4 %collective-permute-start = (f32[32,16,1792]{2,1,0:T(8,128)}, f32[32,16,1792]{2,1,0:T(8,128)}, u32[]{:S(2)}, u32[]{:S(2)}) collective-permute-start(f32[32,16,1792]{2,1,0:T(8,128)} %all-to-all-done.own_ref), channel_id=1, source_target_pairs={{0,1},{1,0},{2,3},{3,2},{4,5},{5,4},{6,7},{7,6},{8,9},{9,8},{10,11... | collective-permute-start | bytes 11010056 | tf_op jit(solution)/shard_map/ppermute | solution.py:447
  65.5 163.1 %all-to-all-start.1 = ((bf16[32,2,32,2048]{3,2,1,0:T(8,128)(2,1)}), bf16[32,2,32,2048]{3,2,1,0:T(8,128)(2,1)}, u32[]{:S(2)}, u32[]{:S(2)}) async-start(bf16[32,2,32,2048]{3,2,1,0:T(8,128)(2,1)} %spread.1), calls=%async_computation.1 | async-start | bytes 16777216 | tf_op jit(solution)/shard_map/all_to_all | solution.py:446
  108.9 32.9 %copy-start.14 = (f32[512,128]{1,0:T(8,128)S(1)}, f32[512,128]{1,0:T(8,128)}, u32[]{:S(2)}) copy-start(f32[512,128]{1,0:T(8,128)} %predict.2) | copy-start | bytes 786436
  141.8 1.5 collective-permute-start.2
  141.8 2.1 collective-permute-start.1
  145.0 59.2 %collective-permute-start.3 = (f32[32,2,16,128]{3,2,1,0:T(8,128)S(1)}, f32[32,2,16,128]{3,2,1,0:T(8,128)S(1)}, u32[]{:S(2)}, u32[]{:S(2)}) collective-permute-start(f32[32,2,16,128]{3,2,1,0:T(8,128)S(1)} %pad_maximum_fusion), channel_id=1, source_target_pairs={{0,2},{2,0},{1,3},{3,1},{4,6},{6,4},{5,7},{7,5},{8,10},{10,8},{9,1... | collective-permute-start | bytes 1572872 | tf_op jit(solution)/shard_map/ppermute | solution.py:460
  209.3 9.4 %collective-permute-start.4 = (bf16[128,1024]{1,0:T(8,128)(2,1)}, bf16[128,1024]{1,0:T(8,128)(2,1)S(1)}, u32[]{:S(2)}, u32[]{:S(2)}) collective-permute-start(bf16[128,1024]{1,0:T(8,128)(2,1)} %solve.1.refs_0_), channel_id=1, source_target_pairs={{0,4},{4,8},{8,12},{12,0},{16,20},{20,24},{24,28},{28,16},{32,36},... | collective-permute-start | bytes 786440 | tf_op jit(solution)/shard_map/ppermute | solution.py:466
  210.8 10.9 %collective-permute-start.5 = (bf16[128,1024]{1,0:T(8,128)(2,1)}, bf16[128,1024]{1,0:T(8,128)(2,1)S(1)}, u32[]{:S(2)}, u32[]{:S(2)}) collective-permute-start(bf16[128,1024]{1,0:T(8,128)(2,1)} %solve.1.refs_0_), channel_id=1, source_target_pairs={{0,12},{4,0},{8,4},{12,8},{16,28},{20,16},{24,20},{28,24},{32,44},... | collective-permute-start | bytes 786440 | tf_op jit(solution)/shard_map/ppermute | solution.py:466
  211.3 13.7 %collective-permute-start.6 = (bf16[128,1024]{1,0:T(8,128)(2,1)}, bf16[128,1024]{1,0:T(8,128)(2,1)S(1)}, u32[]{:S(2)}, u32[]{:S(2)}) collective-permute-start(bf16[128,1024]{1,0:T(8,128)(2,1)} %solve.1.refs_0_), channel_id=1, source_target_pairs={{0,8},{4,12},{8,0},{12,4},{16,24},{20,28},{24,16},{28,20},{32,40},... | collective-permute-start | bytes 786440 | tf_op jit(solution)/shard_map/ppermute | solution.py:466
  213.4 11.6 %collective-permute-start.7 = (bf16[128,1024]{1,0:T(8,128)(2,1)}, bf16[128,1024]{1,0:T(8,128)(2,1)S(1)}, u32[]{:S(2)}, u32[]{:S(2)}) collective-permute-start(bf16[128,1024]{1,0:T(8,128)(2,1)} %solve.1.refs_0_), channel_id=1, source_target_pairs={{0,32},{4,36},{8,40},{12,44},{16,48},{20,52},{24,56},{28,60},{32,6... | collective-permute-start | bytes 786440 | tf_op jit(solution)/shard_map/ppermute | solution.py:467
  214.9 12.2 %collective-permute-start.8 = (bf16[128,1024]{1,0:T(8,128)(2,1)}, bf16[128,1024]{1,0:T(8,128)(2,1)S(1)}, u32[]{:S(2)}, u32[]{:S(2)}) collective-permute-start(bf16[128,1024]{1,0:T(8,128)(2,1)} %solve.1.refs_0_), channel_id=1, source_target_pairs={{0,96},{4,100},{8,104},{12,108},{16,112},{20,116},{24,120},{28,124... | collective-permute-start | bytes 786440 | tf_op jit(solution)/shard_map/ppermute | solution.py:467
  218.7 10.0 %copy-start.11 = (bf16[128,1024]{1,0:T(8,128)(2,1)}, bf16[128,1024]{1,0:T(8,128)(2,1)S(1)}, u32[]{:S(2)}) copy-start(bf16[128,1024]{1,0:T(8,128)(2,1)S(1)} %collective-permute-done.4.refs_1_) | copy-start | bytes 786436
  218.7 9.9 %collective-permute-start.9 = (bf16[128,1024]{1,0:T(8,128)(2,1)}, bf16[128,1024]{1,0:T(8,128)(2,1)S(1)}, u32[]{:S(2)}, u32[]{:S(2)}) collective-permute-start(bf16[128,1024]{1,0:T(8,128)(2,1)} %solve.1.refs_0_), channel_id=1, source_target_pairs={{0,64},{4,68},{8,72},{12,76},{16,80},{20,84},{24,88},{28,92},{32,9... | collective-permute-start | bytes 786440 | tf_op jit(solution)/shard_map/ppermute | solution.py:467
  234.8 14.2 %collective-permute-start.10 = (bf16[128,2048]{1,0:T(8,128)(2,1)}, bf16[128,2048]{1,0:T(8,128)(2,1)S(1)}, u32[]{:S(2)}, u32[]{:S(2)}) collective-permute-start(bf16[128,2048]{1,0:T(8,128)(2,1)} %get-tuple-element.39), channel_id=1, source_target_pairs={{0,12},{4,0},{8,4},{12,8},{16,28},{20,16},{24,20},{28,24},{32,44},... | collective-permute-start | bytes 1572872 | tf_op jit(solution)/shard_map/ppermute | solution.py:470
  236.4 16.0 %collective-permute-start.11 = (bf16[128,2048]{1,0:T(8,128)(2,1)}, bf16[128,2048]{1,0:T(8,128)(2,1)S(1)}, u32[]{:S(2)}, u32[]{:S(2)}) collective-permute-start(bf16[128,2048]{1,0:T(8,128)(2,1)} %get-tuple-element.40), channel_id=1, source_target_pairs={{0,4},{4,8},{8,12},{12,0},{16,20},{20,24},{24,28},{28,16},{32,36},... | collective-permute-start | bytes 1572872 | tf_op jit(solution)/shard_map/ppermute | solution.py:470
  236.9 22.2 %collective-permute-start.12 = (bf16[128,2048]{1,0:T(8,128)(2,1)}, bf16[128,2048]{1,0:T(8,128)(2,1)S(1)}, u32[]{:S(2)}, u32[]{:S(2)}) collective-permute-start(bf16[128,2048]{1,0:T(8,128)(2,1)} %get-tuple-element.41), channel_id=1, source_target_pairs={{0,8},{4,12},{8,0},{12,4},{16,24},{20,28},{24,16},{28,20},{32,40},... | collective-permute-start | bytes 1572872 | tf_op jit(solution)/shard_map/ppermute | solution.py:470
  245.7 15.1 %collective-permute-start.13 = (bf16[128,2048]{1,0:T(8,128)(2,1)}, bf16[128,2048]{1,0:T(8,128)(2,1)S(1)}, u32[]{:S(2)}, u32[]{:S(2)}) collective-permute-start(bf16[128,2048]{1,0:T(8,128)(2,1)} %get-tuple-element.46), channel_id=1, source_target_pairs={{0,96},{4,100},{8,104},{12,108},{16,112},{20,116},{24,120},{28,124... | collective-permute-start | bytes 1572872 | tf_op jit(solution)/shard_map/ppermute | solution.py:472
  247.8 22.8 %collective-permute-start.14 = (bf16[128,2048]{1,0:T(8,128)(2,1)}, bf16[128,2048]{1,0:T(8,128)(2,1)S(1)}, u32[]{:S(2)}, u32[]{:S(2)}) collective-permute-start(bf16[128,2048]{1,0:T(8,128)(2,1)} %get-tuple-element.47), channel_id=1, source_target_pairs={{0,32},{4,36},{8,40},{12,44},{16,48},{20,52},{24,56},{28,60},{32,6... | collective-permute-start | bytes 1572872 | tf_op jit(solution)/shard_map/ppermute | solution.py:472
  249.1 21.5 %copy-start.2 = (bf16[128,2048]{1,0:T(8,128)(2,1)}, bf16[128,2048]{1,0:T(8,128)(2,1)S(1)}, u32[]{:S(2)}) copy-start(bf16[128,2048]{1,0:T(8,128)(2,1)S(1)} %collective-permute-done.10.refs_1_) | copy-start | bytes 1572868
  249.1 21.5 %collective-permute-start.15 = (bf16[128,2048]{1,0:T(8,128)(2,1)}, bf16[128,2048]{1,0:T(8,128)(2,1)S(1)}, u32[]{:S(2)}, u32[]{:S(2)}) collective-permute-start(bf16[128,2048]{1,0:T(8,128)(2,1)} %get-tuple-element.48), channel_id=1, source_target_pairs={{0,64},{4,68},{8,72},{12,76},{16,80},{20,84},{24,88},{28,92},{32,9... | collective-permute-start | bytes 1572872 | tf_op jit(solution)/shard_map/ppermute | solution.py:472
  252.4 18.2 %copy-start.3 = (bf16[128,2048]{1,0:T(8,128)(2,1)}, bf16[128,2048]{1,0:T(8,128)(2,1)S(1)}, u32[]{:S(2)}) copy-start(bf16[128,2048]{1,0:T(8,128)(2,1)S(1)} %collective-permute-done.11.refs_2_) | copy-start | bytes 1572868
  259.1 11.5 %copy-start.4 = (bf16[128,2048]{1,0:T(8,128)(2,1)}, bf16[128,2048]{1,0:T(8,128)(2,1)S(1)}, u32[]{:S(2)}) copy-start(bf16[128,2048]{1,0:T(8,128)(2,1)S(1)} %collective-permute-done.12.refs_3_) | copy-start | bytes 1572868
  271.5 12.1 %copy-start.1 = (s32[32,16]{0,1:T(8,128)S(1)}, s32[32,16]{0,1:T(8,128)}, u32[]{:S(2)}) copy-start(s32[32,16]{0,1:T(8,128)} %param.8) | copy-start | bytes 6148
  (9 other events, 46.6 us)

commit v4 on v3

--- a/solution.py
+++ b/solution.py
@@ -50,8 +50,9 @@
     )(cov_slab)
 
 
-def predict_kernel(place_ref, slots_ref, split_ref, out_ref, dense, *, tile, crossing, block, skip):
+def predict_kernel(place_ref, slots_ref, far_ref, out_ref, dense, split_ref, arrived, *, tile, crossing, block, skip):
     step = pl.program_id(0)
+    fetch = pltpu.make_async_copy(far_ref, split_ref, arrived)
     rows, columns = split_ref.shape
     columns = columns // 2
     pairs = rows // (2 * block)
@@ -63,6 +64,8 @@
 
     @pl.when(step == 0)
     def _():
+        fetch.start()
+
         def clear(i, c):
             dense[i] = jnp.zeros_like(dense[i])
             return c
@@ -88,7 +91,11 @@
 
     lax.fori_loop(0, tile // 8, scatter, 0)
     out_ref[...] = jnp.zeros_like(out_ref)
-    together = 8
+    together = 16
+
+    @pl.when(step == 0)
+    def _():
+        fetch.wait()
 
     def multiply(i, c):
         wide_sum = jnp.zeros((tile, 2 * columns), F32)
@@ -125,10 +132,14 @@
             grid=(count // tile,),
             in_specs=[
                 pl.BlockSpec((tile, width), lambda i, place: (i, 0)),
-                pl.BlockSpec(memory_space=pltpu.VMEM),
+                pl.BlockSpec(memory_space=pl.ANY),
             ],
             out_specs=pl.BlockSpec((tile, columns), lambda i, place: (i, 0)),
-            scratch_shapes=[pltpu.VMEM((rows // (2 * block) + 1, tile, 2 * block), F32)],
+            scratch_shapes=[
+                pltpu.VMEM((rows // (2 * block) + 1, tile, 2 * block), F32),
+                pltpu.VMEM((rows, 2 * columns), BF16),
+                pltpu.SemaphoreType.DMA,
+            ],
         ),
         out_shape=jax.ShapeDtypeStruct((count, columns), F32),
         compiler_params=pltpu.CompilerParams(vmem_limit_bytes=VMEM_LIMIT),
@@ -139,10 +150,14 @@
     )(place, slots, slab_split)
 
 
+def spread_lane(rows, lane):
+    return jnp.take_along_axis(rows, jnp.full(rows.shape, lane, jnp.int32), axis=1)
+
+
 def sweep_rows(rows, first):
     sub = lax.broadcasted_iota(jnp.int32, rows.shape, 0)
     lane = lax.broadcasted_iota(jnp.int32, rows.shape, 1) - first
-    cols = [jnp.broadcast_to(rows[:, first + j : first + j + 1], rows.shape) for j in range(8)]
+    cols = [spread_lane(rows, first + j) for j in range(8)]
 
     def row(v, p):
         return jnp.broadcast_to(v[p : p + 1, :], rows.shape)
@@ -167,37 +182,42 @@
     return jnp.where((lane >= 0) & (lane < 8), -out, out)
 
 
+def take_away(rows, swept, first):
+    lanes = lax.broadcasted_iota(jnp.int32, rows.shape, 1)
+    count = swept.shape[0]
+    even = jnp.where((lanes >= first) & (lanes < first + count), 0.0, rows)
+    odd = jnp.zeros_like(rows)
+    for j in range(0, count, 2):
+        even = even - spread_lane(rows, first + j) * swept[j : j + 1, :]
+        odd = odd + spread_lane(rows, first + j + 1) * swept[j + 1 : j + 2, :]
+    return even - odd
+
+
 def small_sweep(block):
     size = block.shape[0]
     strip = 16
-    lanes = lax.broadcasted_iota(jnp.int32, (8, size), 1)
     all_lanes = lax.broadcasted_iota(jnp.int32, (size, size), 1)
+    rows = [block[at : at + 8, :] for at in range(0, strip, 8)]
     for base in range(0, size, strip):
-        rows = [block[at : at + 8, :] for at in range(base, base + strip, 8)]
         for g in range(strip // 8):
-            first = base + 8 * g
-            top = sweep_rows(rows[g], first)
-            pivots = (lanes >= first) & (lanes < first + 8)
-            for e in range(strip // 8):
-                if e != g:
-                    rest = jnp.where(pivots, 0.0, rows[e])
-                    for j in range(8):
-                        rest = rest - rows[e][:, first + j : first + j + 1] * top[j : j + 1, :]
-                    rows[e] = rest
-            rows[g] = top
+            top = sweep_rows(rows[g], base + 8 * g)
+            rows = [top if e == g else take_away(rows[e], top, base + 8 * g) for e in range(strip // 8)]
         middle = jnp.concatenate(rows, axis=0)
+        after = base + strip
+        ahead = [take_away(block[at : at + 8, :], middle, base) for at in range(after, min(after + strip, size), 8)]
         above = [jnp.zeros((base, size), F32)] if base else []
-        below = [jnp.zeros((size - base - strip, size), F32)] if base + strip < size else []
+        below = [jnp.zeros((size - after, size), F32)] if after < size else []
         high, low = halves(jnp.concatenate(above + [middle] + below, axis=0))
         block_high, block_low = halves(block)
-        keep = jnp.where((all_lanes >= base) & (all_lanes < base + strip), 0.0, block)
+        keep = jnp.where((all_lanes >= base) & (all_lanes < after), 0.0, block)
         new = keep - (
             dot(jnp.concatenate([block_high, block_low], axis=1), jnp.concatenate([high, high], axis=0))
             + dot(block_high, low)
         )
         above = [new[:base]] if base else []
-        below = [new[base + strip :]] if base + strip < size else []
-        block = jnp.concatenate(above + [middle] + below, axis=0)
+        below = [new[after + strip :]] if after + strip < size else []
+        block = jnp.concatenate(above + [middle] + ahead + below, axis=0)
+        rows = ahead
     return block
 
 
@@ -241,15 +261,8 @@
         right[:size, :] = high
         right[size : 2 * size, :] = high
         right[2 * size :, :] = low
-        wide = n // 2
-
-        def update(i, c):
-            here = pl.ds(pl.multiple_of(i * wide, wide), wide)
-            product = dot(left[...], right[: 2 * size, here]) + dot(left[:, :size], right[2 * size :, here])
-            m_ref[:, here] = m_ref[:, here] - product
-            return c
-
-        lax.fori_loop(0, n // wide, update, 0)
+        product = dot(left[...], right[: 2 * size, :]) + dot(left[:, :size], right[2 * size :, :])
+        m_ref[...] = m_ref[...] - product
         m_ref[at, :] = pivot[...]
         return c
 
@@ -356,35 +369,39 @@
     )(*solved, cross)
 
 
-def downdate_kernel(chunk_ref, *refs, pieces):
-    product_refs, cov_ref, out_ref = refs[:-2], refs[-2], refs[-1]
-    tile = cov_ref.shape[0]
+def downdate_kernel(chunk_ref, *refs, count):
+    product_refs, cov_ref, out_ref = refs[:count], refs[count], refs[-1]
     for i, ref in enumerate(product_refs):
-        for k in range(pieces):
-
-            @pl.when(pl.program_id(0) == i * pieces + k)
-            def _():
-                out_ref[...] = cov_ref[...] - ref[:, k * tile : (k + 1) * tile].T.astype(F32)
-
-
-def downdate(chunks, parts, cov_slab):
+
+        @pl.when(pl.program_id(0) == i)
+        def _():
+            out_ref[...] = cov_ref[...] - ref[...].T.astype(F32)
+
+
+def downdate(chunks, parts, cov_slab, so_far=None):
     rows, columns = cov_slab.shape
-    pieces = 1
-    tile = rows // (len(parts) * pieces)
-    spec = pl.BlockSpec((tile, columns), lambda i, chunk: (chunk[i // pieces] * pieces + i % pieces, 0))
-    return pl.pallas_call(
-        functools.partial(downdate_kernel, pieces=pieces),
+    count = len(parts)
+    tile = parts[0].shape[1]
+    spec = pl.BlockSpec((tile, columns), lambda i, chunk: (chunk[i], 0))
+    more = [] if so_far is None else [so_far]
+    return pl.pallas_call(
+        functools.partial(downdate_kernel, count=count),
         grid_spec=pltpu.PrefetchScalarGridSpec(
             num_scalar_prefetch=1,
-            grid=(len(parts) * pieces,),
-            in_specs=[pl.BlockSpec(memory_space=pltpu.VMEM)] * len(parts) + [spec],
+            grid=(count,),
+            in_specs=[pl.BlockSpec(memory_space=pltpu.VMEM)] * count
+            + [spec]
+            + [pl.BlockSpec(memory_space=pl.ANY)] * len(more),
             out_specs=spec,
         ),
         out_shape=jax.ShapeDtypeStruct((rows, columns), F32),
-        compiler_params=pltpu.CompilerParams(vmem_limit_bytes=VMEM_LIMIT),
-        cost_estimate=pl.CostEstimate(flops=rows * columns, bytes_accessed=10 * rows * columns, transcendentals=0),
+        input_output_aliases={count + 2: 0} if more else {},
+        compiler_params=pltpu.CompilerParams(vmem_limit_bytes=VMEM_LIMIT),
+        cost_estimate=pl.CostEstimate(
+            flops=count * tile * columns, bytes_accessed=10 * count * tile * columns, transcendentals=0
+        ),
         name="downdate",
-    )(chunks, *parts, cov_slab)
+    )(jnp.stack(chunks).astype(jnp.int32), *parts, cov_slab, *more)
 
 
 def merged(ray_blocks, weights):
@@ -470,9 +487,9 @@
     back_x = [lax.ppermute(part, "obs", steps_along(2, -d)) for part, d in zip(parts_x[1:], (1, 3, 2))]
     parts_y = products([solved] + from_y, cross, 1)
     back_y = [lax.ppermute(part, "obs", steps_along(0, -d)) for part, d in zip(parts_y[1:], (1, 3, 2))]
-    chunks = jnp.stack([(at_x + d) % 4 for d in (0, 1, 3, 2)] + [4 + (at_y + d) % 4 for d in (0, 1, 3, 2)])
-    parts = [parts_x[0]] + back_x + [parts_y[0]] + back_y
-    return downdate(chunks.astype(jnp.int32), parts, cov_slab)
+    out = downdate([at_x, 4 + at_y], [parts_x[0], parts_y[0]], cov_slab)
+    out = downdate([(at_x + d) % 4 for d in (1, 3, 2)], back_x, cov_slab, out)
+    return downdate([4 + (at_y + d) % 4 for d in (1, 3, 2)], back_y, cov_slab, out)
 
 
 def solution(mesh):

time: 286 us -> 272 us (0.951)
  Pallas kernels: 180 us -> 163 us
    pallas_call x1, Pallas kernels: 57.5 us -> 43.9 us  [minus_inverse(): pl.pallas_call(functools.partial(inverse_kernel, size=size), grid=(1,), i...]
    ppermute x3, waiting for transfers between devices: 11.5 us -> 0.01 us  [shards(): lax.ppermute(part, 'obs', steps_along(0, -d))]
    pallas_call x2, Pallas kernels: 65.6 us -> 58.5 us  [predict(): pl.pallas_call(functools.partial(predict_kernel, tile=tile, crossing=cros...]
    ppermute x3, waiting for transfers between devices: 5.35 us -> 10.8 us  [shards(): from_x = [lax.ppermute(solved, 'obs', steps_along(2, d)) for d in (1, 3, 2)]]
    ppermute x3, waiting for transfers between devices: 8.02 us -> 13.2 us  [shards(): lax.ppermute(part, 'obs', steps_along(2, -d))]
    pallas_call x1 -> x3, Pallas kernels: 12.1 us -> 15.9 us  [downdate(): pl.pallas_call(functools.partial(downdate_kernel, count=count), grid_spec...]
    ppermute x3, starting transfers between devices: 6.23 us -> 9.89 us  [shards(): from_y = [lax.ppermute(solved, 'obs', steps_along(0, d)) for d in (1, 3, 2)]]
  transfers between devices with their start and end apart: 18 -> 18, of which waited for: 11 -> 6; matrix products, arithmetic and copies ran while one was open for 2% -> 3% of each run, Pallas kernels for 57% -> 56%
where the time goes in v4:
time: 272 us; the launch traced here: 270 us
  Pallas kernels  163 us (60%)
  waiting for transfers between devices  50 us (18%)
  starting transfers between devices  42.4 us (16%)
  other arithmetic  7.8 us (3%)
  local copies, waits for them, and re-layouts  6.15 us (2%)
    pallas_call x2, Pallas kernels, predict(): pl.pallas_call(functools.partial(predict_kernel, tile=tile, crossing=cros...  58.5 us
    pallas_call x1, Pallas kernels, minus_inverse(): pl.pallas_call(functools.partial(inverse_kernel, size=size), grid=(1,), i...  43.9 us
    all_to_all x1, waiting for transfers between devices, to_all(): lax.all_to_all(jnp.broadcast_to(piece[None], (everyone,) + piece.shape),...  19.2 us
    pallas_call x1, Pallas kernels, spread(): pl.pallas_call(spread_kernel, grid=(everyone,), in_specs=[pl.BlockSpec((s...  18.7 us
    pallas_call x3, Pallas kernels, downdate(): pl.pallas_call(functools.partial(downdate_kernel, count=count), grid_spec...  15.9 us
    ppermute x3, waiting for transfers between devices, shards(): lax.ppermute(part, 'obs', steps_along(2, -d))  13.2 us
    pallas_call x2, Pallas kernels, products(): pl.pallas_call(functools.partial(product_kernel, members=members), grid=(...  12.2 us
    ppermute x3, waiting for transfers between devices, shards(): from_x = [lax.ppermute(solved, 'obs', steps_along(2, d)) for d in (1, 3, 2)]  10.8 us
  transfers between devices with their start and end apart: 18, of which 6 were waited for; matrix products, arithmetic and copies ran while one was open for 3% of the time, Pallas kernels for 56%

profile of v4, /device:TPU:66, one launch (start us, length us, event | category | flops | bytes accessed | tf_op | source)
XLA Modules:
  0.0 270.0 jit_solution(4173609768384064139)
XLA Ops:
  3.4 2.2 broadcast_in_dim.62
  5.6 10.1 %all-to-all-start = ((f32[32,16,1792]{2,1,0:T(8,128)}), f32[32,16,1792]{2,1,0:T(8,128)}, u32[]{:S(2)}, u32[]{:S(2)}) async-start(f32[32,16,1792]{2,1,0:T(8,128)} %broadcast_in_dim.62), calls=%async_computation | async-start | bytes 7340032 | tf_op jit(solution)/shard_map/all_to_all | solution.py:434
  15.7 18.7 %spread.1 = bf16[32,2,32,2048]{3,2,1,0:T(8,128)(2,1)} custom-call(bf16[32,16384]{1,0:T(8,128)(2,1)} %bitcast.16, bf16[32,16384]{1,0:T(8,128)(2,1)} %bitcast.17), custom_call_target="tpu_custom_call" | custom-call | bytes 8388608 | tf_op jit(solution)/shard_map/spread/pallas_call | solution.py:321
  34.4 9.3 %split.1.far_ref = bf16[16384,256]{1,0:T(8,128)(2,1)} custom-call(f32[16384,128]{1,0:T(8,128)} %refs_3_.3), custom_call_target="tpu_custom_call" | custom-call | flops 8388608 | bytes 16777216 | tf_op jit(solution)/shard_map/split/pallas_call | solution.py:41
  43.7 19.2 %all-to-all-done.own_ref = f32[32,16,1792]{2,1,0:T(8,128)} async-done(((f32[32,16,1792]{2,1,0:T(8,128)}), f32[32,16,1792]{2,1,0:T(8,128)}, u32[]{:S(2)}, u32[]{:S(2)}) %all-to-all-start) | async-done | bytes 3670048 | tf_op jit(solution)/shard_map/all_to_all | solution.py:434
  64.9 8.8 %all-to-all-start.1 = ((bf16[32,2,32,2048]{3,2,1,0:T(8,128)(2,1)}), bf16[32,2,32,2048]{3,2,1,0:T(8,128)(2,1)}, u32[]{:S(2)}, u32[]{:S(2)}) async-start(bf16[32,2,32,2048]{3,2,1,0:T(8,128)(2,1)} %spread.1), calls=%async_computation.1 | async-start | bytes 16777216 | tf_op jit(solution)/shard_map/all_to_all | solution.py:463
  73.7 29.2 %predict.2 = f32[512,128]{1,0:T(8,128)} custom-call(s32[8192]{0:T(1024)} %reshape.52.place_ref, f32[512,1792]{1,0:T(8,128)} %bitcast.6.slots_ref, bf16[16384,256]{1,0:T(8,128)(2,1)} %split.1.far_ref), custom_call_target="tpu_custom_call" | custom-call | flops 12884901888 | bytes 8388608 | tf_op jit(solution)/shard_map/predict/pallas_call | solution.py:128
  104.7 29.3 %predict.3 = f32[512,128]{1,0:T(8,128)} custom-call(s32[8192]{0:T(1024)} %reshape.54.place_ref, f32[512,1792]{1,0:T(8,128)} %bitcast.7.slots_ref, bf16[16384,256]{1,0:T(8,128)(2,1)} %split.1.far_ref), custom_call_target="tpu_custom_call" | custom-call | flops 12884901888 | bytes 8388608 | tf_op jit(solution)/shard_map/predict/pallas_call | solution.py:128
  137.1 1.9 collective-permute-start.3
  139.0 43.9 %minus_inverse.1.minus_ref = f32[1024,1024]{1,0:T(8,128)} custom-call(s32[1]{0:T(128)} %bitcast.3.core_ref, f32[32,16,1792]{2,1,0:T(8,128)} %all-to-all-done.own_ref, f32[32,16,1792]{2,1,0:T(8,128)} %collective-permute-done.other_ref), custom_call_target="tpu_custom_call" | custom-call | flops 64424509440 | bytes 8388608 | tf_op jit(solution)/shard_map/minus_inverse/pallas_call | solution.py:276
  183.8 4.2 %solve.1.refs_0_ = bf16[128,1024]{1,0:T(8,128)(2,1)} custom-call(f32[1024,1024]{1,0:T(8,128)} %minus_inverse.1.minus_ref, f32[32,2,16,128]{3,2,1,0:T(8,128)} %add.104.predicted_ref), custom_call_target="tpu_custom_call" | custom-call | flops 805306368 | bytes 4194304 | tf_op jit(solution)/shard_map/solve/pallas_call | solution.py:301
  190.0 2.1 collective-permute-start.6
  195.3 10.8 %collective-permute-done.4.refs_1_ = bf16[128,1024]{1,0:T(8,128)(2,1)S(1)} collective-permute-done((bf16[128,1024]{1,0:T(8,128)(2,1)}, bf16[128,1024]{1,0:T(8,128)(2,1)S(1)}, u32[]{:S(2)}, u32[]{:S(2)}) %collective-permute-start.4) | collective-permute-done | bytes 262176 | tf_op jit(solution)/shard_map/ppermute | solution.py:483
  206.1 6.7 %collective-permute-start.9 = (bf16[128,1024]{1,0:T(8,128)(2,1)}, bf16[128,1024]{1,0:T(8,128)(2,1)S(1)}, u32[]{:S(2)}, u32[]{:S(2)}) collective-permute-start(bf16[128,1024]{1,0:T(8,128)(2,1)} %solve.1.refs_0_), channel_id=1, source_target_pairs={{0,64},{4,68},{8,72},{12,76},{16,80},{20,84},{24,88},{28,92},{32,9... | collective-permute-start | bytes 786440 | tf_op jit(solution)/shard_map/ppermute | solution.py:484
  212.9 5.3 %collective-permute-done.9.refs_3_ = bf16[128,1024]{1,0:T(8,128)(2,1)S(1)} collective-permute-done((bf16[128,1024]{1,0:T(8,128)(2,1)}, bf16[128,1024]{1,0:T(8,128)(2,1)S(1)}, u32[]{:S(2)}, u32[]{:S(2)}) %collective-permute-start.9) | collective-permute-done | bytes 262176 | tf_op jit(solution)/shard_map/ppermute | solution.py:484
  218.2 6.1 %products.3 = (f32[128,2048]{1,0:T(8,128)}, bf16[128,2048]{1,0:T(8,128)(2,1)}, bf16[128,2048]{1,0:T(8,128)(2,1)}, bf16[128,2048]{1,0:T(8,128)(2,1)}) custom-call(bf16[128,1024]{1,0:T(8,128)(2,1)} %solve.1.refs_0_, bf16[128,1024]{1,0:T(8,128)(2,1)} %copy-done.11, bf16[128,1024]{1,0:T(8,128)(2,1)} %copy-done.12, bf16[128,1024]{1,0:T(8,128)(2,1)} %copy-done.13, ...), custom_call_target="tpu_custom_call" | custom-call | flops 2147483648 | bytes 4194304 | tf_op jit(solution)/shard_map/products/pallas_call | solution.py:356
  224.4 2.0 collective-permute-start.14
  226.5 6.1 %products.2 = (f32[128,2048]{1,0:T(8,128)}, bf16[128,2048]{1,0:T(8,128)(2,1)}, bf16[128,2048]{1,0:T(8,128)(2,1)}, bf16[128,2048]{1,0:T(8,128)(2,1)}) custom-call(bf16[128,1024]{1,0:T(8,128)(2,1)} %solve.1.refs_0_, bf16[128,1024]{1,0:T(8,128)(2,1)} %copy-done.8, bf16[128,1024]{1,0:T(8,128)(2,1)} %copy-done.9, bf16[128,1024]{1,0:T(8,128)(2,1)} %copy-done.10, ...), custom_call_target="tpu_custom_call" | custom-call | flops 2147483648 | bytes 4194304 | tf_op jit(solution)/shard_map/products/pallas_call | solution.py:356
  232.5 2.0 collective-permute-start.11
  234.6 13.2 %collective-permute-done.13.refs_0_ = bf16[128,2048]{1,0:T(8,128)(2,1)S(1)} collective-permute-done((bf16[128,2048]{1,0:T(8,128)(2,1)}, bf16[128,2048]{1,0:T(8,128)(2,1)S(1)}, u32[]{:S(2)}, u32[]{:S(2)}) %collective-permute-start.13) | collective-permute-done | bytes 524320 | tf_op jit(solution)/shard_map/ppermute | solution.py:487
  247.8 3.0 %collective-permute-start.12 = (bf16[128,2048]{1,0:T(8,128)(2,1)}, bf16[128,2048]{1,0:T(8,128)(2,1)S(1)}, u32[]{:S(2)}, u32[]{:S(2)}) collective-permute-start(bf16[128,2048]{1,0:T(8,128)(2,1)} %get-tuple-element.40), channel_id=1, source_target_pairs={{0,64},{4,68},{8,72},{12,76},{16,80},{20,84},{24,88},{28,92},{32,9... | collective-permute-start | bytes 1572872 | tf_op jit(solution)/shard_map/ppermute | solution.py:489
  251.9 4.2 %downdate.3.refs_4_ = f32[16384,128]{1,0:T(8,128)} custom-call(s32[2]{0:T(128)} %pad_add_fusion.2.chunk_ref, f32[128,2048]{1,0:T(8,128)} %get-tuple-element.47.refs_0_, f32[128,2048]{1,0:T(8,128)} %get-tuple-element.48.refs_1_, f32[16384,128]{1,0:T(8,128)} %refs_3_.3), custom_call_target="tpu_custom_call" | custom-call | flops 524288 | bytes 5242880 | tf_op jit(solution)/shard_map/downdate/pallas_call | solution.py:387
  257.2 5.8 %downdate.4.refs_4_ = f32[16384,128]{1,0:T(8,128)} custom-call(s32[3]{0:T(128)} %get-tuple-element.54.chunk_ref, bf16[128,2048]{1,0:T(8,128)(2,1)} %copy-done.2, bf16[128,2048]{1,0:T(8,128)(2,1)} %copy-done.3, bf16[128,2048]{1,0:T(8,128)(2,1)} %copy-done.5, f32[16384,128]{1,0:T(8,128)} %refs_3_.3, ...), custom_call_target="tpu_custom_call", output_to_operand_aliasing={{}: (5, {})} | custom-call | flops 786432 | bytes 7864320 | tf_op jit(solution)/shard_map/downdate/pallas_call | solution.py:387
  264.1 5.9 %downdate.5 = f32[16384,128]{1,0:T(8,128)} custom-call(s32[3]{0:T(128)} %get-tuple-element.53.chunk_ref, bf16[128,2048]{1,0:T(8,128)(2,1)} %copy-done.4, bf16[128,2048]{1,0:T(8,128)(2,1)} %copy-done.6, bf16[128,2048]{1,0:T(8,128)(2,1)} %copy-done.7, f32[16384,128]{1,0:T(8,128)} %refs_3_.3, f32[16384,128]{1,0:T(8,128)} %downdate.4.refs_4_), custom_call_target="tpu_custom_call", output_to_operand_aliasing={{}: (5, {})} | custom-call | flops 786432 | bytes 7864320 | tf_op jit(solution)/shard_map/downdate/pallas_call | solution.py:387
  (75 shorter events, 19.1 us)
Async XLA Ops:
  5.6 57.4 %all-to-all-start = ((f32[32,16,1792]{2,1,0:T(8,128)}), f32[32,16,1792]{2,1,0:T(8,128)}, u32[]{:S(2)}, u32[]{:S(2)}) async-start(f32[32,16,1792]{2,1,0:T(8,128)} %broadcast_in_dim.62), calls=%async_computation | async-start | bytes 7340032 | tf_op jit(solution)/shard_map/all_to_all | solution.py:434
  63.0 39.8 %collective-permute-start = (f32[32,16,1792]{2,1,0:T(8,128)}, f32[32,16,1792]{2,1,0:T(8,128)}, u32[]{:S(2)}, u32[]{:S(2)}) collective-permute-start(f32[32,16,1792]{2,1,0:T(8,128)} %all-to-all-done.own_ref), channel_id=1, source_target_pairs={{0,1},{1,0},{2,3},{3,2},{4,5},{5,4},{6,7},{7,6},{8,9},{9,8},{10,11... | collective-permute-start | bytes 11010056 | tf_op jit(solution)/shard_map/ppermute | solution.py:464
  64.9 153.3 %all-to-all-start.1 = ((bf16[32,2,32,2048]{3,2,1,0:T(8,128)(2,1)}), bf16[32,2,32,2048]{3,2,1,0:T(8,128)(2,1)}, u32[]{:S(2)}, u32[]{:S(2)}) async-start(bf16[32,2,32,2048]{3,2,1,0:T(8,128)(2,1)} %spread.1), calls=%async_computation.1 | async-start | bytes 16777216 | tf_op jit(solution)/shard_map/all_to_all | solution.py:463
  104.7 29.4 %copy-start.14 = (f32[512,128]{1,0:T(8,128)S(1)}, f32[512,128]{1,0:T(8,128)}, u32[]{:S(2)}) copy-start(f32[512,128]{1,0:T(8,128)} %predict.2) | copy-start | bytes 786436
  134.1 1.8 collective-permute-start.1
  134.2 1.9 collective-permute-start.2
  137.1 45.8 %collective-permute-start.3 = (f32[32,2,16,128]{3,2,1,0:T(8,128)S(1)}, f32[32,2,16,128]{3,2,1,0:T(8,128)S(1)}, u32[]{:S(2)}, u32[]{:S(2)}) collective-permute-start(f32[32,2,16,128]{3,2,1,0:T(8,128)S(1)} %pad_maximum_fusion), channel_id=1, source_target_pairs={{0,2},{2,0},{1,3},{3,1},{4,6},{6,4},{5,7},{7,5},{8,10},{10,8},{9,1... | collective-permute-start | bytes 1572872 | tf_op jit(solution)/shard_map/ppermute | solution.py:477
  188.0 18.1 %collective-permute-start.4 = (bf16[128,1024]{1,0:T(8,128)(2,1)}, bf16[128,1024]{1,0:T(8,128)(2,1)S(1)}, u32[]{:S(2)}, u32[]{:S(2)}) collective-permute-start(bf16[128,1024]{1,0:T(8,128)(2,1)} %solve.1.refs_0_), channel_id=1, source_target_pairs={{0,4},{4,8},{8,12},{12,0},{16,20},{20,24},{24,28},{28,16},{32,36},... | collective-permute-start | bytes 786440 | tf_op jit(solution)/shard_map/ppermute | solution.py:483
  189.5 23.3 %collective-permute-start.5 = (bf16[128,1024]{1,0:T(8,128)(2,1)}, bf16[128,1024]{1,0:T(8,128)(2,1)S(1)}, u32[]{:S(2)}, u32[]{:S(2)}) collective-permute-start(bf16[128,1024]{1,0:T(8,128)(2,1)} %solve.1.refs_0_), channel_id=1, source_target_pairs={{0,12},{4,0},{8,4},{12,8},{16,28},{20,16},{24,20},{28,24},{32,44},... | collective-permute-start | bytes 786440 | tf_op jit(solution)/shard_map/ppermute | solution.py:483
  190.0 22.8 %collective-permute-start.6 = (bf16[128,1024]{1,0:T(8,128)(2,1)}, bf16[128,1024]{1,0:T(8,128)(2,1)S(1)}, u32[]{:S(2)}, u32[]{:S(2)}) collective-permute-start(bf16[128,1024]{1,0:T(8,128)(2,1)} %solve.1.refs_0_), channel_id=1, source_target_pairs={{0,8},{4,12},{8,0},{12,4},{16,24},{20,28},{24,16},{28,20},{32,40},... | collective-permute-start | bytes 786440 | tf_op jit(solution)/shard_map/ppermute | solution.py:483
  192.1 20.7 %collective-permute-start.7 = (bf16[128,1024]{1,0:T(8,128)(2,1)}, bf16[128,1024]{1,0:T(8,128)(2,1)S(1)}, u32[]{:S(2)}, u32[]{:S(2)}) collective-permute-start(bf16[128,1024]{1,0:T(8,128)(2,1)} %solve.1.refs_0_), channel_id=1, source_target_pairs={{0,32},{4,36},{8,40},{12,44},{16,48},{20,52},{24,56},{28,60},{32,6... | collective-permute-start | bytes 786440 | tf_op jit(solution)/shard_map/ppermute | solution.py:484
  193.6 19.3 %collective-permute-start.8 = (bf16[128,1024]{1,0:T(8,128)(2,1)}, bf16[128,1024]{1,0:T(8,128)(2,1)S(1)}, u32[]{:S(2)}, u32[]{:S(2)}) collective-permute-start(bf16[128,1024]{1,0:T(8,128)(2,1)} %solve.1.refs_0_), channel_id=1, source_target_pairs={{0,96},{4,100},{8,104},{12,108},{16,112},{20,116},{24,120},{28,124... | collective-permute-start | bytes 786440 | tf_op jit(solution)/shard_map/ppermute | solution.py:484
  206.1 12.1 %copy-start.11 = (bf16[128,1024]{1,0:T(8,128)(2,1)}, bf16[128,1024]{1,0:T(8,128)(2,1)S(1)}, u32[]{:S(2)}) copy-start(bf16[128,1024]{1,0:T(8,128)(2,1)S(1)} %collective-permute-done.4.refs_1_) | copy-start | bytes 786436
  206.1 12.0 %collective-permute-start.9 = (bf16[128,1024]{1,0:T(8,128)(2,1)}, bf16[128,1024]{1,0:T(8,128)(2,1)S(1)}, u32[]{:S(2)}, u32[]{:S(2)}) collective-permute-start(bf16[128,1024]{1,0:T(8,128)(2,1)} %solve.1.refs_0_), channel_id=1, source_target_pairs={{0,64},{4,68},{8,72},{12,76},{16,80},{20,84},{24,88},{28,92},{32,9... | collective-permute-start | bytes 786440 | tf_op jit(solution)/shard_map/ppermute | solution.py:484
  212.8 11.5 %copy-start.8 = (bf16[128,1024]{1,0:T(8,128)(2,1)}, bf16[128,1024]{1,0:T(8,128)(2,1)S(1)}, u32[]{:S(2)}) copy-start(bf16[128,1024]{1,0:T(8,128)(2,1)S(1)} %collective-permute-done.7.refs_1_) | copy-start | bytes 786436
  212.9 11.5 %copy-start.9 = (bf16[128,1024]{1,0:T(8,128)(2,1)}, bf16[128,1024]{1,0:T(8,128)(2,1)S(1)}, u32[]{:S(2)}) copy-start(bf16[128,1024]{1,0:T(8,128)(2,1)S(1)} %collective-permute-done.8.refs_2_) | copy-start | bytes 786436
  218.2 6.2 %copy-start.10 = (bf16[128,1024]{1,0:T(8,128)(2,1)}, bf16[128,1024]{1,0:T(8,128)(2,1)S(1)}, u32[]{:S(2)}) copy-start(bf16[128,1024]{1,0:T(8,128)(2,1)S(1)} %collective-permute-done.9.refs_3_) | copy-start | bytes 786436
  224.4 23.4 %collective-permute-start.13 = (bf16[128,2048]{1,0:T(8,128)(2,1)}, bf16[128,2048]{1,0:T(8,128)(2,1)S(1)}, u32[]{:S(2)}, u32[]{:S(2)}) collective-permute-start(bf16[128,2048]{1,0:T(8,128)(2,1)} %get-tuple-element.44), channel_id=1, source_target_pairs={{0,12},{4,0},{8,4},{12,8},{16,28},{20,16},{24,20},{28,24},{32,44},... | collective-permute-start | bytes 1572872 | tf_op jit(solution)/shard_map/ppermute | solution.py:487
  224.4 31.7 %collective-permute-start.14 = (bf16[128,2048]{1,0:T(8,128)(2,1)}, bf16[128,2048]{1,0:T(8,128)(2,1)S(1)}, u32[]{:S(2)}, u32[]{:S(2)}) collective-permute-start(bf16[128,2048]{1,0:T(8,128)(2,1)} %get-tuple-element.45), channel_id=1, source_target_pairs={{0,4},{4,8},{8,12},{12,0},{16,20},{20,24},{24,28},{28,16},{32,36},... | collective-permute-start | bytes 1572872 | tf_op jit(solution)/shard_map/ppermute | solution.py:487
  226.5 29.7 %collective-permute-start.15 = (bf16[128,2048]{1,0:T(8,128)(2,1)}, bf16[128,2048]{1,0:T(8,128)(2,1)S(1)}, u32[]{:S(2)}, u32[]{:S(2)}) collective-permute-start(bf16[128,2048]{1,0:T(8,128)(2,1)} %get-tuple-element.46), channel_id=1, source_target_pairs={{0,8},{4,12},{8,0},{12,4},{16,24},{20,28},{24,16},{28,20},{32,40},... | collective-permute-start | bytes 1572872 | tf_op jit(solution)/shard_map/ppermute | solution.py:487
  232.5 30.4 %collective-permute-start.10 = (bf16[128,2048]{1,0:T(8,128)(2,1)}, bf16[128,2048]{1,0:T(8,128)(2,1)S(1)}, u32[]{:S(2)}, u32[]{:S(2)}) collective-permute-start(bf16[128,2048]{1,0:T(8,128)(2,1)} %get-tuple-element.38), channel_id=1, source_target_pairs={{0,96},{4,100},{8,104},{12,108},{16,112},{20,116},{24,120},{28,124... | collective-permute-start | bytes 1572872 | tf_op jit(solution)/shard_map/ppermute | solution.py:489
  232.5 30.4 %collective-permute-start.11 = (bf16[128,2048]{1,0:T(8,128)(2,1)}, bf16[128,2048]{1,0:T(8,128)(2,1)S(1)}, u32[]{:S(2)}, u32[]{:S(2)}) collective-permute-start(bf16[128,2048]{1,0:T(8,128)(2,1)} %get-tuple-element.39), channel_id=1, source_target_pairs={{0,32},{4,36},{8,40},{12,44},{16,48},{20,52},{24,56},{28,60},{32,6... | collective-permute-start | bytes 1572872 | tf_op jit(solution)/shard_map/ppermute | solution.py:489
  247.8 8.4 %copy-start.2 = (bf16[128,2048]{1,0:T(8,128)(2,1)}, bf16[128,2048]{1,0:T(8,128)(2,1)S(1)}, u32[]{:S(2)}) copy-start(bf16[128,2048]{1,0:T(8,128)(2,1)S(1)} %collective-permute-done.13.refs_0_) | copy-start | bytes 1572868
  247.8 15.2 %collective-permute-start.12 = (bf16[128,2048]{1,0:T(8,128)(2,1)}, bf16[128,2048]{1,0:T(8,128)(2,1)S(1)}, u32[]{:S(2)}, u32[]{:S(2)}) collective-permute-start(bf16[128,2048]{1,0:T(8,128)(2,1)} %get-tuple-element.40), channel_id=1, source_target_pairs={{0,64},{4,68},{8,72},{12,76},{16,80},{20,84},{24,88},{28,92},{32,9... | collective-permute-start | bytes 1572872 | tf_op jit(solution)/shard_map/ppermute | solution.py:489
  (9 other events, 23.1 us)

commit v5 on v4

--- a/solution.py
+++ b/solution.py
@@ -291,22 +291,22 @@
     )(core, own, other)
 
 
-def solve_kernel(minus_ref, predicted_ref, out_ref):
-    predicted = predicted_ref[...].reshape(minus_ref.shape[0], -1)
+def solve_kernel(minus_ref, here_ref, there_ref, out_ref):
+    predicted = (here_ref[...] + there_ref[...]).reshape(minus_ref.shape[0], -1)
     out_ref[...] = (-dot_split(predicted.T, minus_ref[...])).astype(BF16)
 
 
-def solve_turned(minus, predicted):
-    n, columns = minus.shape[0], predicted.shape[-1]
+def solve_turned(minus, here, there):
+    n, columns = minus.shape[0], here.shape[-1]
     return pl.pallas_call(
         solve_kernel,
-        in_specs=[pl.BlockSpec(memory_space=pltpu.VMEM)] * 2,
+        in_specs=[pl.BlockSpec(memory_space=pltpu.VMEM)] * 3,
         out_specs=pl.BlockSpec(memory_space=pltpu.VMEM),
         out_shape=jax.ShapeDtypeStruct((columns, n), BF16),
         compiler_params=pltpu.CompilerParams(vmem_limit_bytes=VMEM_LIMIT),
         cost_estimate=pl.CostEstimate(flops=6 * n * n * columns, bytes_accessed=4 * n * n, transcendentals=0),
         name="solve",
-    )(minus, predicted)
+    )(minus, here, there)
 
 
 def spread_kernel(by_x_ref, by_y_ref, out_ref):
@@ -352,7 +352,7 @@
     members = len(solved)
     columns, n = solved[0].shape
     everyone, _, slots, width = cross.shape
-    tile = 512
+    tile = 1024
     return pl.pallas_call(
         functools.partial(product_kernel, members=members),
         grid=(width // tile,),
@@ -474,22 +474,22 @@
     high = jnp.where(core == 0, theirs, mine).reshape(everyone, 1, share, columns)
     chip_sum = jnp.concatenate([low, high], axis=1)
     chip_sum, other = lax.optimization_barrier((chip_sum, other))
-    predicted = chip_sum + lax.ppermute(chip_sum, "vox", [(0, 2), (2, 0), (1, 3), (3, 1)])
+    there = lax.ppermute(chip_sum, "vox", [(0, 2), (2, 0), (1, 3), (3, 1)])
     minus = minus_inverse(core_array, own, other, skip)
-    solved = solve_turned(minus, predicted)
+    solved = solve_turned(minus, chip_sum, there)
 
     at_x = device % 4
     at_y = device // 8
-    from_x = [lax.ppermute(solved, "obs", steps_along(2, d)) for d in (1, 3, 2)]
-    from_y = [lax.ppermute(solved, "obs", steps_along(0, d)) for d in (1, 3, 2)]
+    from_x = [lax.ppermute(solved, "obs", steps_along(2, d)) for d in (2, 1, 3)]
+    from_y = [lax.ppermute(solved, "obs", steps_along(0, d)) for d in (2, 1, 3)]
     solved, from_x, from_y = lax.optimization_barrier((solved, from_x, from_y))
     parts_x = products([solved] + from_x, cross, 0)
-    back_x = [lax.ppermute(part, "obs", steps_along(2, -d)) for part, d in zip(parts_x[1:], (1, 3, 2))]
+    back_x = [lax.ppermute(part, "obs", steps_along(2, -d)) for part, d in zip(parts_x[1:], (2, 1, 3))]
     parts_y = products([solved] + from_y, cross, 1)
-    back_y = [lax.ppermute(part, "obs", steps_along(0, -d)) for part, d in zip(parts_y[1:], (1, 3, 2))]
+    back_y = [lax.ppermute(part, "obs", steps_along(0, -d)) for part, d in zip(parts_y[1:], (2, 1, 3))]
     out = downdate([at_x, 4 + at_y], [parts_x[0], parts_y[0]], cov_slab)
-    out = downdate([(at_x + d) % 4 for d in (1, 3, 2)], back_x, cov_slab, out)
-    return downdate([4 + (at_y + d) % 4 for d in (1, 3, 2)], back_y, cov_slab, out)
+    out = downdate([(at_x + d) % 4 for d in (2, 1, 3)], back_x, cov_slab, out)
+    return downdate([4 + (at_y + d) % 4 for d in (2, 1, 3)], back_y, cov_slab, out)
 
 
 def solution(mesh):

time: 272 us -> 270 us (level)
  waiting for transfers between devices: 50 us -> 37.1 us
  starting transfers between devices: 42.4 us -> 53.9 us
    ppermute x3, waiting for transfers between devices: 13.2 us -> 0.01 us  [shards(): lax.ppermute(part, 'obs', steps_along(2, -d))]
    ppermute x3, starting transfers between devices: 4.99 us -> 13.8 us  [shards(): lax.ppermute(part, 'obs', steps_along(0, -d))]
    ppermute x3, waiting for transfers between devices: 0.01 us -> 6.4 us  [shards(): lax.ppermute(part, 'obs', steps_along(0, -d))]
    ppermute x7, waiting for transfers between devices: 16.1 us -> 10.1 us  [the longest x3 6.4 us: shards(): from_x = [lax.ppermute(solved, 'obs', steps_along(2, d)) for d in (2, 1, 3)]]
  transfers between devices with their start and end apart: 18 -> 18, of which waited for: 6 -> 8; matrix products, arithmetic and copies ran while one was open for 3% -> 2% of each run, Pallas kernels for 56% -> 56%
where the time goes in v5:
time: 270 us; the launch traced here: 267 us
  Pallas kernels  162 us (60%)
  starting transfers between devices  53.9 us (20%)
  waiting for transfers between devices  37.1 us (14%)
  other arithmetic  7.04 us (3%)
  local copies, waits for them, and re-layouts  6.6 us (2%)
    pallas_call x2, Pallas kernels, predict(): pl.pallas_call(functools.partial(predict_kernel, tile=tile, crossing=cros...  58.5 us
    pallas_call x1, Pallas kernels, minus_inverse(): pl.pallas_call(functools.partial(inverse_kernel, size=size), grid=(1,), i...  43.9 us
    all_to_all x1, waiting for transfers between devices, to_all(): lax.all_to_all(jnp.broadcast_to(piece[None], (everyone,) + piece.shape),...  19.2 us
    pallas_call x1, Pallas kernels, spread(): pl.pallas_call(spread_kernel, grid=(everyone,), in_specs=[pl.BlockSpec((s...  18.8 us
    pallas_call x3, Pallas kernels, downdate(): pl.pallas_call(functools.partial(downdate_kernel, count=count), grid_spec...  15.9 us
    ppermute x3, starting transfers between devices, shards(): lax.ppermute(part, 'obs', steps_along(0, -d))  13.8 us
    ppermute x3, starting transfers between devices, shards(): from_y = [lax.ppermute(solved, 'obs', steps_along(0, d)) for d in (2, 1, 3)]  12.4 us
    pallas_call x2, Pallas kernels, products(): pl.pallas_call(functools.partial(product_kernel, members=members), grid=(...  11 us
  transfers between devices with their start and end apart: 18, of which 8 were waited for; matrix products, arithmetic and copies ran while one was open for 2% of the time, Pallas kernels for 56%

profile of v5, /device:TPU:66, one launch (start us, length us, event | category | flops | bytes accessed | tf_op | source)
XLA Modules:
  0.0 267.3 jit_solution(14898240314205539185)
XLA Ops:
  3.4 2.2 broadcast_in_dim.62
  5.6 10.1 %all-to-all-start = ((f32[32,16,1792]{2,1,0:T(8,128)}), f32[32,16,1792]{2,1,0:T(8,128)}, u32[]{:S(2)}, u32[]{:S(2)}) async-start(f32[32,16,1792]{2,1,0:T(8,128)} %broadcast_in_dim.62), calls=%async_computation | async-start | bytes 7340032 | tf_op jit(solution)/shard_map/all_to_all | solution.py:434
  15.7 18.8 %spread.1 = bf16[32,2,32,2048]{3,2,1,0:T(8,128)(2,1)} custom-call(bf16[32,16384]{1,0:T(8,128)(2,1)} %bitcast.16, bf16[32,16384]{1,0:T(8,128)(2,1)} %bitcast.17), custom_call_target="tpu_custom_call" | custom-call | bytes 8388608 | tf_op jit(solution)/shard_map/spread/pallas_call | solution.py:321
  34.4 9.3 %split.1.far_ref = bf16[16384,256]{1,0:T(8,128)(2,1)} custom-call(f32[16384,128]{1,0:T(8,128)} %refs_3_.3), custom_call_target="tpu_custom_call" | custom-call | flops 8388608 | bytes 16777216 | tf_op jit(solution)/shard_map/split/pallas_call | solution.py:41
  43.8 19.2 %all-to-all-done.own_ref = f32[32,16,1792]{2,1,0:T(8,128)} async-done(((f32[32,16,1792]{2,1,0:T(8,128)}), f32[32,16,1792]{2,1,0:T(8,128)}, u32[]{:S(2)}, u32[]{:S(2)}) %all-to-all-start) | async-done | bytes 3670048 | tf_op jit(solution)/shard_map/all_to_all | solution.py:434
  64.9 8.8 %all-to-all-start.1 = ((bf16[32,2,32,2048]{3,2,1,0:T(8,128)(2,1)}), bf16[32,2,32,2048]{3,2,1,0:T(8,128)(2,1)}, u32[]{:S(2)}, u32[]{:S(2)}) async-start(bf16[32,2,32,2048]{3,2,1,0:T(8,128)(2,1)} %spread.1), calls=%async_computation.1 | async-start | bytes 16777216 | tf_op jit(solution)/shard_map/all_to_all | solution.py:463
  73.6 29.2 %predict.2 = f32[512,128]{1,0:T(8,128)} custom-call(s32[8192]{0:T(1024)} %reshape.52.place_ref, f32[512,1792]{1,0:T(8,128)} %bitcast.6.slots_ref, bf16[16384,256]{1,0:T(8,128)(2,1)} %split.1.far_ref), custom_call_target="tpu_custom_call" | custom-call | flops 12884901888 | bytes 8388608 | tf_op jit(solution)/shard_map/predict/pallas_call | solution.py:128
  104.7 29.3 %predict.3 = f32[512,128]{1,0:T(8,128)} custom-call(s32[8192]{0:T(1024)} %reshape.54.place_ref, f32[512,1792]{1,0:T(8,128)} %bitcast.7.slots_ref, bf16[16384,256]{1,0:T(8,128)(2,1)} %split.1.far_ref), custom_call_target="tpu_custom_call" | custom-call | flops 12884901888 | bytes 8388608 | tf_op jit(solution)/shard_map/predict/pallas_call | solution.py:128
  139.0 43.9 %minus_inverse.1.minus_ref = f32[1024,1024]{1,0:T(8,128)} custom-call(s32[1]{0:T(128)} %bitcast.3.core_ref, f32[32,16,1792]{2,1,0:T(8,128)} %all-to-all-done.own_ref, f32[32,16,1792]{2,1,0:T(8,128)} %collective-permute-done.other_ref), custom_call_target="tpu_custom_call" | custom-call | flops 64424509440 | bytes 8388608 | tf_op jit(solution)/shard_map/minus_inverse/pallas_call | solution.py:276
  183.7 4.4 %solve.1.refs_0_ = bf16[128,1024]{1,0:T(8,128)(2,1)} custom-call(f32[1024,1024]{1,0:T(8,128)} %minus_inverse.1.minus_ref, f32[32,2,16,128]{3,2,1,0:T(8,128)} %copy-done.2, f32[32,2,16,128]{3,2,1,0:T(8,128)} %copy-done.9), custom_call_target="tpu_custom_call" | custom-call | flops 805306368 | bytes 4194304 | tf_op jit(solution)/shard_map/solve/pallas_call | solution.py:301
  188.1 2.1 collective-permute-start.4
  190.2 2.0 collective-permute-start.6
  192.2 3.0 %collective-permute-start.7 = (bf16[128,1024]{1,0:T(8,128)(2,1)}, bf16[128,1024]{1,0:T(8,128)(2,1)S(1)}, u32[]{:S(2)}, u32[]{:S(2)}) collective-permute-start(bf16[128,1024]{1,0:T(8,128)(2,1)} %solve.1.refs_0_), channel_id=1, source_target_pairs={{0,64},{4,68},{8,72},{12,76},{16,80},{20,84},{24,88},{28,92},{32,9... | collective-permute-start | bytes 786440 | tf_op jit(solution)/shard_map/ppermute | solution.py:484
  195.8 5.4 %collective-permute-done.4.refs_1_ = bf16[128,1024]{1,0:T(8,128)(2,1)S(1)} collective-permute-done((bf16[128,1024]{1,0:T(8,128)(2,1)}, bf16[128,1024]{1,0:T(8,128)(2,1)S(1)}, u32[]{:S(2)}, u32[]{:S(2)}) %collective-permute-start.4) | collective-permute-done | bytes 262176 | tf_op jit(solution)/shard_map/ppermute | solution.py:483
  201.2 8.8 %collective-permute-start.9 = (bf16[128,1024]{1,0:T(8,128)(2,1)}, bf16[128,1024]{1,0:T(8,128)(2,1)S(1)}, u32[]{:S(2)}, u32[]{:S(2)}) collective-permute-start(bf16[128,1024]{1,0:T(8,128)(2,1)} %solve.1.refs_0_), channel_id=1, source_target_pairs={{0,96},{4,100},{8,104},{12,108},{16,112},{20,116},{24,120},{28,124... | collective-permute-start | bytes 786440 | tf_op jit(solution)/shard_map/ppermute | solution.py:484
  211.1 3.7 %collective-permute-done.9.refs_3_ = bf16[128,1024]{1,0:T(8,128)(2,1)S(1)} collective-permute-done((bf16[128,1024]{1,0:T(8,128)(2,1)}, bf16[128,1024]{1,0:T(8,128)(2,1)S(1)}, u32[]{:S(2)}, u32[]{:S(2)}) %collective-permute-start.9) | collective-permute-done | bytes 262176 | tf_op jit(solution)/shard_map/ppermute | solution.py:484
  214.8 5.6 %products.3 = (f32[128,2048]{1,0:T(8,128)}, bf16[128,2048]{1,0:T(8,128)(2,1)}, bf16[128,2048]{1,0:T(8,128)(2,1)}, bf16[128,2048]{1,0:T(8,128)(2,1)}) custom-call(bf16[128,1024]{1,0:T(8,128)(2,1)} %solve.1.refs_0_, bf16[128,1024]{1,0:T(8,128)(2,1)} %copy-done.13, bf16[128,1024]{1,0:T(8,128)(2,1)} %copy-done.14, bf16[128,1024]{1,0:T(8,128)(2,1)} %copy-done.15, ...), custom_call_target="tpu_custom_call" | custom-call | flops 2147483648 | bytes 4194304 | tf_op jit(solution)/shard_map/products/pallas_call | solution.py:356
  220.5 2.0 collective-permute-start.14
  222.6 5.5 %products.2 = (f32[128,2048]{1,0:T(8,128)}, bf16[128,2048]{1,0:T(8,128)(2,1)}, bf16[128,2048]{1,0:T(8,128)(2,1)}, bf16[128,2048]{1,0:T(8,128)(2,1)}) custom-call(bf16[128,1024]{1,0:T(8,128)(2,1)} %solve.1.refs_0_, bf16[128,1024]{1,0:T(8,128)(2,1)} %copy-done.10, bf16[128,1024]{1,0:T(8,128)(2,1)} %copy-done.11, bf16[128,1024]{1,0:T(8,128)(2,1)} %copy-done.12, ...), custom_call_target="tpu_custom_call" | custom-call | flops 2147483648 | bytes 4194304 | tf_op jit(solution)/shard_map/products/pallas_call | solution.py:356
  228.0 11.8 %collective-permute-start.10 = (bf16[128,2048]{1,0:T(8,128)(2,1)}, bf16[128,2048]{1,0:T(8,128)(2,1)S(1)}, u32[]{:S(2)}, u32[]{:S(2)}) collective-permute-start(bf16[128,2048]{1,0:T(8,128)(2,1)} %get-tuple-element.38), channel_id=1, source_target_pairs={{0,64},{4,68},{8,72},{12,76},{16,80},{20,84},{24,88},{28,92},{32,9... | collective-permute-start | bytes 1572872 | tf_op jit(solution)/shard_map/ppermute | solution.py:489
  243.2 4.2 %downdate.3.refs_4_ = f32[16384,128]{1,0:T(8,128)} custom-call(s32[2]{0:T(128)} %pad_add_fusion.2.chunk_ref, f32[128,2048]{1,0:T(8,128)} %get-tuple-element.47.refs_0_, f32[128,2048]{1,0:T(8,128)} %get-tuple-element.48.refs_1_, f32[16384,128]{1,0:T(8,128)} %refs_3_.3), custom_call_target="tpu_custom_call" | custom-call | flops 524288 | bytes 5242880 | tf_op jit(solution)/shard_map/downdate/pallas_call | solution.py:387
  248.5 5.8 %downdate.4.refs_4_ = f32[16384,128]{1,0:T(8,128)} custom-call(s32[3]{0:T(128)} %get-tuple-element.54.chunk_ref, bf16[128,2048]{1,0:T(8,128)(2,1)} %copy-done.3, bf16[128,2048]{1,0:T(8,128)(2,1)} %copy-done.4, bf16[128,2048]{1,0:T(8,128)(2,1)} %copy-done.6, f32[16384,128]{1,0:T(8,128)} %refs_3_.3, ...), custom_call_target="tpu_custom_call", output_to_operand_aliasing={{}: (5, {})} | custom-call | flops 786432 | bytes 7864320 | tf_op jit(solution)/shard_map/downdate/pallas_call | solution.py:387
  254.2 5.2 %collective-permute-done.11.refs_1_ = bf16[128,2048]{1,0:T(8,128)(2,1)S(1)} collective-permute-done((bf16[128,2048]{1,0:T(8,128)(2,1)}, bf16[128,2048]{1,0:T(8,128)(2,1)S(1)}, u32[]{:S(2)}, u32[]{:S(2)}) %collective-permute-start.11) | collective-permute-done | bytes 524320 | tf_op jit(solution)/shard_map/ppermute | solution.py:489
  261.4 5.9 %downdate.5 = f32[16384,128]{1,0:T(8,128)} custom-call(s32[3]{0:T(128)} %get-tuple-element.53.chunk_ref, bf16[128,2048]{1,0:T(8,128)(2,1)} %copy-done.5, bf16[128,2048]{1,0:T(8,128)(2,1)} %copy-done.7, bf16[128,2048]{1,0:T(8,128)(2,1)} %copy-done.8, f32[16384,128]{1,0:T(8,128)} %refs_3_.3, f32[16384,128]{1,0:T(8,128)} %downdate.4.refs_4_), custom_call_target="tpu_custom_call", output_to_operand_aliasing={{}: (5, {})} | custom-call | flops 786432 | bytes 7864320 | tf_op jit(solution)/shard_map/downdate/pallas_call | solution.py:387
  (78 shorter events, 20.4 us)
Async XLA Ops:
  5.6 57.4 %all-to-all-start = ((f32[32,16,1792]{2,1,0:T(8,128)}), f32[32,16,1792]{2,1,0:T(8,128)}, u32[]{:S(2)}, u32[]{:S(2)}) async-start(f32[32,16,1792]{2,1,0:T(8,128)} %broadcast_in_dim.62), calls=%async_computation | async-start | bytes 7340032 | tf_op jit(solution)/shard_map/all_to_all | solution.py:434
  63.0 39.8 %collective-permute-start = (f32[32,16,1792]{2,1,0:T(8,128)}, f32[32,16,1792]{2,1,0:T(8,128)}, u32[]{:S(2)}, u32[]{:S(2)}) collective-permute-start(f32[32,16,1792]{2,1,0:T(8,128)} %all-to-all-done.own_ref), channel_id=1, source_target_pairs={{0,1},{1,0},{2,3},{3,2},{4,5},{5,4},{6,7},{7,6},{8,9},{9,8},{10,11... | collective-permute-start | bytes 11010056 | tf_op jit(solution)/shard_map/ppermute | solution.py:464
  64.9 149.9 %all-to-all-start.1 = ((bf16[32,2,32,2048]{3,2,1,0:T(8,128)(2,1)}), bf16[32,2,32,2048]{3,2,1,0:T(8,128)(2,1)}, u32[]{:S(2)}, u32[]{:S(2)}) async-start(bf16[32,2,32,2048]{3,2,1,0:T(8,128)(2,1)} %spread.1), calls=%async_computation.1 | async-start | bytes 16777216 | tf_op jit(solution)/shard_map/all_to_all | solution.py:463
  104.7 29.4 %copy-start.16 = (f32[512,128]{1,0:T(8,128)S(1)}, f32[512,128]{1,0:T(8,128)}, u32[]{:S(2)}) copy-start(f32[512,128]{1,0:T(8,128)} %predict.2) | copy-start | bytes 786436
  134.0 1.8 collective-permute-start.1
  134.1 1.9 collective-permute-start.2
  137.1 45.8 %copy-start.2 = (f32[32,2,16,128]{3,2,1,0:T(8,128)}, f32[32,2,16,128]{3,2,1,0:T(8,128)S(1)}, u32[]{:S(2)}) copy-start(f32[32,2,16,128]{3,2,1,0:T(8,128)S(1)} %pad_maximum_fusion.here_ref) | copy-start | bytes 1572868
  137.1 45.8 %collective-permute-start.3 = (f32[32,2,16,128]{3,2,1,0:T(8,128)S(1)}, f32[32,2,16,128]{3,2,1,0:T(8,128)S(1)}, u32[]{:S(2)}, u32[]{:S(2)}) collective-permute-start(f32[32,2,16,128]{3,2,1,0:T(8,128)S(1)} %pad_maximum_fusion.here_ref), channel_id=1, source_target_pairs={{0,2},{2,0},{1,3},{3,1},{4,6},{6,4},{5,7},{7,5},{8,10},{10,8},{9,1... | collective-permute-start | bytes 1572872 | tf_op jit(solution)/shard_map/ppermute | solution.py:477
  188.1 13.1 %collective-permute-start.4 = (bf16[128,1024]{1,0:T(8,128)(2,1)}, bf16[128,1024]{1,0:T(8,128)(2,1)S(1)}, u32[]{:S(2)}, u32[]{:S(2)}) collective-permute-start(bf16[128,1024]{1,0:T(8,128)(2,1)} %solve.1.refs_0_), channel_id=1, source_target_pairs={{0,8},{4,12},{8,0},{12,4},{16,24},{20,28},{24,16},{28,20},{32,40},... | collective-permute-start | bytes 786440 | tf_op jit(solution)/shard_map/ppermute | solution.py:483
  190.2 20.9 %collective-permute-start.5 = (bf16[128,1024]{1,0:T(8,128)(2,1)}, bf16[128,1024]{1,0:T(8,128)(2,1)S(1)}, u32[]{:S(2)}, u32[]{:S(2)}) collective-permute-start(bf16[128,1024]{1,0:T(8,128)(2,1)} %solve.1.refs_0_), channel_id=1, source_target_pairs={{0,4},{4,8},{8,12},{12,0},{16,20},{20,24},{24,28},{28,16},{32,36},... | collective-permute-start | bytes 786440 | tf_op jit(solution)/shard_map/ppermute | solution.py:483
  190.2 20.9 %collective-permute-start.6 = (bf16[128,1024]{1,0:T(8,128)(2,1)}, bf16[128,1024]{1,0:T(8,128)(2,1)S(1)}, u32[]{:S(2)}, u32[]{:S(2)}) collective-permute-start(bf16[128,1024]{1,0:T(8,128)(2,1)} %solve.1.refs_0_), channel_id=1, source_target_pairs={{0,12},{4,0},{8,4},{12,8},{16,28},{20,16},{24,20},{28,24},{32,44},... | collective-permute-start | bytes 786440 | tf_op jit(solution)/shard_map/ppermute | solution.py:483
  192.2 18.9 %collective-permute-start.7 = (bf16[128,1024]{1,0:T(8,128)(2,1)}, bf16[128,1024]{1,0:T(8,128)(2,1)S(1)}, u32[]{:S(2)}, u32[]{:S(2)}) collective-permute-start(bf16[128,1024]{1,0:T(8,128)(2,1)} %solve.1.refs_0_), channel_id=1, source_target_pairs={{0,64},{4,68},{8,72},{12,76},{16,80},{20,84},{24,88},{28,92},{32,9... | collective-permute-start | bytes 786440 | tf_op jit(solution)/shard_map/ppermute | solution.py:484
  195.2 15.9 %collective-permute-start.8 = (bf16[128,1024]{1,0:T(8,128)(2,1)}, bf16[128,1024]{1,0:T(8,128)(2,1)S(1)}, u32[]{:S(2)}, u32[]{:S(2)}) collective-permute-start(bf16[128,1024]{1,0:T(8,128)(2,1)} %solve.1.refs_0_), channel_id=1, source_target_pairs={{0,32},{4,36},{8,40},{12,44},{16,48},{20,52},{24,56},{28,60},{32,6... | collective-permute-start | bytes 786440 | tf_op jit(solution)/shard_map/ppermute | solution.py:484
  201.2 13.6 %copy-start.13 = (bf16[128,1024]{1,0:T(8,128)(2,1)}, bf16[128,1024]{1,0:T(8,128)(2,1)S(1)}, u32[]{:S(2)}) copy-start(bf16[128,1024]{1,0:T(8,128)(2,1)S(1)} %collective-permute-done.4.refs_1_) | copy-start | bytes 786436
  201.2 13.6 %collective-permute-start.9 = (bf16[128,1024]{1,0:T(8,128)(2,1)}, bf16[128,1024]{1,0:T(8,128)(2,1)S(1)}, u32[]{:S(2)}, u32[]{:S(2)}) collective-permute-start(bf16[128,1024]{1,0:T(8,128)(2,1)} %solve.1.refs_0_), channel_id=1, source_target_pairs={{0,96},{4,100},{8,104},{12,108},{16,112},{20,116},{24,120},{28,124... | collective-permute-start | bytes 786440 | tf_op jit(solution)/shard_map/ppermute | solution.py:484
  211.1 9.3 %copy-start.10 = (bf16[128,1024]{1,0:T(8,128)(2,1)}, bf16[128,1024]{1,0:T(8,128)(2,1)S(1)}, u32[]{:S(2)}) copy-start(bf16[128,1024]{1,0:T(8,128)(2,1)S(1)} %collective-permute-done.7.refs_1_) | copy-start | bytes 786436
  211.1 9.3 %copy-start.11 = (bf16[128,1024]{1,0:T(8,128)(2,1)}, bf16[128,1024]{1,0:T(8,128)(2,1)S(1)}, u32[]{:S(2)}) copy-start(bf16[128,1024]{1,0:T(8,128)(2,1)S(1)} %collective-permute-done.8.refs_2_) | copy-start | bytes 786436
  220.4 20.4 %collective-permute-start.13 = (bf16[128,2048]{1,0:T(8,128)(2,1)}, bf16[128,2048]{1,0:T(8,128)(2,1)S(1)}, u32[]{:S(2)}, u32[]{:S(2)}) collective-permute-start(bf16[128,2048]{1,0:T(8,128)(2,1)} %get-tuple-element.44), channel_id=1, source_target_pairs={{0,8},{4,12},{8,0},{12,4},{16,24},{20,28},{24,16},{28,20},{32,40},... | collective-permute-start | bytes 1572872 | tf_op jit(solution)/shard_map/ppermute | solution.py:487
  220.5 26.9 %collective-permute-start.14 = (bf16[128,2048]{1,0:T(8,128)(2,1)}, bf16[128,2048]{1,0:T(8,128)(2,1)S(1)}, u32[]{:S(2)}, u32[]{:S(2)}) collective-permute-start(bf16[128,2048]{1,0:T(8,128)(2,1)} %get-tuple-element.45), channel_id=1, source_target_pairs={{0,12},{4,0},{8,4},{12,8},{16,28},{20,16},{24,20},{28,24},{32,44},... | collective-permute-start | bytes 1572872 | tf_op jit(solution)/shard_map/ppermute | solution.py:487
  222.5 25.0 %collective-permute-start.15 = (bf16[128,2048]{1,0:T(8,128)(2,1)}, bf16[128,2048]{1,0:T(8,128)(2,1)S(1)}, u32[]{:S(2)}, u32[]{:S(2)}) collective-permute-start(bf16[128,2048]{1,0:T(8,128)(2,1)} %get-tuple-element.46), channel_id=1, source_target_pairs={{0,4},{4,8},{8,12},{12,0},{16,20},{20,24},{24,28},{28,16},{32,36},... | collective-permute-start | bytes 1572872 | tf_op jit(solution)/shard_map/ppermute | solution.py:487
  228.0 26.2 %collective-permute-start.10 = (bf16[128,2048]{1,0:T(8,128)(2,1)}, bf16[128,2048]{1,0:T(8,128)(2,1)S(1)}, u32[]{:S(2)}, u32[]{:S(2)}) collective-permute-start(bf16[128,2048]{1,0:T(8,128)(2,1)} %get-tuple-element.38), channel_id=1, source_target_pairs={{0,64},{4,68},{8,72},{12,76},{16,80},{20,84},{24,88},{28,92},{32,9... | collective-permute-start | bytes 1572872 | tf_op jit(solution)/shard_map/ppermute | solution.py:489
  239.9 19.6 %collective-permute-start.11 = (bf16[128,2048]{1,0:T(8,128)(2,1)}, bf16[128,2048]{1,0:T(8,128)(2,1)S(1)}, u32[]{:S(2)}, u32[]{:S(2)}) collective-permute-start(bf16[128,2048]{1,0:T(8,128)(2,1)} %get-tuple-element.39), channel_id=1, source_target_pairs={{0,96},{4,100},{8,104},{12,108},{16,112},{20,116},{24,120},{28,124... | collective-permute-start | bytes 1572872 | tf_op jit(solution)/shard_map/ppermute | solution.py:489
  240.7 6.7 %copy-start.3 = (bf16[128,2048]{1,0:T(8,128)(2,1)}, bf16[128,2048]{1,0:T(8,128)(2,1)S(1)}, u32[]{:S(2)}) copy-start(bf16[128,2048]{1,0:T(8,128)(2,1)S(1)} %collective-permute-done.13.refs_0_) | copy-start | bytes 1572868
  240.7 19.9 %collective-permute-start.12 = (bf16[128,2048]{1,0:T(8,128)(2,1)}, bf16[128,2048]{1,0:T(8,128)(2,1)S(1)}, u32[]{:S(2)}, u32[]{:S(2)}) collective-permute-start(bf16[128,2048]{1,0:T(8,128)(2,1)} %get-tuple-element.40), channel_id=1, source_target_pairs={{0,32},{4,36},{8,40},{12,44},{16,48},{20,52},{24,56},{28,60},{32,6... | collective-permute-start | bytes 1572872 | tf_op jit(solution)/shard_map/ppermute | solution.py:489
  (11 other events, 31.7 us)

commit v6 on v5

--- a/solution.py
+++ b/solution.py
@@ -91,7 +91,7 @@
 
     lax.fori_loop(0, tile // 8, scatter, 0)
     out_ref[...] = jnp.zeros_like(out_ref)
-    together = 16
+    together = 32
 
     @pl.when(step == 0)
     def _():

time: 270 us -> 270 us (level)
  no operation moved by 1% of the time
where the time goes in v6:
time: 270 us; the launch traced here: 268 us
  Pallas kernels  161 us (60%)
  starting transfers between devices  54.1 us (20%)
  waiting for transfers between devices  38.1 us (14%)
  other arithmetic  7.04 us (3%)
  local copies, waits for them, and re-layouts  6.6 us (2%)
    pallas_call x2, Pallas kernels, predict(): pl.pallas_call(functools.partial(predict_kernel, tile=tile, crossing=cros...  57.5 us
    pallas_call x1, Pallas kernels, minus_inverse(): pl.pallas_call(functools.partial(inverse_kernel, size=size), grid=(1,), i...  43.9 us
    all_to_all x1, waiting for transfers between devices, to_all(): lax.all_to_all(jnp.broadcast_to(piece[None], (everyone,) + piece.shape),...  19.2 us
    pallas_call x1, Pallas kernels, spread(): pl.pallas_call(spread_kernel, grid=(everyone,), in_specs=[pl.BlockSpec((s...  18.8 us
    pallas_call x3, Pallas kernels, downdate(): pl.pallas_call(functools.partial(downdate_kernel, count=count), grid_spec...  15.9 us
    ppermute x3, starting transfers between devices, shards(): lax.ppermute(part, 'obs', steps_along(0, -d))  13.8 us
    ppermute x3, starting transfers between devices, shards(): from_y = [lax.ppermute(solved, 'obs', steps_along(0, d)) for d in (2, 1, 3)]  12.5 us
    pallas_call x2, Pallas kernels, products(): pl.pallas_call(functools.partial(product_kernel, members=members), grid=(...  11 us
  transfers between devices with their start and end apart: 18, of which 8 were waited for; matrix products, arithmetic and copies ran while one was open for 2% of the time, Pallas kernels for 56%

profile of v6, /device:TPU:66, one launch (start us, length us, event | category | flops | bytes accessed | tf_op | source)
XLA Modules:
  0.0 267.6 jit_solution(8989635311235822931)
XLA Ops:
  3.4 2.2 broadcast_in_dim.62
  5.6 10.1 %all-to-all-start = ((f32[32,16,1792]{2,1,0:T(8,128)}), f32[32,16,1792]{2,1,0:T(8,128)}, u32[]{:S(2)}, u32[]{:S(2)}) async-start(f32[32,16,1792]{2,1,0:T(8,128)} %broadcast_in_dim.62), calls=%async_computation | async-start | bytes 7340032 | tf_op jit(solution)/shard_map/all_to_all | solution.py:434
  15.7 18.8 %spread.1 = bf16[32,2,32,2048]{3,2,1,0:T(8,128)(2,1)} custom-call(bf16[32,16384]{1,0:T(8,128)(2,1)} %bitcast.16, bf16[32,16384]{1,0:T(8,128)(2,1)} %bitcast.17), custom_call_target="tpu_custom_call" | custom-call | bytes 8388608 | tf_op jit(solution)/shard_map/spread/pallas_call | solution.py:321
  34.4 9.3 %split.1.far_ref = bf16[16384,256]{1,0:T(8,128)(2,1)} custom-call(f32[16384,128]{1,0:T(8,128)} %refs_3_.3), custom_call_target="tpu_custom_call" | custom-call | flops 8388608 | bytes 16777216 | tf_op jit(solution)/shard_map/split/pallas_call | solution.py:41
  43.8 19.2 %all-to-all-done.own_ref = f32[32,16,1792]{2,1,0:T(8,128)} async-done(((f32[32,16,1792]{2,1,0:T(8,128)}), f32[32,16,1792]{2,1,0:T(8,128)}, u32[]{:S(2)}, u32[]{:S(2)}) %all-to-all-start) | async-done | bytes 3670048 | tf_op jit(solution)/shard_map/all_to_all | solution.py:434
  64.9 8.8 %all-to-all-start.1 = ((bf16[32,2,32,2048]{3,2,1,0:T(8,128)(2,1)}), bf16[32,2,32,2048]{3,2,1,0:T(8,128)(2,1)}, u32[]{:S(2)}, u32[]{:S(2)}) async-start(bf16[32,2,32,2048]{3,2,1,0:T(8,128)(2,1)} %spread.1), calls=%async_computation.1 | async-start | bytes 16777216 | tf_op jit(solution)/shard_map/all_to_all | solution.py:463
  73.6 28.7 %predict.2 = f32[512,128]{1,0:T(8,128)} custom-call(s32[8192]{0:T(1024)} %reshape.52.place_ref, f32[512,1792]{1,0:T(8,128)} %bitcast.6.slots_ref, bf16[16384,256]{1,0:T(8,128)(2,1)} %split.1.far_ref), custom_call_target="tpu_custom_call" | custom-call | flops 12884901888 | bytes 8388608 | tf_op jit(solution)/shard_map/predict/pallas_call | solution.py:128
  104.3 28.8 %predict.3 = f32[512,128]{1,0:T(8,128)} custom-call(s32[8192]{0:T(1024)} %reshape.54.place_ref, f32[512,1792]{1,0:T(8,128)} %bitcast.7.slots_ref, bf16[16384,256]{1,0:T(8,128)(2,1)} %split.1.far_ref), custom_call_target="tpu_custom_call" | custom-call | flops 12884901888 | bytes 8388608 | tf_op jit(solution)/shard_map/predict/pallas_call | solution.py:128
  138.1 43.9 %minus_inverse.1.minus_ref = f32[1024,1024]{1,0:T(8,128)} custom-call(s32[1]{0:T(128)} %bitcast.3.core_ref, f32[32,16,1792]{2,1,0:T(8,128)} %all-to-all-done.own_ref, f32[32,16,1792]{2,1,0:T(8,128)} %collective-permute-done.other_ref), custom_call_target="tpu_custom_call" | custom-call | flops 64424509440 | bytes 8388608 | tf_op jit(solution)/shard_map/minus_inverse/pallas_call | solution.py:276
  182.7 4.4 %solve.1.refs_0_ = bf16[128,1024]{1,0:T(8,128)(2,1)} custom-call(f32[1024,1024]{1,0:T(8,128)} %minus_inverse.1.minus_ref, f32[32,2,16,128]{3,2,1,0:T(8,128)} %copy-done.2, f32[32,2,16,128]{3,2,1,0:T(8,128)} %copy-done.9), custom_call_target="tpu_custom_call" | custom-call | flops 805306368 | bytes 4194304 | tf_op jit(solution)/shard_map/solve/pallas_call | solution.py:301
  187.1 2.1 collective-permute-start.4
  189.2 2.0 collective-permute-start.6
  191.2 3.0 %collective-permute-start.7 = (bf16[128,1024]{1,0:T(8,128)(2,1)}, bf16[128,1024]{1,0:T(8,128)(2,1)S(1)}, u32[]{:S(2)}, u32[]{:S(2)}) collective-permute-start(bf16[128,1024]{1,0:T(8,128)(2,1)} %solve.1.refs_0_), channel_id=1, source_target_pairs={{0,64},{4,68},{8,72},{12,76},{16,80},{20,84},{24,88},{28,92},{32,9... | collective-permute-start | bytes 786440 | tf_op jit(solution)/shard_map/ppermute | solution.py:484
  194.8 6.4 %collective-permute-done.4.refs_1_ = bf16[128,1024]{1,0:T(8,128)(2,1)S(1)} collective-permute-done((bf16[128,1024]{1,0:T(8,128)(2,1)}, bf16[128,1024]{1,0:T(8,128)(2,1)S(1)}, u32[]{:S(2)}, u32[]{:S(2)}) %collective-permute-start.4) | collective-permute-done | bytes 262176 | tf_op jit(solution)/shard_map/ppermute | solution.py:483
  201.2 8.9 %collective-permute-start.9 = (bf16[128,1024]{1,0:T(8,128)(2,1)}, bf16[128,1024]{1,0:T(8,128)(2,1)S(1)}, u32[]{:S(2)}, u32[]{:S(2)}) collective-permute-start(bf16[128,1024]{1,0:T(8,128)(2,1)} %solve.1.refs_0_), channel_id=1, source_target_pairs={{0,96},{4,100},{8,104},{12,108},{16,112},{20,116},{24,120},{28,124... | collective-permute-start | bytes 786440 | tf_op jit(solution)/shard_map/ppermute | solution.py:484
  211.5 3.4 %collective-permute-done.9.refs_3_ = bf16[128,1024]{1,0:T(8,128)(2,1)S(1)} collective-permute-done((bf16[128,1024]{1,0:T(8,128)(2,1)}, bf16[128,1024]{1,0:T(8,128)(2,1)S(1)}, u32[]{:S(2)}, u32[]{:S(2)}) %collective-permute-start.9) | collective-permute-done | bytes 262176 | tf_op jit(solution)/shard_map/ppermute | solution.py:484
  214.9 5.6 %products.3 = (f32[128,2048]{1,0:T(8,128)}, bf16[128,2048]{1,0:T(8,128)(2,1)}, bf16[128,2048]{1,0:T(8,128)(2,1)}, bf16[128,2048]{1,0:T(8,128)(2,1)}) custom-call(bf16[128,1024]{1,0:T(8,128)(2,1)} %solve.1.refs_0_, bf16[128,1024]{1,0:T(8,128)(2,1)} %copy-done.13, bf16[128,1024]{1,0:T(8,128)(2,1)} %copy-done.14, bf16[128,1024]{1,0:T(8,128)(2,1)} %copy-done.15, ...), custom_call_target="tpu_custom_call" | custom-call | flops 2147483648 | bytes 4194304 | tf_op jit(solution)/shard_map/products/pallas_call | solution.py:356
  220.5 2.3 collective-permute-start.14
  222.9 5.5 %products.2 = (f32[128,2048]{1,0:T(8,128)}, bf16[128,2048]{1,0:T(8,128)(2,1)}, bf16[128,2048]{1,0:T(8,128)(2,1)}, bf16[128,2048]{1,0:T(8,128)(2,1)}) custom-call(bf16[128,1024]{1,0:T(8,128)(2,1)} %solve.1.refs_0_, bf16[128,1024]{1,0:T(8,128)(2,1)} %copy-done.10, bf16[128,1024]{1,0:T(8,128)(2,1)} %copy-done.11, bf16[128,1024]{1,0:T(8,128)(2,1)} %copy-done.12, ...), custom_call_target="tpu_custom_call" | custom-call | flops 2147483648 | bytes 4194304 | tf_op jit(solution)/shard_map/products/pallas_call | solution.py:356
  228.3 11.8 %collective-permute-start.10 = (bf16[128,2048]{1,0:T(8,128)(2,1)}, bf16[128,2048]{1,0:T(8,128)(2,1)S(1)}, u32[]{:S(2)}, u32[]{:S(2)}) collective-permute-start(bf16[128,2048]{1,0:T(8,128)(2,1)} %get-tuple-element.38), channel_id=1, source_target_pairs={{0,64},{4,68},{8,72},{12,76},{16,80},{20,84},{24,88},{28,92},{32,9... | collective-permute-start | bytes 1572872 | tf_op jit(solution)/shard_map/ppermute | solution.py:489
  243.5 4.2 %downdate.3.refs_4_ = f32[16384,128]{1,0:T(8,128)} custom-call(s32[2]{0:T(128)} %pad_add_fusion.2.chunk_ref, f32[128,2048]{1,0:T(8,128)} %get-tuple-element.47.refs_0_, f32[128,2048]{1,0:T(8,128)} %get-tuple-element.48.refs_1_, f32[16384,128]{1,0:T(8,128)} %refs_3_.3), custom_call_target="tpu_custom_call" | custom-call | flops 524288 | bytes 5242880 | tf_op jit(solution)/shard_map/downdate/pallas_call | solution.py:387
  248.8 5.8 %downdate.4.refs_4_ = f32[16384,128]{1,0:T(8,128)} custom-call(s32[3]{0:T(128)} %get-tuple-element.54.chunk_ref, bf16[128,2048]{1,0:T(8,128)(2,1)} %copy-done.3, bf16[128,2048]{1,0:T(8,128)(2,1)} %copy-done.4, bf16[128,2048]{1,0:T(8,128)(2,1)} %copy-done.6, f32[16384,128]{1,0:T(8,128)} %refs_3_.3, ...), custom_call_target="tpu_custom_call", output_to_operand_aliasing={{}: (5, {})} | custom-call | flops 786432 | bytes 7864320 | tf_op jit(solution)/shard_map/downdate/pallas_call | solution.py:387
  254.5 5.2 %collective-permute-done.11.refs_1_ = bf16[128,2048]{1,0:T(8,128)(2,1)S(1)} collective-permute-done((bf16[128,2048]{1,0:T(8,128)(2,1)}, bf16[128,2048]{1,0:T(8,128)(2,1)S(1)}, u32[]{:S(2)}, u32[]{:S(2)}) %collective-permute-start.11) | collective-permute-done | bytes 524320 | tf_op jit(solution)/shard_map/ppermute | solution.py:489
  261.7 5.9 %downdate.5 = f32[16384,128]{1,0:T(8,128)} custom-call(s32[3]{0:T(128)} %get-tuple-element.53.chunk_ref, bf16[128,2048]{1,0:T(8,128)(2,1)} %copy-done.5, bf16[128,2048]{1,0:T(8,128)(2,1)} %copy-done.7, bf16[128,2048]{1,0:T(8,128)(2,1)} %copy-done.8, f32[16384,128]{1,0:T(8,128)} %refs_3_.3, f32[16384,128]{1,0:T(8,128)} %downdate.4.refs_4_), custom_call_target="tpu_custom_call", output_to_operand_aliasing={{}: (5, {})} | custom-call | flops 786432 | bytes 7864320 | tf_op jit(solution)/shard_map/downdate/pallas_call | solution.py:387
  (78 shorter events, 20.6 us)
Async XLA Ops:
  5.6 57.4 %all-to-all-start = ((f32[32,16,1792]{2,1,0:T(8,128)}), f32[32,16,1792]{2,1,0:T(8,128)}, u32[]{:S(2)}, u32[]{:S(2)}) async-start(f32[32,16,1792]{2,1,0:T(8,128)} %broadcast_in_dim.62), calls=%async_computation | async-start | bytes 7340032 | tf_op jit(solution)/shard_map/all_to_all | solution.py:434
  63.0 39.4 %collective-permute-start = (f32[32,16,1792]{2,1,0:T(8,128)}, f32[32,16,1792]{2,1,0:T(8,128)}, u32[]{:S(2)}, u32[]{:S(2)}) collective-permute-start(f32[32,16,1792]{2,1,0:T(8,128)} %all-to-all-done.own_ref), channel_id=1, source_target_pairs={{0,1},{1,0},{2,3},{3,2},{4,5},{5,4},{6,7},{7,6},{8,9},{9,8},{10,11... | collective-permute-start | bytes 11010056 | tf_op jit(solution)/shard_map/ppermute | solution.py:464
  64.9 150.0 %all-to-all-start.1 = ((bf16[32,2,32,2048]{3,2,1,0:T(8,128)(2,1)}), bf16[32,2,32,2048]{3,2,1,0:T(8,128)(2,1)}, u32[]{:S(2)}, u32[]{:S(2)}) async-start(bf16[32,2,32,2048]{3,2,1,0:T(8,128)(2,1)} %spread.1), calls=%async_computation.1 | async-start | bytes 16777216 | tf_op jit(solution)/shard_map/all_to_all | solution.py:463
  104.3 28.9 %copy-start.16 = (f32[512,128]{1,0:T(8,128)S(1)}, f32[512,128]{1,0:T(8,128)}, u32[]{:S(2)}) copy-start(f32[512,128]{1,0:T(8,128)} %predict.2) | copy-start | bytes 786436
  133.1 1.8 collective-permute-start.1
  133.2 1.9 collective-permute-start.2
  136.2 45.8 %copy-start.2 = (f32[32,2,16,128]{3,2,1,0:T(8,128)}, f32[32,2,16,128]{3,2,1,0:T(8,128)S(1)}, u32[]{:S(2)}) copy-start(f32[32,2,16,128]{3,2,1,0:T(8,128)S(1)} %pad_maximum_fusion.here_ref) | copy-start | bytes 1572868
  136.2 45.8 %collective-permute-start.3 = (f32[32,2,16,128]{3,2,1,0:T(8,128)S(1)}, f32[32,2,16,128]{3,2,1,0:T(8,128)S(1)}, u32[]{:S(2)}, u32[]{:S(2)}) collective-permute-start(f32[32,2,16,128]{3,2,1,0:T(8,128)S(1)} %pad_maximum_fusion.here_ref), channel_id=1, source_target_pairs={{0,2},{2,0},{1,3},{3,1},{4,6},{6,4},{5,7},{7,5},{8,10},{10,8},{9,1... | collective-permute-start | bytes 1572872 | tf_op jit(solution)/shard_map/ppermute | solution.py:477
  187.1 14.1 %collective-permute-start.4 = (bf16[128,1024]{1,0:T(8,128)(2,1)}, bf16[128,1024]{1,0:T(8,128)(2,1)S(1)}, u32[]{:S(2)}, u32[]{:S(2)}) collective-permute-start(bf16[128,1024]{1,0:T(8,128)(2,1)} %solve.1.refs_0_), channel_id=1, source_target_pairs={{0,8},{4,12},{8,0},{12,4},{16,24},{20,28},{24,16},{28,20},{32,40},... | collective-permute-start | bytes 786440 | tf_op jit(solution)/shard_map/ppermute | solution.py:483
  189.2 22.2 %collective-permute-start.5 = (bf16[128,1024]{1,0:T(8,128)(2,1)}, bf16[128,1024]{1,0:T(8,128)(2,1)S(1)}, u32[]{:S(2)}, u32[]{:S(2)}) collective-permute-start(bf16[128,1024]{1,0:T(8,128)(2,1)} %solve.1.refs_0_), channel_id=1, source_target_pairs={{0,4},{4,8},{8,12},{12,0},{16,20},{20,24},{24,28},{28,16},{32,36},... | collective-permute-start | bytes 786440 | tf_op jit(solution)/shard_map/ppermute | solution.py:483
  189.2 22.2 %collective-permute-start.6 = (bf16[128,1024]{1,0:T(8,128)(2,1)}, bf16[128,1024]{1,0:T(8,128)(2,1)S(1)}, u32[]{:S(2)}, u32[]{:S(2)}) collective-permute-start(bf16[128,1024]{1,0:T(8,128)(2,1)} %solve.1.refs_0_), channel_id=1, source_target_pairs={{0,12},{4,0},{8,4},{12,8},{16,28},{20,16},{24,20},{28,24},{32,44},... | collective-permute-start | bytes 786440 | tf_op jit(solution)/shard_map/ppermute | solution.py:483
  191.2 20.2 %collective-permute-start.7 = (bf16[128,1024]{1,0:T(8,128)(2,1)}, bf16[128,1024]{1,0:T(8,128)(2,1)S(1)}, u32[]{:S(2)}, u32[]{:S(2)}) collective-permute-start(bf16[128,1024]{1,0:T(8,128)(2,1)} %solve.1.refs_0_), channel_id=1, source_target_pairs={{0,64},{4,68},{8,72},{12,76},{16,80},{20,84},{24,88},{28,92},{32,9... | collective-permute-start | bytes 786440 | tf_op jit(solution)/shard_map/ppermute | solution.py:484
  194.2 17.2 %collective-permute-start.8 = (bf16[128,1024]{1,0:T(8,128)(2,1)}, bf16[128,1024]{1,0:T(8,128)(2,1)S(1)}, u32[]{:S(2)}, u32[]{:S(2)}) collective-permute-start(bf16[128,1024]{1,0:T(8,128)(2,1)} %solve.1.refs_0_), channel_id=1, source_target_pairs={{0,32},{4,36},{8,40},{12,44},{16,48},{20,52},{24,56},{28,60},{32,6... | collective-permute-start | bytes 786440 | tf_op jit(solution)/shard_map/ppermute | solution.py:484
  201.2 13.6 %copy-start.13 = (bf16[128,1024]{1,0:T(8,128)(2,1)}, bf16[128,1024]{1,0:T(8,128)(2,1)S(1)}, u32[]{:S(2)}) copy-start(bf16[128,1024]{1,0:T(8,128)(2,1)S(1)} %collective-permute-done.4.refs_1_) | copy-start | bytes 786436
  201.2 13.6 %collective-permute-start.9 = (bf16[128,1024]{1,0:T(8,128)(2,1)}, bf16[128,1024]{1,0:T(8,128)(2,1)S(1)}, u32[]{:S(2)}, u32[]{:S(2)}) collective-permute-start(bf16[128,1024]{1,0:T(8,128)(2,1)} %solve.1.refs_0_), channel_id=1, source_target_pairs={{0,96},{4,100},{8,104},{12,108},{16,112},{20,116},{24,120},{28,124... | collective-permute-start | bytes 786440 | tf_op jit(solution)/shard_map/ppermute | solution.py:484
  211.4 9.0 %copy-start.10 = (bf16[128,1024]{1,0:T(8,128)(2,1)}, bf16[128,1024]{1,0:T(8,128)(2,1)S(1)}, u32[]{:S(2)}) copy-start(bf16[128,1024]{1,0:T(8,128)(2,1)S(1)} %collective-permute-done.7.refs_1_) | copy-start | bytes 786436
  211.5 8.9 %copy-start.11 = (bf16[128,1024]{1,0:T(8,128)(2,1)}, bf16[128,1024]{1,0:T(8,128)(2,1)S(1)}, u32[]{:S(2)}) copy-start(bf16[128,1024]{1,0:T(8,128)(2,1)S(1)} %collective-permute-done.8.refs_2_) | copy-start | bytes 786436
  220.4 20.6 %collective-permute-start.13 = (bf16[128,2048]{1,0:T(8,128)(2,1)}, bf16[128,2048]{1,0:T(8,128)(2,1)S(1)}, u32[]{:S(2)}, u32[]{:S(2)}) collective-permute-start(bf16[128,2048]{1,0:T(8,128)(2,1)} %get-tuple-element.44), channel_id=1, source_target_pairs={{0,8},{4,12},{8,0},{12,4},{16,24},{20,28},{24,16},{28,20},{32,40},... | collective-permute-start | bytes 1572872 | tf_op jit(solution)/shard_map/ppermute | solution.py:487
  220.5 27.2 %collective-permute-start.14 = (bf16[128,2048]{1,0:T(8,128)(2,1)}, bf16[128,2048]{1,0:T(8,128)(2,1)S(1)}, u32[]{:S(2)}, u32[]{:S(2)}) collective-permute-start(bf16[128,2048]{1,0:T(8,128)(2,1)} %get-tuple-element.45), channel_id=1, source_target_pairs={{0,12},{4,0},{8,4},{12,8},{16,28},{20,16},{24,20},{28,24},{32,44},... | collective-permute-start | bytes 1572872 | tf_op jit(solution)/shard_map/ppermute | solution.py:487
  222.9 24.9 %collective-permute-start.15 = (bf16[128,2048]{1,0:T(8,128)(2,1)}, bf16[128,2048]{1,0:T(8,128)(2,1)S(1)}, u32[]{:S(2)}, u32[]{:S(2)}) collective-permute-start(bf16[128,2048]{1,0:T(8,128)(2,1)} %get-tuple-element.46), channel_id=1, source_target_pairs={{0,4},{4,8},{8,12},{12,0},{16,20},{20,24},{24,28},{28,16},{32,36},... | collective-permute-start | bytes 1572872 | tf_op jit(solution)/shard_map/ppermute | solution.py:487
  228.3 26.2 %collective-permute-start.10 = (bf16[128,2048]{1,0:T(8,128)(2,1)}, bf16[128,2048]{1,0:T(8,128)(2,1)S(1)}, u32[]{:S(2)}, u32[]{:S(2)}) collective-permute-start(bf16[128,2048]{1,0:T(8,128)(2,1)} %get-tuple-element.38), channel_id=1, source_target_pairs={{0,64},{4,68},{8,72},{12,76},{16,80},{20,84},{24,88},{28,92},{32,9... | collective-permute-start | bytes 1572872 | tf_op jit(solution)/shard_map/ppermute | solution.py:489
  240.2 19.6 %collective-permute-start.11 = (bf16[128,2048]{1,0:T(8,128)(2,1)}, bf16[128,2048]{1,0:T(8,128)(2,1)S(1)}, u32[]{:S(2)}, u32[]{:S(2)}) collective-permute-start(bf16[128,2048]{1,0:T(8,128)(2,1)} %get-tuple-element.39), channel_id=1, source_target_pairs={{0,96},{4,100},{8,104},{12,108},{16,112},{20,116},{24,120},{28,124... | collective-permute-start | bytes 1572872 | tf_op jit(solution)/shard_map/ppermute | solution.py:489
  241.0 6.7 %copy-start.3 = (bf16[128,2048]{1,0:T(8,128)(2,1)}, bf16[128,2048]{1,0:T(8,128)(2,1)S(1)}, u32[]{:S(2)}) copy-start(bf16[128,2048]{1,0:T(8,128)(2,1)S(1)} %collective-permute-done.13.refs_0_) | copy-start | bytes 1572868
  241.1 19.9 %collective-permute-start.12 = (bf16[128,2048]{1,0:T(8,128)(2,1)}, bf16[128,2048]{1,0:T(8,128)(2,1)S(1)}, u32[]{:S(2)}, u32[]{:S(2)}) collective-permute-start(bf16[128,2048]{1,0:T(8,128)(2,1)} %get-tuple-element.40), channel_id=1, source_target_pairs={{0,32},{4,36},{8,40},{12,44},{16,48},{20,52},{24,56},{28,60},{32,6... | collective-permute-start | bytes 1572872 | tf_op jit(solution)/shard_map/ppermute | solution.py:489
  (11 other events, 31.0 us)
